TPU v7x, 32 devices: a whole 2x2x4 slice. The times are simulated.
32 devices in a mesh: grid: 16 (over z, y, core), orb: 2 (over x).
Axes of the slice: x: 2, y: 2, z: 4, core: 2. Of those that a mesh axis runs over, the one named last changes fastest.
Arguments:
- orbitals: bfloat16 [16, 884736], P('orb', 'grid'), may hold values from -6 to 6
- potential: float32 [884736], P('grid'), may hold values from -2 to 0
- projector_atom: int32 [24576], P('grid'), may hold values from 0 to 63, as said below
- projector_cell: int32 [24576], P('grid'), may hold values from 0 to 55295
- projector_value: float32 [24576], P('grid'), may hold values from -1.5 to 1.5
- atom_strength: float32 [64], replicated, may hold values from 0.25 to 2
- ritz_rotation: bfloat16 [4, 8, 32], P(None, None, 'orb'), may hold values from -1 to 1
- panel_owner: int32 [4], replicated, may hold values from 0 to 1
Outputs:
- filtered: bfloat16 [16, 884736], P('orb', 'grid')
- rotated: bfloat16 [32, 884736], P('orb', 'grid')
Inputs may be any that keep to these rules, and one draw needn't show every extreme that they name: `projector_atom`: the entries e of slab s (e // 1536 = s) name atoms of slabs s - 1, s and s + 1 only, slab t holding atoms t * 4 to (t + 1) * 4 - 1.
All inputs are finite; a program needn't handle non-finite values.
Results may differ from a plain program's by a relative error of at most 0.0049.
Values may be sent and summed in bfloat16 or wider, within the bound.
No kernel may reach another device: no remote copies, remote signals or barrier semaphores. Data moves between devices by JAX's collectives and lax.ppermute only.
A program may use at most 128 MiB of HBM per device.

v0:
```python
import jax
import jax.numpy as jnp
from jax import lax
from jax.sharding import PartitionSpec as P

NX = 96
NY = 96
REACH = 6
ATOM_DEV = 4


stencil_weights = (
    -5369.0 / 1800.0,
    12.0 / 7.0,
    -15.0 / 56.0,
    10.0 / 189.0,
    -1.0 / 112.0,
    2.0 / 1925.0,
    -1.0 / 16632.0,
)
cheb_center = 6.0
cheb_half = 6.0


def with_halo(block, sides, width):
    for axis, dim in sides:
        count = lax.axis_size(axis)
        forward = [(i, i + 1) for i in range(count - 1)]
        backward = [(target, source) for source, target in forward]
        low = lax.ppermute(
            lax.slice_in_dim(block, block.shape[dim] - width, None, axis=dim), axis, forward
        )
        high = lax.ppermute(lax.slice_in_dim(block, 0, width, axis=dim), axis, backward)
        block = jnp.concatenate([low, block, high], axis=dim)
    return block


def laplace(extended, cell_count, column_pos, row_pos):
    plane_cells = NX * NY
    margin = REACH * plane_cells
    middle = extended[:, margin : margin + cell_count].astype(jnp.float32)
    summed = 3.0 * stencil_weights[0] * middle
    for distance in range(1, REACH + 1):
        plane_jump = distance * plane_cells
        row_jump = distance * NX
        upper_plane = extended[:, margin + plane_jump : margin + plane_jump + cell_count].astype(
            jnp.float32
        )
        lower_plane = extended[:, margin - plane_jump : margin - plane_jump + cell_count].astype(
            jnp.float32
        )
        row_after = extended[:, margin + row_jump : margin + row_jump + cell_count].astype(
            jnp.float32
        )
        row_before = extended[:, margin - row_jump : margin - row_jump + cell_count].astype(
            jnp.float32
        )
        cell_after = extended[:, margin + distance : margin + distance + cell_count].astype(
            jnp.float32
        )
        cell_before = extended[:, margin - distance : margin - distance + cell_count].astype(
            jnp.float32
        )
        neighbours = upper_plane + lower_plane
        neighbours = (
            neighbours
            + jnp.where(row_pos + distance < NY, row_after, 0.0)
            + jnp.where(row_pos >= distance, row_before, 0.0)
        )
        neighbours = (
            neighbours
            + jnp.where(column_pos + distance < NX, cell_after, 0.0)
            + jnp.where(column_pos >= distance, cell_before, 0.0)
        )
        summed = summed + stencil_weights[distance] * neighbours
    return (middle, summed)


def combine_atoms(partial_sums, slab_index, atom_slots):
    slab_count = lax.axis_size("grid")
    atom_table = jnp.zeros((partial_sums.shape[0], (slab_count + 2) * ATOM_DEV), jnp.float32)
    atom_table = lax.dynamic_update_slice_in_dim(atom_table, partial_sums, slab_index * ATOM_DEV, 1)
    table_sums = lax.psum(atom_table, "grid")
    return lax.dynamic_slice_in_dim(table_sums, slab_index * ATOM_DEV, atom_slots, 1)


def body(
    orbitals,
    potential,
    projector_atom,
    projector_cell,
    projector_value,
    atom_strength,
    ritz_rotation,
    panel_owner,
):
    panel_rows, cell_count = orbitals.shape
    margin = REACH * NX * NY
    local_cells = lax.iota(jnp.int32, cell_count)
    column_pos = local_cells % NX
    row_pos = local_cells // NX % NY
    slab_index = lax.axis_index("grid")
    atom_slots = 3 * ATOM_DEV
    relative = projector_atom - (slab_index - 1) * ATOM_DEV
    selector = (lax.iota(jnp.int32, atom_slots)[:, None] == relative[None, :]).astype(jnp.float32)
    padded_strength = jnp.pad(atom_strength, (ATOM_DEV, ATOM_DEV))
    near_strength = lax.dynamic_slice_in_dim(padded_strength, slab_index * ATOM_DEV, atom_slots)

    def hamiltonian(extended):
        middle, summed = laplace(extended, cell_count, column_pos, row_pos)
        gathered = jnp.take(middle, projector_cell, axis=1)
        weighted = gathered * projector_value
        partial_sums = lax.dot_general(
            weighted,
            selector,
            (((1,), (1,)), ((), ())),
            precision=lax.Precision.HIGHEST,
            preferred_element_type=jnp.float32,
        )
        near_sums = combine_atoms(partial_sums, slab_index, atom_slots)
        scaled = near_sums * near_strength
        spread = (
            jnp.dot(
                scaled,
                selector,
                precision=lax.Precision.HIGHEST,
                preferred_element_type=jnp.float32,
            )
            * projector_value
        )
        nonlocal_term = jnp.zeros_like(middle).at[:, projector_cell].add(spread)
        return -0.5 * summed + potential * middle + nonlocal_term

    initial = orbitals.astype(jnp.float32)
    first_extended = with_halo(orbitals, (("grid", 1),), margin)
    first_image = hamiltonian(first_extended)
    step_field = (first_image - cheb_center * initial) / cheb_half
    second_extended = with_halo(step_field, (("grid", 1),), margin)
    second = hamiltonian(second_extended)
    filtered = (2.0 * (second - cheb_center * step_field) / cheb_half - initial).astype(
        jnp.bfloat16
    )
    step_count = ritz_rotation.shape[0]
    everyone = lax.all_gather(filtered, "orb", axis=0, tiled=True)
    stacked = jnp.take(
        everyone.reshape(lax.axis_size("orb"), panel_rows, cell_count), panel_owner, axis=0
    ).reshape(step_count * panel_rows, cell_count)
    rotation_rows = ritz_rotation.reshape(step_count * panel_rows, ritz_rotation.shape[2])
    column_total = rotation_rows.shape[1]
    block_width = max(column_total // 4, 1)
    blocks = []
    for first_column in range(0, column_total, block_width):
        part_rows = rotation_rows[:, first_column : first_column + block_width]
        product = lax.dot_general(
            part_rows, stacked, (((0,), (0,)), ((), ())), preferred_element_type=jnp.float32
        )
        blocks.append(product.astype(jnp.bfloat16))
    rotated = jnp.concatenate(blocks, 0)
    return (filtered, rotated)


def solution(mesh):
    in_specs = (
        P("orb", "grid"),
        P("grid"),
        P("grid"),
        P("grid"),
        P("grid"),
        P(),
        P(None, None, "orb"),
        P(),
    )
    out_specs = (P("orb", "grid"), P("orb", "grid"))
    return jax.shard_map(body, mesh=mesh, in_specs=in_specs, out_specs=out_specs, check_vma=False)
```

profile of v0, /device:TPU:11, one launch (start us, length us, event | category | flops | bytes accessed | tf_op | source)
XLA Modules:
  0.0 372.9 jit_solution(11059837443291751908)
XLA Ops:
  7.2 2.7 collective-permute-start
  9.9 3.0 collective-permute-start.1
  13.0 0.7 compare_and_fusion
  13.7 0.7 compare_select_fusion
  14.4 0.8 broadcast_compare_fusion.4
  15.2 0.8 broadcast_compare_fusion.2
  16.1 0.8 broadcast_compare_fusion
  16.9 0.9 add_compare_fusion.4
  17.8 0.9 add_compare_fusion.2
  18.7 0.9 add_compare_fusion
  19.5 0.8 fusion.129
  20.3 0.8 fusion.127
  21.1 0.8 fusion.125
  21.9 0.8 fusion.121
  22.7 0.8 fusion.117
  23.5 11.5 %copy.163 = f32[8,55296]{0,1:T(8,128)} copy(bf16[8,55296]{1,0:T(8,128)(2,1)S(1)} %copy-done) | data formatting | bytes 2654208 | tf_op jit(solution)/shard_map/convert_element_type | solution.py:41
  35.0 11.6 %gather_fusion.1 = f32[1536,8]{1,0:T(8,128)S(1)} fusion(f32[8,55296]{0,1:T(8,128)} %copy.163, s32[2048]{0:T(1024)S(1)} %pad_clamp_fusion), kind=kCustom, calls=%fused_computation.clone | custom fusion | bytes 104448 | tf_op jit(solution)/shard_map/jit(_take)/gather | solution.py:111
  47.4 21.4 %psum.14 = f32[8,72]{1,0:T(8,128)S(1)} all-reduce(f32[8,72]{1,0:T(8,128)S(1)} %dynamic_update_slice.6), channel_id=1, replica_groups=mesh['grid'=16,'orb'=2] {'grid'}, use_global_device_ids=true, to_apply=%region_0.2 | all-reduce | flops 576 | bytes 4608 | tf_op jit(solution)/shard_map/psum | solution.py:83
  69.0 1.2 copy.166
  70.8 0.5 copy-done.1
  72.0 0.6 copy-done.2
  72.5 15.0 %multiply_add_fusion = f32[8,55296]{1,0:T(8,128)S(1)} fusion(bf16[8,55296]{1,0:T(8,128)(2,1)S(1)} %copy-done.2, bf16[8,55296]{1,0:T(8,128)(2,1)S(1)} %collective-permute-done, bf16[8,55296]{1,0:T(8,128)(2,1)S(1)} %copy-done, bf16[8,110592]{1,0:T(8,128)(2,1)S(1)} %get-tuple-element.10, bf16[8,110592]{1,0:T(8,128)(2,1)S(1)} %constant_dynamic-update-slice_fusion, ...), kind=kLoop, calls=%fused_computation.186 | loop fusion | flops 47333376 | bytes 36052992 | tf_op jit(solution)/shard_map/add | solution.py:132
  87.5 14.0 %copy.165 = f32[8,55296]{0,1:T(8,128)} copy(f32[8,55296]{1,0:T(8,128)S(1)} %multiply_add_fusion) | data formatting | bytes 3538944 | tf_op jit(solution)/shard_map/add | solution.py:132
  101.5 26.6 %scatter_fusion = f32[8,55296]{0,1:T(8,128)} fusion(f32[8,55296]{0,1:T(8,128)} %copy.165, s32[1536]{0:T(1024)S(1)} %compare_select_fusion, f32[1536,8]{1,0:T(8,128)} %copy.166), kind=kCustom, calls=%fused_computation.3 | custom fusion | flops 12288 | bytes 153600 | tf_op jit(solution)/shard_map/scatter-add | solution.py:131
  128.2 15.5 %copy.167 = f32[8,55296]{1,0:T(8,128)S(1)} copy(f32[8,55296]{0,1:T(8,128)} %scatter_fusion) | data formatting | bytes 3538944 | tf_op jit(solution)/shard_map/scatter-add | solution.py:131
  143.7 1.4 fusion.105
  145.2 3.9 %collective-permute-start.3 = (f32[8,55296]{1,0:T(8,128)}, f32[8,55296]{1,0:T(8,128)}, u32[]{:S(2)}, u32[]{:S(2)}) collective-permute-start(f32[8,55296]{1,0:T(8,128)} %fusion.105), channel_id=1, source_target_pairs={{0,2},{2,4},{4,6},{6,8},{8,10},{10,12},{12,14},{14,16},{16,18},{18... | collective-permute-start | bytes 5308424 | tf_op jit(solution)/shard_map/ppermute | solution.py:30
  149.0 3.2 collective-permute-start.2
  152.3 0.7 broadcast_multiply_fusion
  153.0 13.8 %copy.168 = f32[8,55296]{0,1:T(8,128)} copy(f32[8,55296]{1,0:T(8,128)} %fusion.105) | data formatting | bytes 3538944 | tf_op jit(solution)/shard_map/div | solution.py:137
  166.8 12.1 %gather_fusion.2 = f32[1536,8]{1,0:T(8,128)S(1)} fusion(f32[8,55296]{0,1:T(8,128)} %copy.168, s32[2048]{0:T(1024)} %copy-done.36), kind=kCustom, calls=%fused_computation.1.clone | custom fusion | bytes 104448 | tf_op jit(solution)/shard_map/jit(_take)/gather | solution.py:111
  178.9 0.9 copy.169
  179.7 1.0 fusion.132
  181.0 28.8 %psum.15 = f32[8,72]{1,0:T(8,128)S(1)} all-reduce(f32[8,72]{1,0:T(8,128)S(1)} %dynamic_update_slice.7), channel_id=1, replica_groups=mesh['grid'=16,'orb'=2] {'grid'}, use_global_device_ids=true, to_apply=%region_2.4 | all-reduce | flops 576 | bytes 4608 | tf_op jit(solution)/shard_map/psum | solution.py:83
  209.8 1.6 fusion.5
  211.4 1.1 copy.171
  212.5 48.9 %fusion.14 = f32[8,55296]{1,0:T(8,128)} fusion(f32[8,55296]{1,0:T(8,128)} %collective-permute-done.3, f32[8,55296]{1,0:T(8,128)} %fusion.105, f32[8,55296]{1,0:T(8,128)} %collective-permute-done.2, f32[8,55296]{1,0:T(8,128)S(1)} %copy.167, bf16[8,55296]{1,0:T(8,128)(2,1)S(1)} %copy-done, f32[55296]{0:T(1024)} %broadcast_multiply_fusion, ...), kind=kLoop, calls=%fused_computation.90 | loop fusion | flops 47333376 | bytes 11280384 | tf_op jit(solution)/shard_map/add | solution.py:132
  261.4 13.9 %copy.170 = f32[8,55296]{0,1:T(8,128)} copy(f32[8,55296]{1,0:T(8,128)} %fusion.14) | data formatting | bytes 3538944 | tf_op jit(solution)/shard_map/add | solution.py:132
  275.2 26.2 %scatter_fusion.1 = f32[8,55296]{0,1:T(8,128)} fusion(f32[8,55296]{0,1:T(8,128)} %copy.170, s32[1536]{0:T(1024)S(1)} %copy-done.34, f32[1536,8]{1,0:T(8,128)S(1)} %copy.171), kind=kCustom, calls=%fused_computation.4 | custom fusion | flops 12288 | bytes 153600 | tf_op jit(solution)/shard_map/scatter-add | solution.py:131
  301.5 15.4 %copy.172 = f32[8,55296]{1,0:T(8,128)} copy(f32[8,55296]{0,1:T(8,128)} %scatter_fusion.1) | data formatting | bytes 3538944 | tf_op jit(solution)/shard_map/scatter-add | solution.py:131
  316.9 2.8 subtract_convert_fusion
  319.9 34.7 %all-gather.2.cloned.1.call-done = bf16[16,55296]{1,0:T(8,128)(2,1)} async-done(((bf16[8,55296]{1,0:T(8,128)(2,1)}), bf16[16,55296]{1,0:T(8,128)(2,1)}) %all-gather.2.cloned.1.call-update) | async-done | bytes 1769488 | tf_op jit(solution)/shard_map/all_gather | solution.py:144
  354.6 4.0 %gather_fusion = bf16[4,8,55296]{2,1,0:T(8,128)(2,1)} fusion(bf16[2,8,55296]{2,1,0:T(8,128)(2,1)} %bitcast.26, s32[1024]{0:T(1024)S(1)} %pad_clamp_fusion.1), kind=kCustom, calls=%fused_computation.2 | custom fusion | bytes 7077904 | tf_op jit(solution)/shard_map/jit(_take)/gather | solution.py:145
  358.6 2.9 fusion.1
  361.7 0.7 fusion.2
  362.4 0.7 fusion.3
  363.2 0.7 fusion
  363.9 2.2 pad_maximum_fusion.2
  (109 shorter events, 2.8 us)
Async XLA Ops:
  7.2 16.3 %copy-start = (bf16[8,55296]{1,0:T(8,128)(2,1)S(1)}, bf16[8,55296]{1,0:T(8,128)(2,1)}, u32[]{:S(2)}) copy-start(bf16[8,55296]{1,0:T(8,128)(2,1)} %param.10) | copy-start | bytes 2654212
  7.2 347.4 %all-gather.2.cloned.1.call-start = ((), (), s32[]{:S(2)}) async-start(), calls=%async_computation | async-start | bytes 2654208 | tf_op jit(solution)/shard_map/all_gather | solution.py:144
  7.2 64.0 %collective-permute-start = (bf16[8,55296]{1,0:T(8,128)(2,1)}, bf16[8,55296]{1,0:T(8,128)(2,1)S(1)}, u32[]{:S(2)}, u32[]{:S(2)}) collective-permute-start(bf16[8,55296]{1,0:T(8,128)(2,1)} %param.10), channel_id=1, source_target_pairs={{2,0},{4,2},{6,4},{8,6},{10,8},{12,10},{14,12},{16,14},{18,16},{20... | collective-permute-start | bytes 2654216 | tf_op jit(solution)/shard_map/ppermute | solution.py:33
  9.9 60.4 %collective-permute-start.1 = (bf16[8,55296]{1,0:T(8,128)(2,1)}, bf16[8,55296]{1,0:T(8,128)(2,1)S(1)}, u32[]{:S(2)}, u32[]{:S(2)}) collective-permute-start(bf16[8,55296]{1,0:T(8,128)(2,1)} %param.10), channel_id=1, source_target_pairs={{0,2},{2,4},{4,6},{6,8},{8,10},{10,12},{12,14},{14,16},{16,18},{18... | collective-permute-start | bytes 2654216 | tf_op jit(solution)/shard_map/ppermute | solution.py:30
  13.7 33.3 %copy-start.37 = (pred[1536]{0:T(1024)(128)(4,1)}, pred[1536]{0:T(1024)(128)(4,1)S(1)}, u32[]{:S(2)}) copy-start(pred[1536]{0:T(1024)(128)(4,1)S(1)} %compare_and_fusion) | copy-start | bytes 4612
  14.4 87.1 %copy-start.33 = (s32[1536]{0:T(1024)}, s32[1536]{0:T(1024)S(1)}, u32[]{:S(2)}) copy-start(s32[1536]{0:T(1024)S(1)} %compare_select_fusion) | copy-start | bytes 18436
  23.5 23.4 %copy-start.41 = (f32[64]{0:T(128)S(1)}, f32[64]{0:T(128)}, u32[]{:S(2)}) copy-start(f32[64]{0:T(128)} %param.15) | copy-start | bytes 772
  23.5 23.5 %copy-start.38 = (s32[1536]{0:T(1024)S(1)}, s32[1536]{0:T(1024)}, u32[]{:S(2)}) copy-start(s32[1536]{0:T(1024)} %param.12) | copy-start | bytes 18436
  23.5 23.5 %copy-start.35 = (f32[1536]{0:T(1024)S(1)}, f32[1536]{0:T(1024)}, u32[]{:S(2)}) copy-start(f32[1536]{0:T(1024)} %param.14) | copy-start | bytes 18436
  35.0 35.4 %copy-start.36 = (s32[2048]{0:T(1024)}, s32[2048]{0:T(1024)S(1)}, u32[]{:S(2)}) copy-start(s32[2048]{0:T(1024)S(1)} %pad_clamp_fusion) | copy-start | bytes 24580
  47.0 23.8 %copy-start.39 = (f32[12]{0:T(128)}, f32[12]{0:T(128)S(1)}, u32[]{:S(2)}) copy-start(f32[12]{0:T(128)S(1)} %pad_dynamic-slice_fusion) | copy-start | bytes 148
  47.0 23.8 %copy-start.32 = (s32[1536]{0:T(1024)}, s32[1536]{0:T(1024)S(1)}, u32[]{:S(2)}) copy-start(s32[1536]{0:T(1024)S(1)} %broadcast_subtract_fusion) | copy-start | bytes 18436
  70.3 1.0 copy-start.30
  70.3 1.0 copy-start.31
  70.3 0.9 copy-start.1
  70.4 1.2 copy-start.4
  70.4 1.2 copy-start.6
  70.4 1.2 copy-start.8
  70.4 1.2 copy-start.10
  70.4 1.2 copy-start.11
  70.5 1.2 copy-start.12
  70.5 1.2 copy-start.13
  70.5 1.3 copy-start.14
  70.5 1.3 copy-start.15
  70.5 1.3 copy-start.16
  70.5 1.3 copy-start.17
  70.5 1.3 copy-start.18
  70.5 1.3 copy-start.19
  70.5 1.3 copy-start.20
  70.5 1.3 copy-start.21
  70.6 1.3 copy-start.22
  70.6 1.3 copy-start.23
  70.6 1.3 copy-start.24
  70.6 1.3 copy-start.25
  70.6 1.3 copy-start.26
  70.6 1.3 copy-start.27
  70.6 1.3 copy-start.28
  70.6 1.4 copy-start.29
  71.2 1.3 copy-start.2
  143.7 8.5 %copy-start.5 = (f32[55296]{0:T(1024)S(1)}, f32[55296]{0:T(1024)}, u32[]{:S(2)}) copy-start(f32[55296]{0:T(1024)} %param.11) | copy-start | bytes 663556
  145.2 67.3 %collective-permute-start.3 = (f32[8,55296]{1,0:T(8,128)}, f32[8,55296]{1,0:T(8,128)}, u32[]{:S(2)}, u32[]{:S(2)}) collective-permute-start(f32[8,55296]{1,0:T(8,128)} %fusion.105), channel_id=1, source_target_pairs={{0,2},{2,4},{4,6},{6,8},{8,10},{10,12},{12,14},{14,16},{16,18},{18... | collective-permute-start | bytes 5308424 | tf_op jit(solution)/shard_map/ppermute | solution.py:30
  149.0 63.4 %collective-permute-start.2 = (f32[8,55296]{1,0:T(8,128)}, f32[8,55296]{1,0:T(8,128)}, u32[]{:S(2)}, u32[]{:S(2)}) collective-permute-start(f32[8,55296]{1,0:T(8,128)} %fusion.105), channel_id=1, source_target_pairs={{2,0},{4,2},{6,4},{8,6},{10,8},{12,10},{14,12},{16,14},{18,16},{20... | collective-permute-start | bytes 5308424 | tf_op jit(solution)/shard_map/ppermute | solution.py:33
  166.8 45.6 %copy-start.7 = (pred[55296]{0:T(1024)(128)(4,1)S(1)}, pred[55296]{0:T(1024)(128)(4,1)}, u32[]{:S(2)}) copy-start(pred[55296]{0:T(1024)(128)(4,1)} %get-tuple-element.33) | copy-start | bytes 165892
  166.8 45.6 %copy-start.9 = (pred[55296]{0:T(1024)(128)(4,1)S(1)}, pred[55296]{0:T(1024)(128)(4,1)}, u32[]{:S(2)}) copy-start(pred[55296]{0:T(1024)(128)(4,1)} %get-tuple-element.34) | copy-start | bytes 165892
  261.3 13.9 %copy-start.34 = (s32[1536]{0:T(1024)S(1)}, s32[1536]{0:T(1024)}, u32[]{:S(2)}) copy-start(s32[1536]{0:T(1024)} %copy-done.33) | copy-start | bytes 18436
  316.9 2.8 copy-start.42
  354.6 4.0 %copy-start.40 = (bf16[4,8,16]{2,1,0:T(8,128)(2,1)S(1)}, bf16[4,8,16]{2,1,0:T(8,128)(2,1)}, u32[]{:S(2)}) copy-start(bf16[4,8,16]{2,1,0:T(8,128)(2,1)} %param.16) | copy-start | bytes 3076
  358.6 3.1 copy-start.3
Sparse Core Ops, SparseCore 0:
  319.8 34.7 all-gather.1
where the time goes:
time: 377 us; the launch traced here: 373 us
  other arithmetic  135 us (36%)
  local copies, waits for them, and re-layouts  118 us (31%)
  blocking collectives  50.2 us (13%)
  waiting for transfers between devices  34.7 us (9%)
  between operations  14.6 us (4%)
  starting transfers between devices  12.9 us (3%)
  matrix products  7.9 us (2%)
    add x2, other arithmetic, hamiltonian(): return -0.5 * summed + potential * middle + nonlocal_term  63.9 us
    scatter-add x2, other arithmetic, hamiltonian(): nonlocal_term = jnp.zeros_like(middle).at[:, projector_cell].add(spread)  52.9 us
    psum x2, blocking collectives, combine_atoms(): table_sums = lax.psum(atom_table, 'grid')  50.2 us
    all_gather x1, waiting for transfers between devices, body(): everyone = lax.all_gather(filtered, 'orb', axis=0, tiled=True)  34.7 us
    scatter-add x2, local copies, waits for them, and re-layouts, hamiltonian(): nonlocal_term = jnp.zeros_like(middle).at[:, projector_cell].add(spread)  30.9 us
    add x2, local copies, waits for them, and re-layouts, hamiltonian(): return -0.5 * summed + potential * middle + nonlocal_term  27.9 us
    gather x4, local copies, waits for them, and re-layouts, hamiltonian(): gathered = jnp.take(middle, projector_cell, axis=1)  24.8 us
    div x1, local copies, waits for them, and re-layouts, body(): step_field = (first_image - cheb_center * initial) / cheb_half  13.8 us
  transfers between devices with their start and end apart: 5, of which 1 were waited for; matrix products, arithmetic and copies ran while one was open for 18% of the time, Pallas kernels for 0%

commit v1 on v0

v1 whole, which is shorter than its diff:
```python
import functools

import jax
import jax.numpy as jnp
import numpy as np
from jax import lax
from jax.experimental import pallas as pl
from jax.experimental.pallas import tpu as pltpu
from jax.sharding import PartitionSpec as P

NX = 96
NY = 96
REACH = 6
ATOM_DEV = 4
PLANE = NX * NY
BLOCK_ROWS = 8
BLOCK = BLOCK_ROWS * NX
SLOTS = 16
TILE = 256
LANES = 128

stencil_weights = (
    -5369.0 / 1800.0,
    12.0 / 7.0,
    -15.0 / 56.0,
    10.0 / 189.0,
    -1.0 / 112.0,
    2.0 / 1925.0,
    -1.0 / 16632.0,
)
cheb_center = 6.0
cheb_half = 6.0

TAPS = {
    0: ((0, 0, 3), (1, 0, 3), (2, 0, 1)),
    1: ((0, 1, 3), (1, 0, 3), (2, 0, 2)),
    2: ((0, 2, 3), (1, 0, 3), (2, 0, 3)),
}


def plane_taps():
    cell = np.arange(BLOCK)
    row, column = cell // NX, cell % NX
    out = np.zeros((3, BLOCK, BLOCK), np.float64)
    for block in range(3):
        source_row = row + (block - 1) * BLOCK_ROWS
        jump_row = np.abs(source_row[:, None] - row[None, :])
        jump_column = np.abs(column[:, None] - column[None, :])
        for distance in range(1, REACH + 1):
            hit = ((jump_row == distance) & (jump_column == 0)) | (
                (jump_row == 0) & (jump_column == distance)
            )
            out[block][hit] = stencil_weights[distance] / stencil_weights[1]
    return out.astype(jnp.bfloat16)


def z_sum(planes, target, first):
    total = None
    for at, values in enumerate(planes):
        distance = abs(first + at - target)
        if 1 <= distance <= REACH:
            term = stencil_weights[distance] * values
            total = term if total is None else total + term
    return total


def block_diagonal(depth, rows, columns):
    row = lax.broadcasted_iota(jnp.int32, (depth * rows, depth * columns), 0) // rows
    column = lax.broadcasted_iota(jnp.int32, (depth * rows, depth * columns), 1) // columns
    return row == column


def pack_planes(source, target, depth, panel, blocks, part):
    stride = depth * panel
    zero = jnp.zeros((stride, BLOCK), jnp.bfloat16)
    target[0:stride, :] = zero
    target[(blocks + 1) * stride : (blocks + 2) * stride, :] = zero

    def one(block, carry):
        for pair in range(depth // 2):
            halves = []
            for plane in (2 * pair, 2 * pair + 1):
                start = pl.multiple_of(plane * PLANE + block * BLOCK, LANES)
                halves.append(part(source[:, pl.ds(start, BLOCK)].astype(jnp.float32)))
            packed = jnp.concatenate(halves, axis=0).astype(jnp.bfloat16)
            start = pl.multiple_of((block + 1) * stride + pair * 2 * panel, 16)
            target[pl.ds(start, 2 * panel), :] = packed
        return carry

    lax.fori_loop(0, blocks, one, 0)


def apply_taps(packs, taps, out, stride, blocks):
    rows = blocks * stride
    for tile, parts in TAPS.items():
        total = None
        for packed in packs:
            for block, low, high in parts:
                term = jnp.dot(
                    packed[block * stride : block * stride + rows, low * TILE : high * TILE],
                    taps[block, low * TILE : high * TILE, tile * TILE : (tile + 1) * TILE],
                    preferred_element_type=jnp.float32,
                )
                total = term if total is None else total + term
        out[:, tile * TILE : (tile + 1) * TILE] = total


def atom_partial(packs, table, out, depth, panel, blocks):
    stride, atoms = depth * panel, depth * SLOTS

    def one(block, total):
        weights = table[pl.ds(pl.multiple_of(block * atoms, 16), atoms), :]
        for packed in packs:
            rows = packed[pl.ds(pl.multiple_of((block + 1) * stride, 16), stride), :]
            total = total + lax.dot_general(
                rows, weights, (((1,), (1,)), ((), ())), preferred_element_type=jnp.float32
            )
        return total

    total = lax.fori_loop(0, blocks, one, jnp.zeros((stride, atoms), jnp.float32))
    total = jnp.where(block_diagonal(depth, panel, SLOTS), total, 0.0)
    folded = total[0:panel, :]
    for plane in range(1, depth):
        folded = folded + total[plane * panel : (plane + 1) * panel, :]
    slot = lax.broadcasted_iota(jnp.int32, (atoms, LANES), 0) % SLOTS
    lane = lax.broadcasted_iota(jnp.int32, (atoms, LANES), 1)
    out[...] = jnp.dot(
        folded,
        (slot == lane).astype(jnp.float32),
        precision=lax.Precision.HIGHEST,
        preferred_element_type=jnp.float32,
    )


def spread_rows(tables, strength, depth, panel):
    total = None
    for offset, table in tables.items():
        value = table[...]
        if offset:
            value = pltpu.roll(value, (offset * ATOM_DEV) % LANES, 1)
        total = value if total is None else total + value
    lane = lax.broadcasted_iota(jnp.int32, total.shape, 1)
    total = jnp.where(lane < 3 * ATOM_DEV, total * strength[...], 0.0)
    slot = lax.broadcasted_iota(jnp.int32, (LANES, depth * SLOTS), 1) % SLOTS
    lane = lax.broadcasted_iota(jnp.int32, (LANES, depth * SLOTS), 0)
    wide = jnp.dot(
        total,
        (slot == lane).astype(jnp.float32),
        precision=lax.Precision.HIGHEST,
        preferred_element_type=jnp.float32,
    )
    wide = jnp.where(
        block_diagonal(depth, panel, SLOTS), jnp.concatenate([wide] * depth, axis=0), 0.0
    )
    high = wide.astype(jnp.bfloat16)
    return high, (wide - high.astype(jnp.float32)).astype(jnp.bfloat16)


def local_part(field, potential, sums, out, depth, panel, blocks, finish):
    def one(block, carry):
        for part in range(BLOCK // TILE):
            starts = [
                pl.multiple_of(plane * PLANE + block * BLOCK + part * TILE, LANES)
                for plane in range(depth)
            ]
            planes = [field[:, pl.ds(start, TILE)].astype(jnp.float32) for start in starts]
            for plane in range(depth):
                row = pl.multiple_of(block * depth * panel + plane * panel, 8)
                lap = (
                    3.0 * stencil_weights[0] * planes[plane]
                    + stencil_weights[1]
                    * sums[pl.ds(row, panel), part * TILE : (part + 1) * TILE]
                    + z_sum(planes, plane, 0)
                )
                first = plane * (PLANE // LANES) + block * (BLOCK // LANES) + part * 2
                level = jnp.concatenate(
                    [
                        jnp.broadcast_to(potential[pl.ds(first + k, 1), :], (panel, LANES))
                        for k in range(TILE // LANES)
                    ],
                    axis=1,
                )
                cells = pl.ds(starts[plane], TILE)
                out[:, cells] = finish(planes[plane], lap, level, cells)
        return carry

    lax.fori_loop(0, blocks, one, 0)


def halo_part(low, high, rows, table, emit, depth, panel, blocks):
    atoms = depth * SLOTS
    stride = depth * panel
    row_high, row_low = rows

    def one(block, carry):
        weights = table[pl.ds(pl.multiple_of(block * atoms, 16), atoms), :]
        spread = jnp.dot(row_high, weights, preferred_element_type=jnp.float32)
        spread = spread + jnp.dot(row_low, weights, preferred_element_type=jnp.float32)
        for part in range(BLOCK // TILE):
            cut = slice(part * TILE, (part + 1) * TILE)
            starts = [
                pl.multiple_of(plane * PLANE + block * BLOCK + part * TILE, LANES)
                for plane in range(depth)
            ]
            below = [low[:, pl.ds(start, TILE)].astype(jnp.float32) for start in starts]
            sums = [z_sum(below, plane, -depth) for plane in range(depth)]
            above = [high[:, pl.ds(start, TILE)].astype(jnp.float32) for start in starts]
            for plane in range(depth):
                lap = sums[plane] + z_sum(above, plane, depth)
                near = spread[plane * panel : (plane + 1) * panel, cut]
                emit(pl.ds(starts[plane], TILE), lap, near)
        return carry

    lax.fori_loop(0, blocks, one, 0)


def first_local_kernel(
    depth, panel, blocks, field, potential, row_ref, lane_ref, value_ref, taps,
    table, partial, out, packed, sums, place,
):
    stride, atoms = depth * panel, depth * SLOTS
    entries = row_ref.shape[1]
    lane = lax.broadcasted_iota(jnp.int32, (BLOCK, entries), 0)
    place[...] = jnp.where(lane == lane_ref[...], value_ref[...], 0.0).astype(jnp.bfloat16)
    chunk = 4 * atoms

    def build(at, carry):
        first = pl.multiple_of(at * chunk, 16)
        row = lax.broadcasted_iota(jnp.int32, (chunk, entries), 0) + first
        hit = jnp.where(row == row_ref[...], 1.0, 0.0).astype(jnp.bfloat16)
        table[pl.ds(first, chunk), :] = lax.dot_general(
            hit, place[...], (((1,), (1,)), ((), ())), preferred_element_type=jnp.float32
        ).astype(jnp.bfloat16)
        return carry

    lax.fori_loop(0, blocks * atoms // chunk, build, 0)
    pack_planes(field, packed, depth, panel, blocks, lambda x: x)
    atom_partial((packed,), table, partial, depth, panel, blocks)
    apply_taps((packed,), taps, sums, stride, blocks)

    def finish(values, lap, level, cells):
        return (-0.5 * lap + (level - cheb_center) * values) * (1.0 / cheb_half)

    local_part(field, potential, sums, out, depth, panel, blocks, finish)


def first_halo_kernel(
    depth, panel, blocks, local, low, high, table, strength, *refs
):
    *tables, out, sent = refs
    tables = dict(zip((0, 1, -1, 2, -2), tables))
    rows = spread_rows(tables, strength, depth, panel)

    def emit(cells, lap, near):
        value = local[:, cells] + (near - 0.5 * lap) * (1.0 / cheb_half)
        out[:, cells] = value
        sent[:, cells] = value.astype(jnp.bfloat16)

    halo_part(low, high, rows, table, emit, depth, panel, blocks)


def second_local_kernel(
    depth, panel, blocks, field, initial, potential, table, taps,
    partial, out, packed, rest, sums,
):
    stride = depth * panel
    pack_planes(field, packed, depth, panel, blocks, lambda x: x)
    pack_planes(
        field, rest, depth, panel, blocks,
        lambda x: x - x.astype(jnp.bfloat16).astype(jnp.float32),
    )
    packs = (packed, rest)
    atom_partial(packs, table, partial, depth, panel, blocks)
    apply_taps(packs, taps, sums, stride, blocks)

    def finish(values, lap, level, cells):
        return (-0.5 * lap + (level - cheb_center) * values) * (2.0 / cheb_half) - initial[
            :, cells
        ].astype(jnp.float32)

    local_part(field, potential, sums, out, depth, panel, blocks, finish)


def second_halo_kernel(depth, panel, blocks, local, low, high, table, strength, *refs):
    *tables, out = refs
    tables = dict(zip((0, 1, -1, 2, -2), tables))
    rows = spread_rows(tables, strength, depth, panel)

    def emit(cells, lap, near):
        value = local[:, cells] + (near - 0.5 * lap) * (2.0 / cheb_half)
        out[:, cells] = value.astype(jnp.bfloat16)

    halo_part(low, high, rows, table, emit, depth, panel, blocks)


def rotate_kernel(rotation_high, rotation_low, *refs):
    *panels, out = refs
    rows = jnp.concatenate([p[...].astype(jnp.float32) for p in panels], axis=0).astype(
        jnp.bfloat16
    )
    total = jnp.dot(rotation_high[...], rows, preferred_element_type=jnp.float32)
    total = total + jnp.dot(rotation_low[...], rows, preferred_element_type=jnp.float32)
    out[...] = total.astype(jnp.bfloat16)


def call(kernel, out_shape, scratch, flops, *operands):
    bytes_accessed = sum(int(np.prod(o.shape)) * o.dtype.itemsize for o in operands)
    return pl.pallas_call(
        kernel,
        out_shape=out_shape,
        in_specs=[pl.BlockSpec(memory_space=pltpu.VMEM)] * len(operands),
        out_specs=jax.tree.map(lambda _: pl.BlockSpec(memory_space=pltpu.VMEM), out_shape),
        scratch_shapes=scratch,
        compiler_params=pltpu.CompilerParams(vmem_limit_bytes=48 * 2**20),
        cost_estimate=pl.CostEstimate(
            flops=flops, bytes_accessed=bytes_accessed, transcendentals=0
        ),
    )(*operands)


def shifted(block, offset):
    count = lax.axis_size("grid")
    pairs = [(i, i + offset) for i in range(count) if 0 <= i + offset < count]
    return lax.ppermute(block, "grid", pairs)


def body(
    orbitals,
    potential,
    projector_atom,
    projector_cell,
    projector_value,
    atom_strength,
    ritz_rotation,
    panel_owner,
):
    panel, cells = orbitals.shape
    depth = cells // PLANE
    blocks = PLANE // BLOCK
    stride, atoms = depth * panel, depth * SLOTS
    entries = projector_atom.shape[0]
    slab_index = lax.axis_index("grid")
    taps = jnp.asarray(plane_taps())
    level = potential.reshape(cells // LANES, LANES)

    plane = projector_cell // PLANE
    inside = projector_cell % PLANE
    slot = projector_atom - (slab_index - 1) * ATOM_DEV
    row_at = ((inside // BLOCK) * depth + plane) * SLOTS + slot
    lane_at = inside % BLOCK
    padded_strength = jnp.pad(atom_strength, (ATOM_DEV, LANES))
    strength = lax.dynamic_slice_in_dim(padded_strength, slab_index * ATOM_DEV, LANES)[None, :]

    bf16, f32 = jnp.bfloat16, jnp.float32
    shape = jax.ShapeDtypeStruct
    field = shape((panel, cells), f32)
    narrow = shape((panel, cells), bf16)
    sums = shape((panel, LANES), f32)
    packed = pltpu.VMEM(((blocks + 2) * stride, BLOCK), bf16)
    tap_sums = pltpu.VMEM((blocks * stride, BLOCK), f32)
    sizes = (depth, panel, blocks)

    below, above = shifted(orbitals, 1), shifted(orbitals, -1)
    table, partial, local = call(
        functools.partial(first_local_kernel, *sizes),
        (shape((blocks * atoms, BLOCK), bf16), sums, field),
        [packed, tap_sums, pltpu.VMEM((BLOCK, entries), bf16)],
        5 * 10**9,
        orbitals, level, row_at[None, :], lane_at[None, :], projector_value[None, :], taps,
    )
    near = [partial] + [shifted(partial, -k) for k in (1, -1, 2, -2)]
    step_field, sent = call(
        functools.partial(first_halo_kernel, *sizes),
        (field, narrow), [], 10**9,
        local, below, above, table, strength, *near,
    )
    below, above = shifted(sent, 1), shifted(sent, -1)
    partial, local = call(
        functools.partial(second_local_kernel, *sizes),
        (sums, field), [packed, packed, tap_sums], 4 * 10**9,
        step_field, orbitals, level, table, taps,
    )
    near = [partial] + [shifted(partial, -k) for k in (1, -1, 2, -2)]
    filtered = call(
        functools.partial(second_halo_kernel, *sizes),
        narrow, [], 10**9,
        local, below, above, table, strength, *near,
    )

    orb_count = lax.axis_size("orb")
    orb_index = lax.axis_index("orb")
    panels = [filtered]
    for k in range(1, orb_count):
        panels.append(
            lax.ppermute(filtered, "orb", [(i, (i + k) % orb_count) for i in range(orb_count)])
        )
    source = (orb_index - jnp.arange(orb_count)) % orb_count
    chosen = (panel_owner[None, :] == source[:, None]).astype(f32)
    rotation = jnp.sum(
        chosen[:, :, None, None] * ritz_rotation.astype(f32)[None], axis=1
    )
    rotation = rotation.reshape(orb_count * panel, ritz_rotation.shape[2]).T
    rotation_high = rotation.astype(bf16)
    rotation_low = (rotation - rotation_high.astype(f32)).astype(bf16)
    columns = ritz_rotation.shape[2]
    rotated = pl.pallas_call(
        rotate_kernel,
        grid=(depth,),
        out_shape=shape((columns, cells), bf16),
        in_specs=[pl.BlockSpec(rotation.shape, lambda i: (0, 0))] * 2
        + [pl.BlockSpec((panel, PLANE), lambda i: (0, i))] * orb_count,
        out_specs=pl.BlockSpec((columns, PLANE), lambda i: (0, i)),
        compiler_params=pltpu.CompilerParams(vmem_limit_bytes=48 * 2**20),
    )(rotation_high, rotation_low, *panels)
    return (filtered, rotated)


def solution(mesh):
    in_specs = (
        P("orb", "grid"),
        P("grid"),
        P("grid"),
        P("grid"),
        P("grid"),
        P(),
        P(None, None, "orb"),
        P(),
    )
    out_specs = (P("orb", "grid"), P("orb", "grid"))
    return jax.shard_map(body, mesh=mesh, in_specs=in_specs, out_specs=out_specs, check_vma=False)
```

time: 377 us -> 100 us (0.27)
  the two profiles are of different devices: /device:TPU:11 before, /device:TPU:6 now
where the time goes in v1:
time: 100 us; the launch traced here: 99.7 us
  starting transfers between devices  35 us (35%)
  Pallas kernels  32.7 us (33%)
  waiting for transfers between devices  24.2 us (24%)
  local copies, waits for them, and re-layouts  6.03 us (6%)
    ppermute x12, starting transfers between devices, shifted(): return lax.ppermute(block, 'grid', pairs)  34.4 us
    pallas_call x4, Pallas kernels, call(): pl.pallas_call(kernel, out_shape=out_shape, in_specs=[pl.BlockSpec(memory...  29.4 us
    ppermute x1, waiting for transfers between devices, body(): lax.ppermute(filtered, 'orb', [(i, (i + k) % orb_count) for i in range(or...  21.2 us
    unnamed x18, local copies, waits for them, and re-layouts  4.5 us
    pallas_call x1, Pallas kernels, body(): pl.pallas_call(rotate_kernel, grid=(depth,), out_shape=shape((columns, ce...  3.3 us
    ppermute x12, waiting for transfers between devices, shifted(): return lax.ppermute(block, 'grid', pairs)  3.08 us
  transfers between devices with their start and end apart: 13, of which 3 were waited for; matrix products, arithmetic and copies ran while one was open for 2% of the time, Pallas kernels for 22%

profile of v1, /device:TPU:6, one launch (start us, length us, event | category | flops | bytes accessed | tf_op | source)
XLA Modules:
  0.0 99.7 jit_solution(5696005393840456401)
XLA Ops:
  0.6 1.9 %collective-permute-start = (bf16[8,55296]{1,0:T(8,128)(2,1)}, bf16[8,55296]{1,0:T(8,128)(2,1)S(1)}, u32[]{:S(2)}, u32[]{:S(2)}) collective-permute-start(bf16[8,55296]{1,0:T(8,128)(2,1)} %initial.1), channel_id=1, source_target_pairs={{0,2},{2,4},{4,6},{6,8},{8,10},{10,12},{12,14},{14,16},{16,18},{18... | collective-permute-start | bytes 2654216 | tf_op jit(solution)/shard_map/ppermute | solution.py:324
  2.6 3.6 %collective-permute-start.1 = (bf16[8,55296]{1,0:T(8,128)(2,1)}, bf16[8,55296]{1,0:T(8,128)(2,1)S(1)}, u32[]{:S(2)}, u32[]{:S(2)}) collective-permute-start(bf16[8,55296]{1,0:T(8,128)(2,1)} %initial.1), channel_id=1, source_target_pairs={{2,0},{4,2},{6,4},{8,6},{10,8},{12,10},{14,12},{16,14},{18,16},{20... | collective-permute-start | bytes 2654216 | tf_op jit(solution)/shard_map/ppermute | solution.py:324
  6.2 0.7 add_select_fusion
  7.0 0.7 broadcast_in_dim.18.value_ref
  7.7 1.2 %copy-done.3 = bf16[8,55296]{1,0:T(8,128)(2,1)S(1)} copy-done((bf16[8,55296]{1,0:T(8,128)(2,1)S(1)}, bf16[8,55296]{1,0:T(8,128)(2,1)}, u32[]{:S(2)}) %copy-start.3) | copy-done | bytes 884760
  8.9 0.9 copy-done.5
  9.8 11.3 %shard_map.104 = (bf16[1152,768]{1,0:T(8,128)(2,1)S(1)}, f32[8,128]{1,0:T(8,128)S(1)}, f32[8,55296]{1,0:T(8,128)S(1)}) custom-call(bf16[8,55296]{1,0:T(8,128)(2,1)S(1)} %copy-done.3, f32[432,128]{1,0:T(8,128)S(1)} %bitcast.10, s32[1,1536]{1,0:T(1,128)S(1)} %broadcast_in_dim.16.row_ref, s32[1,1536]{1,0:T(1,128)S(1)} %broadcast_in_dim.17.lane_ref, ...), custom_call_target="tpu_custom_call" | custom-call | flops 5000000000 | bytes 4663296 | tf_op jit(solution)/shard_map/pallas_call | solution.py:308
  21.1 0.0 copy-start
  21.1 1.2 %copy-done = bf16[1152,768]{1,0:T(8,128)(2,1)} copy-done((bf16[1152,768]{1,0:T(8,128)(2,1)}, bf16[1152,768]{1,0:T(8,128)(2,1)S(1)}, u32[]{:S(2)}) %copy-start) | copy-done | bytes 1769496
  22.3 1.9 %collective-permute-start.2 = (f32[8,128]{1,0:T(8,128)S(1)}, f32[8,128]{1,0:T(8,128)S(1)}, u32[]{:S(2)}, u32[]{:S(2)}) collective-permute-start(f32[8,128]{1,0:T(8,128)S(1)} %get-tuple-element.11.refs_0_), channel_id=1, source_target_pairs={{2,0},{4,2},{6,4},{8,6},{10,8},{12,10},{14,12},{16,14},{18,16},{20... | collective-permute-start | bytes 12296 | tf_op jit(solution)/shard_map/ppermute | solution.py:324
  24.2 2.4 %collective-permute-start.3 = (f32[8,128]{1,0:T(8,128)S(1)}, f32[8,128]{1,0:T(8,128)S(1)}, u32[]{:S(2)}, u32[]{:S(2)}) collective-permute-start(f32[8,128]{1,0:T(8,128)S(1)} %get-tuple-element.11.refs_0_), channel_id=1, source_target_pairs={{0,2},{2,4},{4,6},{6,8},{8,10},{10,12},{12,14},{14,16},{16,18},{18... | collective-permute-start | bytes 12296 | tf_op jit(solution)/shard_map/ppermute | solution.py:324
  26.6 1.9 %collective-permute-start.4 = (f32[8,128]{1,0:T(8,128)S(1)}, f32[8,128]{1,0:T(8,128)S(1)}, u32[]{:S(2)}, u32[]{:S(2)}) collective-permute-start(f32[8,128]{1,0:T(8,128)S(1)} %get-tuple-element.11.refs_0_), channel_id=1, source_target_pairs={{4,0},{6,2},{8,4},{10,6},{12,8},{14,10},{16,12},{18,14},{20,16},{2... | collective-permute-start | bytes 12296 | tf_op jit(solution)/shard_map/ppermute | solution.py:324
  28.5 0.0 collective-permute-done.2.refs_1_
  28.6 4.8 %collective-permute-start.5 = (f32[8,128]{1,0:T(8,128)S(1)}, f32[8,128]{1,0:T(8,128)S(1)}, u32[]{:S(2)}, u32[]{:S(2)}) collective-permute-start(f32[8,128]{1,0:T(8,128)S(1)} %get-tuple-element.11.refs_0_), channel_id=1, source_target_pairs={{0,4},{2,6},{4,8},{6,10},{8,12},{10,14},{12,16},{14,18},{16,20},{1... | collective-permute-start | bytes 12296 | tf_op jit(solution)/shard_map/ppermute | solution.py:324
  33.4 0.7 fusion.7.strength
  34.1 0.0 collective-permute-done.3.refs_2_
  34.1 0.0 collective-permute-done.4.refs_3_
  34.1 0.6 collective-permute-done.5.refs_4_
  34.7 0.0 collective-permute-done.low
  34.7 0.0 collective-permute-done.1.high
  34.7 4.1 %shard_map.105 = (f32[8,55296]{1,0:T(8,128)S(1)}, bf16[8,55296]{1,0:T(8,128)(2,1)S(1)}) custom-call(f32[8,55296]{1,0:T(8,128)S(1)} %get-tuple-element.9.local, bf16[8,55296]{1,0:T(8,128)(2,1)S(1)} %collective-permute-done.low, bf16[8,55296]{1,0:T(8,128)(2,1)S(1)} %collective-permute-done.1.high, bf16[1152,768]{1,0:T(8,128)(2,1)} %copy-done, ...), custom_call_target="tpu_custom_call" | custom-call | flops 1000000000 | bytes 5329408 | tf_op jit(solution)/shard_map/pallas_call | solution.py:308
  38.9 2.9 %collective-permute-start.6 = (bf16[8,55296]{1,0:T(8,128)(2,1)S(1)}, bf16[8,55296]{1,0:T(8,128)(2,1)S(1)}, u32[]{:S(2)}, u32[]{:S(2)}) collective-permute-start(bf16[8,55296]{1,0:T(8,128)(2,1)S(1)} %get-tuple-element.14), channel_id=1, source_target_pairs={{0,2},{2,4},{4,6},{6,8},{8,10},{10,12},{12,14},{14,16},{16,18},{18... | collective-permute-start | bytes 2654216 | tf_op jit(solution)/shard_map/ppermute | solution.py:324
  41.7 2.7 %collective-permute-start.7 = (bf16[8,55296]{1,0:T(8,128)(2,1)S(1)}, bf16[8,55296]{1,0:T(8,128)(2,1)S(1)}, u32[]{:S(2)}, u32[]{:S(2)}) collective-permute-start(bf16[8,55296]{1,0:T(8,128)(2,1)S(1)} %get-tuple-element.14), channel_id=1, source_target_pairs={{2,0},{4,2},{6,4},{8,6},{10,8},{12,10},{14,12},{16,14},{18,16},{20... | collective-permute-start | bytes 2654216 | tf_op jit(solution)/shard_map/ppermute | solution.py:324
  44.4 0.0 copy-done.4
  44.4 0.0 copy-done.6
  44.4 0.0 copy-start.1
  44.5 10.5 %shard_map.106 = (f32[8,128]{1,0:T(8,128)S(1)}, f32[8,55296]{1,0:T(8,128)S(1)}) custom-call(f32[8,55296]{1,0:T(8,128)S(1)} %get-tuple-element.12.field, bf16[8,55296]{1,0:T(8,128)(2,1)S(1)} %copy-done.4, f32[432,128]{1,0:T(8,128)S(1)} %bitcast.11, bf16[1152,768]{1,0:T(8,128)(2,1)} %copy-done, bf16[3,768,768]{2,1,0:T(8,128)(2,1)} %constant.69.clone.taps), custom_call_target="tpu_custom_call" | custom-call | flops 4000000000 | bytes 8183808 | tf_op jit(solution)/shard_map/pallas_call | solution.py:308
  55.0 1.9 %collective-permute-start.10 = (f32[8,128]{1,0:T(8,128)S(1)}, f32[8,128]{1,0:T(8,128)S(1)}, u32[]{:S(2)}, u32[]{:S(2)}) collective-permute-start(f32[8,128]{1,0:T(8,128)S(1)} %get-tuple-element.15.refs_0_), channel_id=1, source_target_pairs={{4,0},{6,2},{8,4},{10,6},{12,8},{14,10},{16,12},{18,14},{20,16},{2... | collective-permute-start | bytes 12296 | tf_op jit(solution)/shard_map/ppermute | solution.py:324
  56.9 6.0 %collective-permute-start.11 = (f32[8,128]{1,0:T(8,128)S(1)}, f32[8,128]{1,0:T(8,128)S(1)}, u32[]{:S(2)}, u32[]{:S(2)}) collective-permute-start(f32[8,128]{1,0:T(8,128)S(1)} %get-tuple-element.15.refs_0_), channel_id=1, source_target_pairs={{0,4},{2,6},{4,8},{6,10},{8,12},{10,14},{12,16},{14,18},{16,20},{1... | collective-permute-start | bytes 12296 | tf_op jit(solution)/shard_map/ppermute | solution.py:324
  62.9 1.9 %collective-permute-start.8 = (f32[8,128]{1,0:T(8,128)S(1)}, f32[8,128]{1,0:T(8,128)S(1)}, u32[]{:S(2)}, u32[]{:S(2)}) collective-permute-start(f32[8,128]{1,0:T(8,128)S(1)} %get-tuple-element.15.refs_0_), channel_id=1, source_target_pairs={{2,0},{4,2},{6,4},{8,6},{10,8},{12,10},{14,12},{16,14},{18,16},{20... | collective-permute-start | bytes 12296 | tf_op jit(solution)/shard_map/ppermute | solution.py:324
  64.8 0.0 collective-permute-done.10.refs_3_
  64.8 2.4 %collective-permute-start.9 = (f32[8,128]{1,0:T(8,128)S(1)}, f32[8,128]{1,0:T(8,128)S(1)}, u32[]{:S(2)}, u32[]{:S(2)}) collective-permute-start(f32[8,128]{1,0:T(8,128)S(1)} %get-tuple-element.15.refs_0_), channel_id=1, source_target_pairs={{0,2},{2,4},{4,6},{6,8},{8,10},{10,12},{12,14},{14,16},{16,18},{18... | collective-permute-start | bytes 12296 | tf_op jit(solution)/shard_map/ppermute | solution.py:324
  67.3 0.0 collective-permute-done.11.refs_4_
  67.3 0.0 collective-permute-done.8.refs_1_
  67.3 2.5 %collective-permute-done.9.refs_2_ = f32[8,128]{1,0:T(8,128)S(1)} collective-permute-done((f32[8,128]{1,0:T(8,128)S(1)}, f32[8,128]{1,0:T(8,128)S(1)}, u32[]{:S(2)}, u32[]{:S(2)}) %collective-permute-start.9) | collective-permute-done | bytes 4128 | tf_op jit(solution)/shard_map/ppermute | solution.py:324
  69.8 0.0 collective-permute-done.6.low
  69.8 0.0 collective-permute-done.7.high
  69.8 0.0 copy-done.1
  69.8 0.0 copy-start.7
  69.8 0.0 copy-start.8
  69.8 3.5 %shard_map.107.refs_0_ = bf16[8,55296]{1,0:T(8,128)(2,1)} custom-call(f32[8,55296]{1,0:T(8,128)S(1)} %get-tuple-element.13.local, bf16[8,55296]{1,0:T(8,128)(2,1)S(1)} %collective-permute-done.6.low, bf16[8,55296]{1,0:T(8,128)(2,1)S(1)} %collective-permute-done.7.high, bf16[1152,768]{1,0:T(8,128)(2,1)S(1)} %copy-done.1, f32[1,128]{1,0:T(1,128)S(1)} %fusion.7.strength, ...), custom_call_target="tpu_custom_call" | custom-call | flops 1000000000 | bytes 5329408 | tf_op jit(solution)/shard_map/pallas_call | solution.py:308
  73.3 0.5 collective-permute-start.12
  73.8 0.1 compare_convert_fusion
  73.9 0.1 multiply_reduce_fusion
  74.0 0.1 copy.12
  74.1 21.2 %collective-permute-done.12.refs_1_ = bf16[8,55296]{1,0:T(8,128)(2,1)S(1)} collective-permute-done((bf16[8,55296]{1,0:T(8,128)(2,1)}, bf16[8,55296]{1,0:T(8,128)(2,1)S(1)}, u32[]{:S(2)}, u32[]{:S(2)}) %collective-permute-start.12) | collective-permute-done | bytes 884768 | tf_op jit(solution)/shard_map/ppermute | solution.py:395
  95.2 1.2 %copy-done.2 = bf16[8,55296]{1,0:T(8,128)(2,1)S(1)} copy-done((bf16[8,55296]{1,0:T(8,128)(2,1)S(1)}, bf16[8,55296]{1,0:T(8,128)(2,1)}, u32[]{:S(2)}) %copy-start.2) | copy-done | bytes 884760
  96.4 3.3 %shard_map.108 = bf16[16,55296]{1,0:T(8,128)(2,1)} custom-call(bf16[16,16]{1,0:T(8,128)(2,1)S(1)} %get-tuple-element.17.rotation_high, bf16[16,16]{1,0:T(8,128)(2,1)S(1)} %get-tuple-element.16.rotation_low, bf16[8,55296]{1,0:T(8,128)(2,1)S(1)} %copy-done.2, bf16[8,55296]{1,0:T(8,128)(2,1)S(1)} %collective-permute-done.12.refs_1_), custom_call_target="tpu_custom_call" | custom-call | tf_op jit(solution)/shard_map/pallas_call | solution.py:406
  (12 shorter events, 0.0 us)
Async XLA Ops:
  0.6 34.1 %collective-permute-start = (bf16[8,55296]{1,0:T(8,128)(2,1)}, bf16[8,55296]{1,0:T(8,128)(2,1)S(1)}, u32[]{:S(2)}, u32[]{:S(2)}) collective-permute-start(bf16[8,55296]{1,0:T(8,128)(2,1)} %initial.1), channel_id=1, source_target_pairs={{0,2},{2,4},{4,6},{6,8},{8,10},{10,12},{12,14},{14,16},{16,18},{18... | collective-permute-start | bytes 2654216 | tf_op jit(solution)/shard_map/ppermute | solution.py:324
  2.6 32.1 %collective-permute-start.1 = (bf16[8,55296]{1,0:T(8,128)(2,1)}, bf16[8,55296]{1,0:T(8,128)(2,1)S(1)}, u32[]{:S(2)}, u32[]{:S(2)}) collective-permute-start(bf16[8,55296]{1,0:T(8,128)(2,1)} %initial.1), channel_id=1, source_target_pairs={{2,0},{4,2},{6,4},{8,6},{10,8},{12,10},{14,12},{16,14},{18,16},{20... | collective-permute-start | bytes 2654216 | tf_op jit(solution)/shard_map/ppermute | solution.py:324
  7.7 1.2 %copy-start.3 = (bf16[8,55296]{1,0:T(8,128)(2,1)S(1)}, bf16[8,55296]{1,0:T(8,128)(2,1)}, u32[]{:S(2)}) copy-start(bf16[8,55296]{1,0:T(8,128)(2,1)} %initial.1) | copy-start | bytes 2654212
  8.9 0.9 copy-start.5
  21.1 1.2 %copy-start = (bf16[1152,768]{1,0:T(8,128)(2,1)}, bf16[1152,768]{1,0:T(8,128)(2,1)S(1)}, u32[]{:S(2)}) copy-start(bf16[1152,768]{1,0:T(8,128)(2,1)S(1)} %get-tuple-element.10.table) | copy-start | bytes 5308420
  22.3 6.3 %collective-permute-start.2 = (f32[8,128]{1,0:T(8,128)S(1)}, f32[8,128]{1,0:T(8,128)S(1)}, u32[]{:S(2)}, u32[]{:S(2)}) collective-permute-start(f32[8,128]{1,0:T(8,128)S(1)} %get-tuple-element.11.refs_0_), channel_id=1, source_target_pairs={{2,0},{4,2},{6,4},{8,6},{10,8},{12,10},{14,12},{16,14},{18,16},{20... | collective-permute-start | bytes 12296 | tf_op jit(solution)/shard_map/ppermute | solution.py:324
  24.2 9.9 %collective-permute-start.3 = (f32[8,128]{1,0:T(8,128)S(1)}, f32[8,128]{1,0:T(8,128)S(1)}, u32[]{:S(2)}, u32[]{:S(2)}) collective-permute-start(f32[8,128]{1,0:T(8,128)S(1)} %get-tuple-element.11.refs_0_), channel_id=1, source_target_pairs={{0,2},{2,4},{4,6},{6,8},{8,10},{10,12},{12,14},{14,16},{16,18},{18... | collective-permute-start | bytes 12296 | tf_op jit(solution)/shard_map/ppermute | solution.py:324
  26.6 7.5 %collective-permute-start.4 = (f32[8,128]{1,0:T(8,128)S(1)}, f32[8,128]{1,0:T(8,128)S(1)}, u32[]{:S(2)}, u32[]{:S(2)}) collective-permute-start(f32[8,128]{1,0:T(8,128)S(1)} %get-tuple-element.11.refs_0_), channel_id=1, source_target_pairs={{4,0},{6,2},{8,4},{10,6},{12,8},{14,10},{16,12},{18,14},{20,16},{2... | collective-permute-start | bytes 12296 | tf_op jit(solution)/shard_map/ppermute | solution.py:324
  28.6 6.1 %collective-permute-start.5 = (f32[8,128]{1,0:T(8,128)S(1)}, f32[8,128]{1,0:T(8,128)S(1)}, u32[]{:S(2)}, u32[]{:S(2)}) collective-permute-start(f32[8,128]{1,0:T(8,128)S(1)} %get-tuple-element.11.refs_0_), channel_id=1, source_target_pairs={{0,4},{2,6},{4,8},{6,10},{8,12},{10,14},{12,16},{14,18},{16,20},{1... | collective-permute-start | bytes 12296 | tf_op jit(solution)/shard_map/ppermute | solution.py:324
  34.7 9.7 %copy-start.4 = (bf16[8,55296]{1,0:T(8,128)(2,1)S(1)}, bf16[8,55296]{1,0:T(8,128)(2,1)}, u32[]{:S(2)}) copy-start(bf16[8,55296]{1,0:T(8,128)(2,1)} %initial.1) | copy-start | bytes 2654212
  34.7 9.7 %copy-start.6 = (f32[55296]{0:T(1024)S(1)}, f32[55296]{0:T(1024)}, u32[]{:S(2)}) copy-start(f32[55296]{0:T(1024)} %param.10) | copy-start | bytes 663556
  38.9 30.9 %collective-permute-start.6 = (bf16[8,55296]{1,0:T(8,128)(2,1)S(1)}, bf16[8,55296]{1,0:T(8,128)(2,1)S(1)}, u32[]{:S(2)}, u32[]{:S(2)}) collective-permute-start(bf16[8,55296]{1,0:T(8,128)(2,1)S(1)} %get-tuple-element.14), channel_id=1, source_target_pairs={{0,2},{2,4},{4,6},{6,8},{8,10},{10,12},{12,14},{14,16},{16,18},{18... | collective-permute-start | bytes 2654216 | tf_op jit(solution)/shard_map/ppermute | solution.py:324
  41.7 28.1 %collective-permute-start.7 = (bf16[8,55296]{1,0:T(8,128)(2,1)S(1)}, bf16[8,55296]{1,0:T(8,128)(2,1)S(1)}, u32[]{:S(2)}, u32[]{:S(2)}) collective-permute-start(bf16[8,55296]{1,0:T(8,128)(2,1)S(1)} %get-tuple-element.14), channel_id=1, source_target_pairs={{2,0},{4,2},{6,4},{8,6},{10,8},{12,10},{14,12},{16,14},{18,16},{20... | collective-permute-start | bytes 2654216 | tf_op jit(solution)/shard_map/ppermute | solution.py:324
  44.4 25.3 %copy-start.1 = (bf16[1152,768]{1,0:T(8,128)(2,1)S(1)}, bf16[1152,768]{1,0:T(8,128)(2,1)}, u32[]{:S(2)}) copy-start(bf16[1152,768]{1,0:T(8,128)(2,1)} %copy-done) | copy-start | bytes 5308420
  55.0 9.9 %collective-permute-start.10 = (f32[8,128]{1,0:T(8,128)S(1)}, f32[8,128]{1,0:T(8,128)S(1)}, u32[]{:S(2)}, u32[]{:S(2)}) collective-permute-start(f32[8,128]{1,0:T(8,128)S(1)} %get-tuple-element.15.refs_0_), channel_id=1, source_target_pairs={{4,0},{6,2},{8,4},{10,6},{12,8},{14,10},{16,12},{18,14},{20,16},{2... | collective-permute-start | bytes 12296 | tf_op jit(solution)/shard_map/ppermute | solution.py:324
  56.9 10.4 %collective-permute-start.11 = (f32[8,128]{1,0:T(8,128)S(1)}, f32[8,128]{1,0:T(8,128)S(1)}, u32[]{:S(2)}, u32[]{:S(2)}) collective-permute-start(f32[8,128]{1,0:T(8,128)S(1)} %get-tuple-element.15.refs_0_), channel_id=1, source_target_pairs={{0,4},{2,6},{4,8},{6,10},{8,12},{10,14},{12,16},{14,18},{16,20},{1... | collective-permute-start | bytes 12296 | tf_op jit(solution)/shard_map/ppermute | solution.py:324
  62.9 4.4 %collective-permute-start.8 = (f32[8,128]{1,0:T(8,128)S(1)}, f32[8,128]{1,0:T(8,128)S(1)}, u32[]{:S(2)}, u32[]{:S(2)}) collective-permute-start(f32[8,128]{1,0:T(8,128)S(1)} %get-tuple-element.15.refs_0_), channel_id=1, source_target_pairs={{2,0},{4,2},{6,4},{8,6},{10,8},{12,10},{14,12},{16,14},{18,16},{20... | collective-permute-start | bytes 12296 | tf_op jit(solution)/shard_map/ppermute | solution.py:324
  64.8 4.9 %collective-permute-start.9 = (f32[8,128]{1,0:T(8,128)S(1)}, f32[8,128]{1,0:T(8,128)S(1)}, u32[]{:S(2)}, u32[]{:S(2)}) collective-permute-start(f32[8,128]{1,0:T(8,128)S(1)} %get-tuple-element.15.refs_0_), channel_id=1, source_target_pairs={{0,2},{2,4},{4,6},{6,8},{8,10},{10,12},{12,14},{14,16},{16,18},{18... | collective-permute-start | bytes 12296 | tf_op jit(solution)/shard_map/ppermute | solution.py:324
  69.8 4.0 %copy-start.7 = (bf16[4,8,16]{2,1,0:T(8,128)(2,1)S(1)}, bf16[4,8,16]{2,1,0:T(8,128)(2,1)}, u32[]{:S(2)}) copy-start(bf16[4,8,16]{2,1,0:T(8,128)(2,1)} %param.15) | copy-start | bytes 3076
  69.8 4.0 %copy-start.8 = (s32[4]{0:T(128)S(1)}, s32[4]{0:T(128)}, u32[]{:S(2)}) copy-start(s32[4]{0:T(128)} %param.16) | copy-start | bytes 52
  73.3 22.0 %collective-permute-start.12 = (bf16[8,55296]{1,0:T(8,128)(2,1)}, bf16[8,55296]{1,0:T(8,128)(2,1)S(1)}, u32[]{:S(2)}, u32[]{:S(2)}) collective-permute-start(bf16[8,55296]{1,0:T(8,128)(2,1)} %shard_map.107.refs_0_), channel_id=1, source_target_pairs={{0,1},{1,0},{2,3},{3,2},{4,5},{5,4},{6,7},{7,6},{8,9},{9,8},{10,11... | collective-permute-start | bytes 2654216 | tf_op jit(solution)/shard_map/ppermute | solution.py:395
  95.2 1.2 %copy-start.2 = (bf16[8,55296]{1,0:T(8,128)(2,1)S(1)}, bf16[8,55296]{1,0:T(8,128)(2,1)}, u32[]{:S(2)}) copy-start(bf16[8,55296]{1,0:T(8,128)(2,1)} %shard_map.107.refs_0_) | copy-start | bytes 2654212

commit v2 on v1

v2 whole, which is shorter than its diff:
```python
import functools

import jax
import jax.numpy as jnp
import numpy as np
from jax import lax
from jax.experimental import pallas as pl
from jax.experimental.pallas import tpu as pltpu
from jax.sharding import PartitionSpec as P

NX = 96
NY = 96
REACH = 6
ATOM_DEV = 4
PLANE = NX * NY
BLOCK_ROWS = 8
BLOCK = BLOCK_ROWS * NX
SLOTS = 16
TILE = 256
LANES = 128
VMEM_LIMIT = 24 * 2**20

stencil_weights = (
    -5369.0 / 1800.0,
    12.0 / 7.0,
    -15.0 / 56.0,
    10.0 / 189.0,
    -1.0 / 112.0,
    2.0 / 1925.0,
    -1.0 / 16632.0,
)
cheb_center = 6.0
cheb_half = 6.0

TAPS = {
    0: ((0, 0, 3), (1, 0, 3), (2, 0, 1)),
    1: ((0, 1, 3), (1, 0, 3), (2, 0, 2)),
    2: ((0, 2, 3), (1, 0, 3), (2, 0, 3)),
}


def plane_taps():
    cell = np.arange(BLOCK)
    row, column = cell // NX, cell % NX
    out = np.zeros((3, BLOCK, BLOCK), np.float64)
    for block in range(3):
        source_row = row + (block - 1) * BLOCK_ROWS
        jump_row = np.abs(source_row[:, None] - row[None, :])
        jump_column = np.abs(column[:, None] - column[None, :])
        for distance in range(1, REACH + 1):
            hit = ((jump_row == distance) & (jump_column == 0)) | (
                (jump_row == 0) & (jump_column == distance)
            )
            out[block][hit] = stencil_weights[distance] / stencil_weights[1]
    return out.astype(jnp.bfloat16)


def z_sum(planes, target, first):
    total = None
    for at, values in enumerate(planes):
        distance = abs(first + at - target)
        if 1 <= distance <= REACH:
            term = stencil_weights[distance] * values
            total = term if total is None else total + term
    return total


def block_diagonal(depth, rows, columns):
    row = lax.broadcasted_iota(jnp.int32, (depth * rows, depth * columns), 0) // rows
    column = lax.broadcasted_iota(jnp.int32, (depth * rows, depth * columns), 1) // columns
    return row == column


def split(values):
    high = values.astype(jnp.bfloat16)
    return high, (values - high.astype(jnp.float32)).astype(jnp.bfloat16)


def aligned(index, multiple):
    return pl.multiple_of(index, multiple)


class Sizes:
    def __init__(self, panel, cells, entries):
        self.panel, self.cells, self.entries = panel, cells, entries
        self.depth = cells // PLANE
        self.blocks = PLANE // BLOCK
        self.stride = self.depth * panel
        self.atoms = self.depth * SLOTS
        self.half = panel // 2
        self.half_plane = PLANE // 2
        self.half_blocks = self.blocks // 2


def pack_planes(n, source, targets):
    zero = jnp.zeros((n.stride, BLOCK), jnp.bfloat16)
    for target in targets:
        target[0 : n.stride, :] = zero
        target[(n.blocks + 1) * n.stride : (n.blocks + 2) * n.stride, :] = zero

    def one(block, carry):
        for pair in range(n.depth // 2):
            halves = []
            for plane in (2 * pair, 2 * pair + 1):
                start = aligned(plane * PLANE + block * BLOCK, LANES)
                halves.append(source[:, pl.ds(start, BLOCK)].astype(jnp.float32))
            parts = split(jnp.concatenate(halves, axis=0))
            start = aligned((block + 1) * n.stride + pair * 2 * n.panel, 16)
            for target, part in zip(targets, parts):
                target[pl.ds(start, 2 * n.panel), :] = part
        return carry

    lax.fori_loop(0, n.blocks, one, 0)


def apply_taps(n, packs, taps, out):
    rows = n.blocks * n.stride
    for tile, parts in TAPS.items():
        total = None
        for packed in packs:
            for block, low, high in parts:
                term = jnp.dot(
                    packed[block * n.stride : block * n.stride + rows, low * TILE : high * TILE],
                    taps[block, low * TILE : high * TILE, tile * TILE : (tile + 1) * TILE],
                    preferred_element_type=jnp.float32,
                )
                total = term if total is None else total + term
        out[:, tile * TILE : (tile + 1) * TILE] = total


def atom_partial(n, packs, table, out):
    total = None
    for block in range(n.blocks):
        weights = table[block * n.atoms : (block + 1) * n.atoms, :]
        for packed in packs:
            rows = packed[(block + 1) * n.stride : (block + 2) * n.stride, :]
            term = lax.dot_general(
                rows, weights, (((1,), (1,)), ((), ())), preferred_element_type=jnp.float32
            )
            total = term if total is None else total + term
    total = jnp.where(block_diagonal(n.depth, n.panel, SLOTS), total, 0.0)
    folded = total[0 : n.panel, :]
    for plane in range(1, n.depth):
        folded = folded + total[plane * n.panel : (plane + 1) * n.panel, :]
    slot = lax.broadcasted_iota(jnp.int32, (n.atoms, LANES), 0) % SLOTS
    lane = lax.broadcasted_iota(jnp.int32, (n.atoms, LANES), 1)
    out[...] = jnp.dot(
        folded,
        (slot == lane).astype(jnp.float32),
        precision=lax.Precision.HIGHEST,
        preferred_element_type=jnp.float32,
    )


def near_sums(n, tables, strength):
    own, partner, far, partner_far = tables
    outward = 2 * (lax.axis_index("grid") % 2) - 1
    slab = lax.axis_index("grid")
    total = own[...]
    for table, offset in (
        (partner[...], -outward),
        (far[0 : n.panel, :], outward),
        (far[n.panel : 2 * n.panel, :], 2 * outward),
        (partner_far[0 : n.panel, :], -2 * outward),
        (partner_far[n.panel : 2 * n.panel, :], -3 * outward),
    ):
        total = total + pltpu.roll(table, (offset * ATOM_DEV + LANES) % LANES, 1)
    count = strength.shape[1]
    atom = lax.broadcasted_iota(jnp.int32, (count, LANES), 0)
    slot = lax.broadcasted_iota(jnp.int32, (count, LANES), 1) + (slab - 1) * ATOM_DEV
    near = jnp.dot(
        jnp.broadcast_to(strength[...], (n.panel, count)),
        (atom == slot).astype(jnp.float32),
        precision=lax.Precision.HIGHEST,
        preferred_element_type=jnp.float32,
    )
    lane = lax.broadcasted_iota(jnp.int32, total.shape, 1)
    total = jnp.where(lane < 3 * ATOM_DEV, total * near, 0.0)
    slot = lax.broadcasted_iota(jnp.int32, (LANES, n.atoms), 1) % SLOTS
    lane = lax.broadcasted_iota(jnp.int32, (LANES, n.atoms), 0)
    return jnp.dot(
        total,
        (slot == lane).astype(jnp.float32),
        precision=lax.Precision.HIGHEST,
        preferred_element_type=jnp.float32,
    )


def spread_of(n, rows, weights):
    both = jnp.dot(rows, weights, preferred_element_type=jnp.float32)
    return both[0 : n.stride, :] + both[n.stride : 2 * n.stride, :]


def halves_of(n, values):
    low, high = values
    return [
        jnp.concatenate([low[c : c + n.half, :], high[c : c + n.half, :]], axis=0)
        for c in (0, n.half)
    ]


def by_side(inner, outer, run):
    odd = lax.axis_index("grid") % 2
    pl.when(odd == 0)(functools.partial(run, outer, inner))
    pl.when(odd == 1)(functools.partial(run, inner, outer))


def tile_loop(n, one_tile):
    def one(block, carry):
        for part in range(BLOCK // TILE):
            one_tile(block, part)
        return carry

    lax.fori_loop(0, n.half_blocks, one, 0)


def level_of(n, potential, plane, block, part):
    first = plane * (PLANE // LANES) + block * (BLOCK // LANES) + part * (TILE // LANES)
    return jnp.concatenate(
        [
            jnp.broadcast_to(potential[pl.ds(first + k, 1), :], (n.panel, LANES))
            for k in range(TILE // LANES)
        ],
        axis=1,
    )


def local_lap(n, planes, plane, sums, block, part):
    row = aligned(block * n.stride + plane * n.panel, 8)
    return (
        3.0 * stencil_weights[0] * planes[plane]
        + stencil_weights[1] * sums[pl.ds(row, n.panel), part * TILE : (part + 1) * TILE]
        + z_sum(planes, plane, 0)
    )


def table_kernel(n, field, atom_ref, cell_ref, value_ref, table, partial, packed, place):
    def entry_row(ref):
        return jnp.concatenate([ref[k : k + 1, :] for k in range(n.entries // LANES)], axis=1)

    cell = entry_row(cell_ref)
    slot = entry_row(atom_ref) - (lax.axis_index("grid") - 1) * ATOM_DEV
    plane, inside = cell // PLANE, cell % PLANE
    row_at = ((inside // BLOCK) * n.depth + plane) * SLOTS + slot
    lane_at = inside % BLOCK
    lane = lax.broadcasted_iota(jnp.int32, (BLOCK, n.entries), 0)
    place[...] = jnp.where(lane == lane_at, entry_row(value_ref), 0.0).astype(jnp.bfloat16)
    chunk = 4 * n.atoms

    def build(at, carry):
        first = aligned(at * chunk, 16)
        row = lax.broadcasted_iota(jnp.int32, (chunk, n.entries), 0) + first
        hit = jnp.where(row == row_at, 1.0, 0.0).astype(jnp.bfloat16)
        table[pl.ds(first, chunk), :] = lax.dot_general(
            hit, place[...], (((1,), (1,)), ((), ())), preferred_element_type=jnp.float32
        ).astype(jnp.bfloat16)
        return carry

    lax.fori_loop(0, n.blocks * n.atoms // chunk, build, 0)
    pack_planes(n, field, (packed,))
    atom_partial(n, (packed,), table, partial)


def first_local_kernel(n, field, packed, potential, taps, out, sums):
    apply_taps(n, (packed,), taps, sums)

    def one_tile(half_block, part):
        for block in (half_block, half_block + n.half_blocks):
            starts = [
                aligned(plane * PLANE + block * BLOCK + part * TILE, LANES)
                for plane in range(n.depth)
            ]
            planes = [field[:, pl.ds(start, TILE)].astype(jnp.float32) for start in starts]
            for plane in range(n.depth):
                lap = local_lap(n, planes, plane, sums, block, part)
                level = level_of(n, potential, plane, block, part)
                out[:, pl.ds(starts[plane], TILE)] = (
                    -0.5 * lap + (level - cheb_center) * planes[plane]
                ) * (1.0 / cheb_half)

    tile_loop(n, one_tile)


def first_halo_kernel(n, local, inner, outer, table, strength, *refs):
    *tables, out, sent_first, sent_second = refs
    wide = near_sums(n, tables, strength)
    rows = jnp.where(
        block_diagonal(n.depth, n.panel, SLOTS), jnp.concatenate([wide] * n.depth, axis=0), 0.0
    )
    rows = jnp.concatenate(split(rows), axis=0)

    def one(low, high, half_block, carry):
        blocks = (half_block, half_block + n.half_blocks)
        spreads = [
            spread_of(n, rows, table[pl.ds(aligned(b * n.atoms, 16), n.atoms), :]) for b in blocks
        ]
        for part in range(BLOCK // TILE):
            cut = slice(part * TILE, (part + 1) * TILE)
            values = [[], []]
            for side, block in enumerate(blocks):
                starts = [
                    aligned(plane * PLANE + block * BLOCK + part * TILE, LANES)
                    for plane in range(n.depth)
                ]
                below = [low[:, pl.ds(start, TILE)].astype(jnp.float32) for start in starts]
                above = [high[:, pl.ds(start, TILE)].astype(jnp.float32) for start in starts]
                for plane in range(n.depth):
                    lap = z_sum(below, plane, -n.depth) + z_sum(above, plane, n.depth)
                    near = spreads[side][plane * n.panel : (plane + 1) * n.panel, cut]
                    cells = pl.ds(starts[plane], TILE)
                    value = local[:, cells] + (near - 0.5 * lap) * (1.0 / cheb_half)
                    out[:, cells] = value
                    values[side].append(value)
            for plane in range(n.depth):
                start = aligned(plane * n.half_plane + half_block * BLOCK + part * TILE, LANES)
                first, second = halves_of(n, (values[0][plane], values[1][plane]))
                sent_first[:, pl.ds(start, TILE)] = first.astype(jnp.bfloat16)
                sent_second[:, pl.ds(start, TILE)] = second.astype(jnp.bfloat16)
        return carry

    by_side(
        inner,
        outer,
        lambda low, high: lax.fori_loop(
            0, n.half_blocks, functools.partial(one, low, high), None
        ),
    )


def second_sums_kernel(n, field, table, partial, packed, rest):
    pack_planes(n, field, (packed, rest))
    atom_partial(n, (packed, rest), table, partial)


def second_local_kernel(
    n, field, packed, rest, initial, potential, taps, out_first, out_second, sums
):
    apply_taps(n, (packed, rest), taps, sums)

    def one_tile(half_block, part):
        values = [[], []]
        for side, block in enumerate((half_block, half_block + n.half_blocks)):
            starts = [
                aligned(plane * PLANE + block * BLOCK + part * TILE, LANES)
                for plane in range(n.depth)
            ]
            planes = [field[:, pl.ds(start, TILE)] for start in starts]
            for plane in range(n.depth):
                lap = local_lap(n, planes, plane, sums, block, part)
                level = level_of(n, potential, plane, block, part)
                start = initial[:, pl.ds(starts[plane], TILE)].astype(jnp.float32)
                values[side].append(
                    (-0.5 * lap + (level - cheb_center) * planes[plane]) * (2.0 / cheb_half)
                    - start
                )
        for plane in range(n.depth):
            start = aligned(plane * n.half_plane + half_block * BLOCK + part * TILE, LANES)
            first, second = halves_of(n, (values[0][plane], values[1][plane]))
            out_first[:, pl.ds(start, TILE)] = first
            out_second[:, pl.ds(start, TILE)] = second

    tile_loop(n, one_tile)


def second_halo_kernel(n, chunk, local, inner, outer, table, strength, *refs):
    *tables, out = refs
    wide = near_sums(n, tables, strength)[chunk * n.half : (chunk + 1) * n.half, :]
    rows = jnp.concatenate([wide] * (2 * n.depth), axis=0)
    rows = jnp.where(block_diagonal(n.depth, n.panel, SLOTS), rows, 0.0)
    side = lax.broadcasted_iota(jnp.int32, rows.shape, 0) // n.half % 2
    rows = [jnp.concatenate(split(jnp.where(side == at, rows, 0.0)), axis=0) for at in (0, 1)]

    def one(low, high, half_block, carry):
        spread = None
        for at, block in enumerate((half_block, half_block + n.half_blocks)):
            weights = table[pl.ds(aligned(block * n.atoms, 16), n.atoms), :]
            term = spread_of(n, rows[at], weights)
            spread = term if spread is None else spread + term
        for part in range(BLOCK // TILE):
            cut = slice(part * TILE, (part + 1) * TILE)
            starts = [
                aligned(plane * n.half_plane + half_block * BLOCK + part * TILE, LANES)
                for plane in range(n.depth)
            ]
            below = [low[:, pl.ds(start, TILE)].astype(jnp.float32) for start in starts]
            above = [high[:, pl.ds(start, TILE)].astype(jnp.float32) for start in starts]
            for plane in range(n.depth):
                lap = z_sum(below, plane, -n.depth) + z_sum(above, plane, n.depth)
                near = spread[plane * n.panel : (plane + 1) * n.panel, cut]
                cells = pl.ds(starts[plane], TILE)
                value = local[:, cells] + (near - 0.5 * lap) * (2.0 / cheb_half)
                out[:, cells] = value.astype(jnp.bfloat16)
        return carry

    by_side(
        inner,
        outer,
        lambda low, high: lax.fori_loop(
            0, n.half_blocks, functools.partial(one, low, high), None
        ),
    )


def rotate_kernel(n, columns, rotation, *refs):
    *panels, filtered, rotated = refs
    for block in range(n.half_blocks):
        cut = slice(block * BLOCK, (block + 1) * BLOCK)
        parts = [panel[:, cut].astype(jnp.float32) for panel in panels]
        stack = jnp.concatenate(parts, axis=0).astype(jnp.bfloat16)
        both = jnp.dot(rotation[...], stack, preferred_element_type=jnp.float32)
        total = both[0 : 2 * columns, :] + both[2 * columns : 4 * columns, :]
        for side in range(2):
            first = side * n.half_plane + block * BLOCK
            rows = slice(side * n.half, (side + 1) * n.half)
            filtered[:, first : first + BLOCK] = jnp.concatenate(
                [parts[0][rows, :], parts[1][rows, :]], axis=0
            ).astype(jnp.bfloat16)
            rotated[:, first : first + BLOCK] = total[
                side * columns : (side + 1) * columns, :
            ].astype(jnp.bfloat16)


def call(kernel, out_shape, scratch, flops, *operands):
    bytes_accessed = sum(int(np.prod(o.shape)) * o.dtype.itemsize for o in operands)
    return pl.pallas_call(
        kernel,
        out_shape=out_shape,
        in_specs=[pl.BlockSpec(memory_space=pltpu.VMEM)] * len(operands),
        out_specs=jax.tree.map(lambda _: pl.BlockSpec(memory_space=pltpu.VMEM), out_shape),
        scratch_shapes=scratch,
        compiler_params=pltpu.CompilerParams(vmem_limit_bytes=VMEM_LIMIT),
        cost_estimate=pl.CostEstimate(
            flops=flops, bytes_accessed=bytes_accessed, transcendentals=0
        ),
    )(*operands)


def swapped(block, partner):
    count = lax.axis_size("grid")
    pairs = [(i, partner(i)) for i in range(count) if 0 <= partner(i) < count]
    return lax.ppermute(block, "grid", pairs)


def core_partner(i):
    return i ^ 1


def outer_partner(i):
    return i + 1 if i % 2 else i - 1


def exchange_sums(partial):
    partner = swapped(partial, core_partner)
    both = jnp.concatenate([partial, partner], axis=0)
    far = swapped(both, outer_partner)
    return partial, partner, far, swapped(far, core_partner)


def body(
    orbitals,
    potential,
    projector_atom,
    projector_cell,
    projector_value,
    atom_strength,
    ritz_rotation,
    panel_owner,
):
    n = Sizes(orbitals.shape[0], orbitals.shape[1], projector_atom.shape[0])
    taps = jnp.asarray(plane_taps())
    level = potential.reshape(n.cells // LANES, LANES)
    lists = [
        entry.reshape(n.entries // LANES, LANES)
        for entry in (projector_atom, projector_cell, projector_value)
    ]
    strength = atom_strength[None, :]

    bf16, f32 = jnp.bfloat16, jnp.float32
    shape = jax.ShapeDtypeStruct
    field = shape((n.panel, n.cells), f32)
    chunk_field = shape((n.panel, n.cells // 2), f32)
    chunk_narrow = shape((n.panel, n.cells // 2), bf16)
    sums = shape((n.panel, LANES), f32)
    packed_shape = shape(((n.blocks + 2) * n.stride, BLOCK), bf16)
    tap_sums = pltpu.VMEM((n.blocks * n.stride, BLOCK), f32)

    inner = swapped(orbitals, core_partner)
    outer = swapped(orbitals, outer_partner)
    table, partial, packed = call(
        functools.partial(table_kernel, n),
        (shape((n.blocks * n.atoms, BLOCK), bf16), sums, packed_shape),
        [pltpu.VMEM((BLOCK, n.entries), bf16)],
        4 * 10**9,
        orbitals, *lists,
    )
    near = exchange_sums(partial)
    local = call(
        functools.partial(first_local_kernel, n), field, [tap_sums], 2 * 10**9,
        orbitals, packed, level, taps,
    )
    step_field, sent_first, sent_second = call(
        functools.partial(first_halo_kernel, n),
        (field, chunk_narrow, chunk_narrow), [], 10**9,
        local, inner, outer, table, strength, *near,
    )
    outers = [swapped(sent_first, outer_partner)]
    inners = [swapped(sent_first, core_partner)]
    partial, packed, rest = call(
        functools.partial(second_sums_kernel, n),
        (sums, packed_shape, packed_shape), [], 10**9,
        step_field, table,
    )
    near = exchange_sums(partial)
    sent_second, _ = lax.optimization_barrier((sent_second, near[2]))
    outers.append(swapped(sent_second, outer_partner))
    inners.append(swapped(sent_second, core_partner))
    locals_ = call(
        functools.partial(second_local_kernel, n),
        (chunk_field, chunk_field), [tap_sums], 3 * 10**9,
        step_field, packed, rest, orbitals, level, taps,
    )

    orb_count = lax.axis_size("orb")
    orb_index = lax.axis_index("orb")
    shares = []
    for chunk in range(2):
        share = call(
            functools.partial(second_halo_kernel, n, chunk),
            chunk_narrow, [], 10**8,
            locals_[chunk], inners[chunk], outers[chunk], table, strength, *near,
        )
        shares.append(
            [share]
            + [
                lax.ppermute(share, "orb", [(i, (i + k) % orb_count) for i in range(orb_count)])
                for k in range(1, orb_count)
            ]
        )
    panels = [shares[chunk][k] for k in range(orb_count) for chunk in range(2)]
    source = (orb_index - jnp.arange(orb_count)) % orb_count
    chosen = (panel_owner[None, :] == source[:, None]).astype(f32)
    rotation = jnp.sum(
        chosen[:, :, None, None] * ritz_rotation.astype(f32)[None], axis=1
    )
    columns = ritz_rotation.shape[2]
    rotation = rotation.reshape(orb_count * 2, 1, n.half, columns)
    sides = jnp.eye(2, dtype=f32)
    rotation = (
        sides[:, None, None, :, None] * rotation.transpose(3, 0, 1, 2)[None]
    ).reshape(2 * columns, orb_count * 2 * n.panel)
    rotation = jnp.concatenate(split(rotation), axis=0)
    filtered, rotated = pl.pallas_call(
        functools.partial(rotate_kernel, n, columns),
        grid=(n.depth,),
        out_shape=(shape((n.panel, n.cells), bf16), shape((columns, n.cells), bf16)),
        in_specs=[pl.BlockSpec(rotation.shape, lambda i: (0, 0))]
        + [pl.BlockSpec((n.panel, n.half_plane), lambda i: (0, i))] * len(panels),
        out_specs=(
            pl.BlockSpec((n.panel, PLANE), lambda i: (0, i)),
            pl.BlockSpec((columns, PLANE), lambda i: (0, i)),
        ),
        compiler_params=pltpu.CompilerParams(vmem_limit_bytes=VMEM_LIMIT),
    )(rotation, *panels)
    return (filtered, rotated)


def solution(mesh):
    in_specs = (
        P("orb", "grid"),
        P("grid"),
        P("grid"),
        P("grid"),
        P("grid"),
        P(),
        P(None, None, "orb"),
        P(),
    )
    out_specs = (P("orb", "grid"), P("orb", "grid"))
    return jax.shard_map(body, mesh=mesh, in_specs=in_specs, out_specs=out_specs, check_vma=False)
```

time: 100 us -> 80.4 us (0.80)
  the two profiles are of different devices: /device:TPU:6 before, /device:TPU:11 now
where the time goes in v2:
time: 80.4 us; the launch traced here: 79.2 us
  waiting for transfers between devices  30.1 us (37%)
  Pallas kernels  25 us (31%)
  starting transfers between devices  18.8 us (23%)
  local copies, waits for them, and re-layouts  4.11 us (5%)
  between operations  0.9 us (1%)
    pallas_call x7, Pallas kernels, call(): pl.pallas_call(kernel, out_shape=out_shape, in_specs=[pl.BlockSpec(memory...  21.6 us
    ppermute x12, waiting for transfers between devices, swapped(): return lax.ppermute(block, 'grid', pairs)  20.4 us
    ppermute x12, starting transfers between devices, swapped(): return lax.ppermute(block, 'grid', pairs)  18.1 us
    ppermute x2, waiting for transfers between devices, body(): lax.ppermute(share, 'orb', [(i, (i + k) % orb_count) for i in range(orb_c...  9.76 us
    unnamed x26, local copies, waits for them, and re-layouts  3.95 us
    pallas_call x1, Pallas kernels, body(): pl.pallas_call(functools.partial(rotate_kernel, n, columns), grid=(n.dept...  3.37 us
  transfers between devices with their start and end apart: 14, of which 7 were waited for; matrix products, arithmetic and copies ran while one was open for 1% of the time, Pallas kernels for 20%

profile of v2, /device:TPU:11, one launch (start us, length us, event | category | flops | bytes accessed | tf_op | source)
XLA Modules:
  0.0 79.2 jit_solution(1609898084595966659)
XLA Ops:
  0.6 0.7 collective-permute-start
  1.4 3.1 %collective-permute-start.1 = (bf16[8,55296]{1,0:T(8,128)(2,1)}, bf16[8,55296]{1,0:T(8,128)(2,1)}, u32[]{:S(2)}, u32[]{:S(2)}) collective-permute-start(bf16[8,55296]{1,0:T(8,128)(2,1)} %initial.1), channel_id=1, source_target_pairs={{2,4},{4,2},{6,8},{8,6},{10,12},{12,10},{14,16},{16,14},{18,20},{2... | collective-permute-start | bytes 2654216 | tf_op jit(solution)/shard_map/ppermute | solution.py:441
  4.4 0.0 copy-start.2
  4.4 1.2 %copy-done.2 = bf16[8,55296]{1,0:T(8,128)(2,1)S(1)} copy-done((bf16[8,55296]{1,0:T(8,128)(2,1)S(1)}, bf16[8,55296]{1,0:T(8,128)(2,1)}, u32[]{:S(2)}) %copy-start.2) | copy-done | bytes 884760
  5.6 0.7 copy-done.8
  6.3 0.7 copy-done.9
  7.0 0.7 copy-done.10
  7.7 4.8 %shard_map.104 = (bf16[1152,768]{1,0:T(8,128)(2,1)S(1)}, f32[8,128]{1,0:T(8,128)S(1)}, bf16[672,768]{1,0:T(8,128)(2,1)S(1)}) custom-call(bf16[8,55296]{1,0:T(8,128)(2,1)S(1)} %copy-done.2, s32[12,128]{1,0:T(8,128)S(1)} %bitcast.17, s32[12,128]{1,0:T(8,128)S(1)} %bitcast.18, f32[12,128]{1,0:T(8,128)S(1)} %bitcast.19), custom_call_target="tpu_custom_call" | custom-call | flops 4000000000 | bytes 903168 | tf_op jit(solution)/shard_map/pallas_call | solution.py:425
  12.5 0.4 collective-permute-start.2
  12.9 0.8 %collective-permute-done.2.refs_1_ = f32[8,128]{1,0:T(8,128)S(1)} collective-permute-done((f32[8,128]{1,0:T(8,128)S(1)}, f32[8,128]{1,0:T(8,128)S(1)}, u32[]{:S(2)}, u32[]{:S(2)}) %collective-permute-start.2) | collective-permute-done | bytes 4128 | tf_op jit(solution)/shard_map/ppermute | solution.py:441
  13.7 3.2 %collective-permute-start.3 = (f32[16,128]{1,0:T(8,128)S(1)}, f32[16,128]{1,0:T(8,128)S(1)}, u32[]{:S(2)}, u32[]{:S(2)}) collective-permute-start(f32[16,128]{1,0:T(8,128)S(1)} %pad_maximum_fusion.1), channel_id=1, source_target_pairs={{2,4},{4,2},{6,8},{8,6},{10,12},{12,10},{14,16},{16,14},{18,20},{2... | collective-permute-start | bytes 24584 | tf_op jit(solution)/shard_map/ppermute | solution.py:441
  16.9 8.7 %collective-permute-done.3.refs_2_ = f32[16,128]{1,0:T(8,128)S(1)} collective-permute-done((f32[16,128]{1,0:T(8,128)S(1)}, f32[16,128]{1,0:T(8,128)S(1)}, u32[]{:S(2)}, u32[]{:S(2)}) %collective-permute-start.3) | collective-permute-done | bytes 8224 | tf_op jit(solution)/shard_map/ppermute | solution.py:441
  25.6 0.0 collective-permute-start.4
  25.6 3.0 %shard_map.105.local = f32[8,55296]{1,0:T(8,128)S(1)} custom-call(bf16[8,55296]{1,0:T(8,128)(2,1)S(1)} %copy-done.2, bf16[672,768]{1,0:T(8,128)(2,1)S(1)} %get-tuple-element.14.packed, f32[432,128]{1,0:T(8,128)S(1)} %bitcast.12, bf16[3,768,768]{2,1,0:T(8,128)(2,1)S(1)} %copy-done), custom_call_target="tpu_custom_call" | custom-call | flops 2000000000 | bytes 5677056 | tf_op jit(solution)/shard_map/pallas_call | solution.py:425
  28.7 0.0 collective-permute-done.inner
  28.7 0.0 collective-permute-done.1.outer
  28.7 0.0 copy-start.6
  28.7 0.6 copy-done.6
  29.4 3.7 %shard_map.106 = (f32[8,55296]{1,0:T(8,128)S(1)}, bf16[8,27648]{1,0:T(8,128)(2,1)S(1)}, bf16[8,27648]{1,0:T(8,128)(2,1)S(1)}) custom-call(f32[8,55296]{1,0:T(8,128)S(1)} %shard_map.105.local, bf16[8,55296]{1,0:T(8,128)(2,1)} %collective-permute-done.inner, bf16[8,55296]{1,0:T(8,128)(2,1)} %collective-permute-done.1.outer, ...), custom_call_target="tpu_custom_call" | custom-call | flops 1000000000 | bytes 5333248 | tf_op jit(solution)/shard_map/pallas_call | solution.py:425
  33.1 0.0 copy-start.1
  33.1 0.0 copy-start.5
  33.1 1.7 %shard_map.107 = (f32[8,128]{1,0:T(8,128)S(1)}, bf16[672,768]{1,0:T(8,128)(2,1)S(1)}, bf16[672,768]{1,0:T(8,128)(2,1)S(1)}) custom-call(f32[8,55296]{1,0:T(8,128)S(1)} %get-tuple-element.17.field, bf16[1152,768]{1,0:T(8,128)(2,1)S(1)} %get-tuple-element.15.table), custom_call_target="tpu_custom_call" | custom-call | flops 1000000000 | bytes 3538944 | tf_op jit(solution)/shard_map/pallas_call | solution.py:425
  34.9 0.6 collective-permute-start.7
  35.4 0.8 %collective-permute-done.7.refs_1_ = f32[8,128]{1,0:T(8,128)S(1)} collective-permute-done((f32[8,128]{1,0:T(8,128)S(1)}, f32[8,128]{1,0:T(8,128)S(1)}, u32[]{:S(2)}, u32[]{:S(2)}) %collective-permute-start.7) | collective-permute-done | bytes 4128 | tf_op jit(solution)/shard_map/ppermute | solution.py:441
  36.2 3.1 %collective-permute-start.8 = (f32[16,128]{1,0:T(8,128)S(1)}, f32[16,128]{1,0:T(8,128)S(1)}, u32[]{:S(2)}, u32[]{:S(2)}) collective-permute-start(f32[16,128]{1,0:T(8,128)S(1)} %pad_maximum_fusion.2), channel_id=1, source_target_pairs={{2,4},{4,2},{6,8},{8,6},{10,12},{12,10},{14,16},{16,14},{18,20},{2... | collective-permute-start | bytes 24584 | tf_op jit(solution)/shard_map/ppermute | solution.py:441
  39.3 0.1 compare_convert_fusion
  39.4 0.2 collective-permute-start.5
  39.6 3.6 %collective-permute-start.6 = (bf16[8,27648]{1,0:T(8,128)(2,1)S(1)}, bf16[8,27648]{1,0:T(8,128)(2,1)S(1)}, u32[]{:S(2)}, u32[]{:S(2)}) collective-permute-start(bf16[8,27648]{1,0:T(8,128)(2,1)S(1)} %get-tuple-element.21), channel_id=1, source_target_pairs={{2,4},{4,2},{6,8},{8,6},{10,12},{12,10},{14,16},{16,14},{18,20},{2... | collective-permute-start | bytes 1327112 | tf_op jit(solution)/shard_map/ppermute | solution.py:441
  43.2 0.0 collective-permute-done.8.refs_2_
  43.2 0.1 collective-permute-start.10
  43.3 3.2 %collective-permute-start.11 = (bf16[8,27648]{1,0:T(8,128)(2,1)S(1)}, bf16[8,27648]{1,0:T(8,128)(2,1)S(1)}, u32[]{:S(2)}, u32[]{:S(2)}) collective-permute-start(bf16[8,27648]{1,0:T(8,128)(2,1)S(1)} %get-tuple-element.25), channel_id=1, source_target_pairs={{2,4},{4,2},{6,8},{8,6},{10,12},{12,10},{14,16},{16,14},{18,20},{2... | collective-permute-start | bytes 1327112 | tf_op jit(solution)/shard_map/ppermute | solution.py:441
  46.6 0.1 multiply_reduce_fusion
  46.7 0.0 collective-permute-start.9
  46.7 0.0 copy-start.7
  46.7 4.9 %shard_map.108 = (f32[8,27648]{1,0:T(8,128)S(1)}, f32[8,27648]{1,0:T(8,128)S(1)}) custom-call(f32[8,55296]{1,0:T(8,128)S(1)} %get-tuple-element.17.field, bf16[672,768]{1,0:T(8,128)(2,1)S(1)} %get-tuple-element.18.packed, bf16[672,768]{1,0:T(8,128)(2,1)S(1)} %get-tuple-element.19.rest, bf16[8,55296]{1,0:T(8,128)(2,1)S(1)} %copy-done.3, ...), custom_call_target="tpu_custom_call" | custom-call | flops 3000000000 | bytes 8478720 | tf_op jit(solution)/shard_map/pallas_call | solution.py:425
  51.7 0.0 collective-permute-done.5.inner
  51.7 7.3 %collective-permute-done.6.outer = bf16[8,27648]{1,0:T(8,128)(2,1)S(1)} collective-permute-done((bf16[8,27648]{1,0:T(8,128)(2,1)S(1)}, bf16[8,27648]{1,0:T(8,128)(2,1)S(1)}, u32[]{:S(2)}, u32[]{:S(2)}) %collective-permute-start.6) | collective-permute-done | bytes 442400 | tf_op jit(solution)/shard_map/ppermute | solution.py:441
  59.0 1.7 %shard_map.109.refs_0_ = bf16[8,27648]{1,0:T(8,128)(2,1)S(1)} custom-call(f32[8,27648]{1,0:T(8,128)S(1)} %get-tuple-element.20.local, bf16[8,27648]{1,0:T(8,128)(2,1)S(1)} %collective-permute-done.5.inner, bf16[8,27648]{1,0:T(8,128)(2,1)S(1)} %collective-permute-done.6.outer, bf16[1152,768]{1,0:T(8,128)(2,1)S(1)} %get-tuple-element.15.table, ...), custom_call_target="tpu_custom_call" | custom-call | flops 100000000 | bytes 3563776 | tf_op jit(solution)/shard_map/pallas_call | solution.py:425
  60.7 0.3 collective-permute-start.12
  61.0 2.7 %collective-permute-done.11.outer = bf16[8,27648]{1,0:T(8,128)(2,1)S(1)} collective-permute-done((bf16[8,27648]{1,0:T(8,128)(2,1)S(1)}, bf16[8,27648]{1,0:T(8,128)(2,1)S(1)}, u32[]{:S(2)}, u32[]{:S(2)}) %collective-permute-start.11) | collective-permute-done | bytes 442400 | tf_op jit(solution)/shard_map/ppermute | solution.py:441
  63.7 1.7 %shard_map.110.refs_1_ = bf16[8,27648]{1,0:T(8,128)(2,1)S(1)} custom-call(f32[8,27648]{1,0:T(8,128)S(1)} %get-tuple-element.23.local, bf16[8,27648]{1,0:T(8,128)(2,1)S(1)} %collective-permute-done.10.inner, bf16[8,27648]{1,0:T(8,128)(2,1)S(1)} %collective-permute-done.11.outer, bf16[1152,768]{1,0:T(8,128)(2,1)S(1)} %get-tuple-element.15.table, ...), custom_call_target="tpu_custom_call" | custom-call | flops 100000000 | bytes 3563776 | tf_op jit(solution)/shard_map/pallas_call | solution.py:425
  65.5 0.3 collective-permute-start.13
  65.8 0.1 broadcast_multiply_fusion
  65.9 0.1 mul.39
  66.0 0.1 copy.13
  66.0 5.0 %collective-permute-done.12.refs_2_ = bf16[8,27648]{1,0:T(8,128)(2,1)S(1)} collective-permute-done((bf16[8,27648]{1,0:T(8,128)(2,1)S(1)}, bf16[8,27648]{1,0:T(8,128)(2,1)S(1)}, u32[]{:S(2)}, u32[]{:S(2)}) %collective-permute-start.12) | collective-permute-done | bytes 442400 | tf_op jit(solution)/shard_map/ppermute | solution.py:535
  71.1 4.7 %collective-permute-done.13.refs_3_ = bf16[8,27648]{1,0:T(8,128)(2,1)S(1)} collective-permute-done((bf16[8,27648]{1,0:T(8,128)(2,1)S(1)}, bf16[8,27648]{1,0:T(8,128)(2,1)S(1)}, u32[]{:S(2)}, u32[]{:S(2)}) %collective-permute-start.13) | collective-permute-done | bytes 442400 | tf_op jit(solution)/shard_map/ppermute | solution.py:535
  75.8 3.4 %shard_map.111 = (bf16[8,55296]{1,0:T(8,128)(2,1)}, bf16[16,55296]{1,0:T(8,128)(2,1)}) custom-call(bf16[64,32]{1,0:T(8,128)(2,1)S(1)} %pad_maximum_fusion.rotation, bf16[8,27648]{1,0:T(8,128)(2,1)S(1)} %shard_map.109.refs_0_, bf16[8,27648]{1,0:T(8,128)(2,1)S(1)} %shard_map.110.refs_1_, bf16[8,27648]{1,0:T(8,128)(2,1)S(1)} %collective-permute-done.12.refs_2_, ...), custom_call_target="tpu_custom_call" | custom-call | tf_op jit(solution)/shard_map/pallas_call | solution.py:552
  (26 shorter events, 0.1 us)
Async XLA Ops:
  0.6 28.1 %collective-permute-start = (bf16[8,55296]{1,0:T(8,128)(2,1)}, bf16[8,55296]{1,0:T(8,128)(2,1)}, u32[]{:S(2)}, u32[]{:S(2)}) collective-permute-start(bf16[8,55296]{1,0:T(8,128)(2,1)} %initial.1), channel_id=1, source_target_pairs={{0,2},{2,0},{4,6},{6,4},{8,10},{10,8},{12,14},{14,12},{16,18},{18,... | collective-permute-start | bytes 2654216 | tf_op jit(solution)/shard_map/ppermute | solution.py:441
  1.4 27.3 %collective-permute-start.1 = (bf16[8,55296]{1,0:T(8,128)(2,1)}, bf16[8,55296]{1,0:T(8,128)(2,1)}, u32[]{:S(2)}, u32[]{:S(2)}) collective-permute-start(bf16[8,55296]{1,0:T(8,128)(2,1)} %initial.1), channel_id=1, source_target_pairs={{2,4},{4,2},{6,8},{8,6},{10,12},{12,10},{14,16},{16,14},{18,20},{2... | collective-permute-start | bytes 2654216 | tf_op jit(solution)/shard_map/ppermute | solution.py:441
  4.4 1.2 %copy-start.2 = (bf16[8,55296]{1,0:T(8,128)(2,1)S(1)}, bf16[8,55296]{1,0:T(8,128)(2,1)}, u32[]{:S(2)}) copy-start(bf16[8,55296]{1,0:T(8,128)(2,1)} %initial.1) | copy-start | bytes 2654212
  5.6 0.7 copy-start.8
  6.3 0.7 copy-start.9
  7.0 0.7 copy-start.10
  7.7 17.9 %copy-start = (bf16[3,768,768]{2,1,0:T(8,128)(2,1)S(1)}, bf16[3,768,768]{2,1,0:T(8,128)(2,1)}, u32[]{:S(2)}) copy-start(bf16[3,768,768]{2,1,0:T(8,128)(2,1)} %constant.23.clone.taps) | copy-start | bytes 10616836
  7.7 17.9 %copy-start.4 = (f32[55296]{0:T(1024)S(1)}, f32[55296]{0:T(1024)}, u32[]{:S(2)}) copy-start(f32[55296]{0:T(1024)} %param.10) | copy-start | bytes 663556
  12.5 1.3 %collective-permute-start.2 = (f32[8,128]{1,0:T(8,128)S(1)}, f32[8,128]{1,0:T(8,128)S(1)}, u32[]{:S(2)}, u32[]{:S(2)}) collective-permute-start(f32[8,128]{1,0:T(8,128)S(1)} %get-tuple-element.16.refs_0_), channel_id=1, source_target_pairs={{0,2},{2,0},{4,6},{6,4},{8,10},{10,8},{12,14},{14,12},{16,18},{18,... | collective-permute-start | bytes 12296 | tf_op jit(solution)/shard_map/ppermute | solution.py:441
  13.7 11.9 %collective-permute-start.3 = (f32[16,128]{1,0:T(8,128)S(1)}, f32[16,128]{1,0:T(8,128)S(1)}, u32[]{:S(2)}, u32[]{:S(2)}) collective-permute-start(f32[16,128]{1,0:T(8,128)S(1)} %pad_maximum_fusion.1), channel_id=1, source_target_pairs={{2,4},{4,2},{6,8},{8,6},{10,12},{12,10},{14,16},{16,14},{18,20},{2... | collective-permute-start | bytes 24584 | tf_op jit(solution)/shard_map/ppermute | solution.py:441
  25.6 3.1 %collective-permute-start.4 = (f32[16,128]{1,0:T(8,128)S(1)}, f32[16,128]{1,0:T(8,128)}, u32[]{:S(2)}, u32[]{:S(2)}) collective-permute-start(f32[16,128]{1,0:T(8,128)S(1)} %collective-permute-done.3.refs_2_), channel_id=1, source_target_pairs={{0,2},{2,0},{4,6},{6,4},{8,10},{10,8},{12,14},{14,12},{16,18},{18,... | collective-permute-start | bytes 24584 | tf_op jit(solution)/shard_map/ppermute | solution.py:441
  28.7 0.7 copy-start.6
  29.4 9.9 %copy-start.12 = (s32[4]{0:T(128)S(1)}, s32[4]{0:T(128)}, u32[]{:S(2)}) copy-start(s32[4]{0:T(128)} %param.16) | copy-start | bytes 52
  29.4 17.2 %copy-start.11 = (bf16[4,8,16]{2,1,0:T(8,128)(2,1)S(1)}, bf16[4,8,16]{2,1,0:T(8,128)(2,1)}, u32[]{:S(2)}) copy-start(bf16[4,8,16]{2,1,0:T(8,128)(2,1)} %param.15) | copy-start | bytes 3076
  29.4 17.3 %copy-start.3 = (bf16[8,55296]{1,0:T(8,128)(2,1)S(1)}, bf16[8,55296]{1,0:T(8,128)(2,1)}, u32[]{:S(2)}) copy-start(bf16[8,55296]{1,0:T(8,128)(2,1)} %initial.1) | copy-start | bytes 2654212
  33.1 13.6 %copy-start.1 = (bf16[3,768,768]{2,1,0:T(8,128)(2,1)S(1)}, bf16[3,768,768]{2,1,0:T(8,128)(2,1)}, u32[]{:S(2)}) copy-start(bf16[3,768,768]{2,1,0:T(8,128)(2,1)} %constant.23.clone.taps) | copy-start | bytes 10616836
  33.1 13.6 %copy-start.5 = (f32[55296]{0:T(1024)S(1)}, f32[55296]{0:T(1024)}, u32[]{:S(2)}) copy-start(f32[55296]{0:T(1024)} %param.10) | copy-start | bytes 663556
  34.9 1.4 %collective-permute-start.7 = (f32[8,128]{1,0:T(8,128)S(1)}, f32[8,128]{1,0:T(8,128)S(1)}, u32[]{:S(2)}, u32[]{:S(2)}) collective-permute-start(f32[8,128]{1,0:T(8,128)S(1)} %get-tuple-element.22.refs_0_), channel_id=1, source_target_pairs={{0,2},{2,0},{4,6},{6,4},{8,10},{10,8},{12,14},{14,12},{16,18},{18,... | collective-permute-start | bytes 12296 | tf_op jit(solution)/shard_map/ppermute | solution.py:441
  36.2 7.0 %collective-permute-start.8 = (f32[16,128]{1,0:T(8,128)S(1)}, f32[16,128]{1,0:T(8,128)S(1)}, u32[]{:S(2)}, u32[]{:S(2)}) collective-permute-start(f32[16,128]{1,0:T(8,128)S(1)} %pad_maximum_fusion.2), channel_id=1, source_target_pairs={{2,4},{4,2},{6,8},{8,6},{10,12},{12,10},{14,16},{16,14},{18,20},{2... | collective-permute-start | bytes 24584 | tf_op jit(solution)/shard_map/ppermute | solution.py:441
  39.4 12.3 %collective-permute-start.5 = (bf16[8,27648]{1,0:T(8,128)(2,1)S(1)}, bf16[8,27648]{1,0:T(8,128)(2,1)S(1)}, u32[]{:S(2)}, u32[]{:S(2)}) collective-permute-start(bf16[8,27648]{1,0:T(8,128)(2,1)S(1)} %get-tuple-element.21), channel_id=1, source_target_pairs={{0,2},{2,0},{4,6},{6,4},{8,10},{10,8},{12,14},{14,12},{16,18},{18,... | collective-permute-start | bytes 1327112 | tf_op jit(solution)/shard_map/ppermute | solution.py:441
  39.6 19.4 %collective-permute-start.6 = (bf16[8,27648]{1,0:T(8,128)(2,1)S(1)}, bf16[8,27648]{1,0:T(8,128)(2,1)S(1)}, u32[]{:S(2)}, u32[]{:S(2)}) collective-permute-start(bf16[8,27648]{1,0:T(8,128)(2,1)S(1)} %get-tuple-element.21), channel_id=1, source_target_pairs={{2,4},{4,2},{6,8},{8,6},{10,12},{12,10},{14,16},{16,14},{18,20},{2... | collective-permute-start | bytes 1327112 | tf_op jit(solution)/shard_map/ppermute | solution.py:441
  43.2 17.8 %collective-permute-start.10 = (bf16[8,27648]{1,0:T(8,128)(2,1)S(1)}, bf16[8,27648]{1,0:T(8,128)(2,1)S(1)}, u32[]{:S(2)}, u32[]{:S(2)}) collective-permute-start(bf16[8,27648]{1,0:T(8,128)(2,1)S(1)} %get-tuple-element.25), channel_id=1, source_target_pairs={{0,2},{2,0},{4,6},{6,4},{8,10},{10,8},{12,14},{14,12},{16,18},{18,... | collective-permute-start | bytes 1327112 | tf_op jit(solution)/shard_map/ppermute | solution.py:441
  43.3 20.4 %collective-permute-start.11 = (bf16[8,27648]{1,0:T(8,128)(2,1)S(1)}, bf16[8,27648]{1,0:T(8,128)(2,1)S(1)}, u32[]{:S(2)}, u32[]{:S(2)}) collective-permute-start(bf16[8,27648]{1,0:T(8,128)(2,1)S(1)} %get-tuple-element.25), channel_id=1, source_target_pairs={{2,4},{4,2},{6,8},{8,6},{10,12},{12,10},{14,16},{16,14},{18,20},{2... | collective-permute-start | bytes 1327112 | tf_op jit(solution)/shard_map/ppermute | solution.py:441
  46.7 5.0 %collective-permute-start.9 = (f32[16,128]{1,0:T(8,128)S(1)}, f32[16,128]{1,0:T(8,128)S(1)}, u32[]{:S(2)}, u32[]{:S(2)}) collective-permute-start(f32[16,128]{1,0:T(8,128)S(1)} %collective-permute-done.8.refs_2_), channel_id=1, source_target_pairs={{0,2},{2,0},{4,6},{6,4},{8,10},{10,8},{12,14},{14,12},{16,18},{18,... | collective-permute-start | bytes 24584 | tf_op jit(solution)/shard_map/ppermute | solution.py:441
  46.7 12.3 %copy-start.7 = (f32[64]{0:T(128)S(1)}, f32[64]{0:T(128)}, u32[]{:S(2)}) copy-start(f32[64]{0:T(128)} %param.14) | copy-start | bytes 772
  60.7 10.3 %collective-permute-start.12 = (bf16[8,27648]{1,0:T(8,128)(2,1)S(1)}, bf16[8,27648]{1,0:T(8,128)(2,1)S(1)}, u32[]{:S(2)}, u32[]{:S(2)}) collective-permute-start(bf16[8,27648]{1,0:T(8,128)(2,1)S(1)} %shard_map.109.refs_0_), channel_id=1, source_target_pairs={{0,1},{1,0},{2,3},{3,2},{4,5},{5,4},{6,7},{7,6},{8,9},{9,8},{10,11... | collective-permute-start | bytes 1327112 | tf_op jit(solution)/shard_map/ppermute | solution.py:535
  65.5 10.3 %collective-permute-start.13 = (bf16[8,27648]{1,0:T(8,128)(2,1)S(1)}, bf16[8,27648]{1,0:T(8,128)(2,1)S(1)}, u32[]{:S(2)}, u32[]{:S(2)}) collective-permute-start(bf16[8,27648]{1,0:T(8,128)(2,1)S(1)} %shard_map.110.refs_1_), channel_id=1, source_target_pairs={{0,1},{1,0},{2,3},{3,2},{4,5},{5,4},{6,7},{7,6},{8,9},{9,8},{10,11... | collective-permute-start | bytes 1327112 | tf_op jit(solution)/shard_map/ppermute | solution.py:535

commit v3 on v2

v3 whole, which is shorter than its diff:
```python
import functools

import jax
import jax.numpy as jnp
import numpy as np
from jax import lax
from jax.experimental import pallas as pl
from jax.experimental.pallas import tpu as pltpu
from jax.sharding import PartitionSpec as P

NX = 96
NY = 96
REACH = 6
ATOM_DEV = 4
PLANE = NX * NY
BLOCK_ROWS = 8
BLOCK = BLOCK_ROWS * NX
SLOTS = 16
TILE = 256
LANES = 128
CHUNKS = ((0, 12),)
VMEM_LIMIT = 24 * 2**20

stencil_weights = (
    -5369.0 / 1800.0,
    12.0 / 7.0,
    -15.0 / 56.0,
    10.0 / 189.0,
    -1.0 / 112.0,
    2.0 / 1925.0,
    -1.0 / 16632.0,
)
cheb_center = 6.0
cheb_half = 6.0

TAPS = {
    0: ((0, 0, 3), (1, 0, 3), (2, 0, 1)),
    1: ((0, 1, 3), (1, 0, 3), (2, 0, 2)),
    2: ((0, 2, 3), (1, 0, 3), (2, 0, 3)),
}


def plane_taps():
    cell = np.arange(BLOCK)
    row, column = cell // NX, cell % NX
    out = np.zeros((3, BLOCK, BLOCK), np.float64)
    for block in range(3):
        source_row = row + (block - 1) * BLOCK_ROWS
        jump_row = np.abs(source_row[:, None] - row[None, :])
        jump_column = np.abs(column[:, None] - column[None, :])
        for distance in range(1, REACH + 1):
            hit = ((jump_row == distance) & (jump_column == 0)) | (
                (jump_row == 0) & (jump_column == distance)
            )
            out[block][hit] = stencil_weights[distance] / stencil_weights[1]
    return out.astype(jnp.bfloat16)


def z_sum(planes, target, first):
    total = None
    for at, values in enumerate(planes):
        distance = abs(first + at - target)
        if 1 <= distance <= REACH:
            term = stencil_weights[distance] * values
            total = term if total is None else total + term
    return total


def block_diagonal(depth, rows, columns):
    row = lax.broadcasted_iota(jnp.int32, (depth * rows, depth * columns), 0) // rows
    column = lax.broadcasted_iota(jnp.int32, (depth * rows, depth * columns), 1) // columns
    return row == column


def split(values):
    high = values.astype(jnp.bfloat16)
    return high, (values - high.astype(jnp.float32)).astype(jnp.bfloat16)


def aligned(index, multiple):
    return pl.multiple_of(index, multiple)


class Sizes:
    def __init__(self, panel, cells, entries):
        self.panel, self.cells, self.entries = panel, cells, entries
        self.depth = cells // PLANE
        self.blocks = PLANE // BLOCK
        self.stride = self.depth * panel
        self.atoms = self.depth * SLOTS

    def chunk_cells(self, chunk):
        low, high = CHUNKS[chunk]
        return self.depth * (high - low) * BLOCK

    def start(self, plane, block, part=0):
        return aligned(plane * PLANE + block * BLOCK + part * TILE, LANES)

    def chunk_start(self, chunk, plane, block, part=0):
        low, high = CHUNKS[chunk]
        at = plane * (high - low) * BLOCK + (block - low) * BLOCK + part * TILE
        return aligned(at, LANES)

    def each_block(self, chunk, one):
        def step(block, carry):
            one(block)
            return carry

        lax.fori_loop(*CHUNKS[chunk], step, None)


def pack_planes(n, source, targets):
    zero = jnp.zeros((n.stride, BLOCK), jnp.bfloat16)
    for target in targets:
        target[0 : n.stride, :] = zero
        target[(n.blocks + 1) * n.stride : (n.blocks + 2) * n.stride, :] = zero

    def one(block, carry):
        for pair in range(n.depth // 2):
            halves = [
                source[:, pl.ds(n.start(plane, block), BLOCK)].astype(jnp.float32)
                for plane in (2 * pair, 2 * pair + 1)
            ]
            parts = split(jnp.concatenate(halves, axis=0))
            row = aligned((block + 1) * n.stride + pair * 2 * n.panel, 16)
            for target, part in zip(targets, parts):
                target[pl.ds(row, 2 * n.panel), :] = part
        return carry

    lax.fori_loop(0, n.blocks, one, None)


def apply_taps(n, packs, taps, out):
    rows = n.blocks * n.stride
    for tile, parts in TAPS.items():
        total = None
        for packed in packs:
            for block, low, high in parts:
                term = jnp.dot(
                    packed[block * n.stride : block * n.stride + rows, low * TILE : high * TILE],
                    taps[block, low * TILE : high * TILE, tile * TILE : (tile + 1) * TILE],
                    preferred_element_type=jnp.float32,
                )
                total = term if total is None else total + term
        out[:, tile * TILE : (tile + 1) * TILE] = total


def atom_partial(n, packs, table, out):
    total = None
    for block in range(n.blocks):
        weights = table[block * n.atoms : (block + 1) * n.atoms, :]
        for packed in packs:
            rows = packed[(block + 1) * n.stride : (block + 2) * n.stride, :]
            term = lax.dot_general(
                rows, weights, (((1,), (1,)), ((), ())), preferred_element_type=jnp.float32
            )
            total = term if total is None else total + term
    total = jnp.where(block_diagonal(n.depth, n.panel, SLOTS), total, 0.0)
    folded = total[0 : n.panel, :]
    for plane in range(1, n.depth):
        folded = folded + total[plane * n.panel : (plane + 1) * n.panel, :]
    slot = lax.broadcasted_iota(jnp.int32, (n.atoms, LANES), 0) % SLOTS
    lane = lax.broadcasted_iota(jnp.int32, (n.atoms, LANES), 1)
    out[...] = jnp.dot(
        folded,
        (slot == lane).astype(jnp.float32),
        precision=lax.Precision.HIGHEST,
        preferred_element_type=jnp.float32,
    )


def near_sums(n, tables, strength):
    own, partner, far, partner_far = tables
    outward = 2 * (lax.axis_index("grid") % 2) - 1
    slab = lax.axis_index("grid")
    total = own[...]
    for table, offset in (
        (partner[...], -outward),
        (far[0 : n.panel, :], outward),
        (far[n.panel : 2 * n.panel, :], 2 * outward),
        (partner_far[0 : n.panel, :], -2 * outward),
        (partner_far[n.panel : 2 * n.panel, :], -3 * outward),
    ):
        total = total + pltpu.roll(table, (offset * ATOM_DEV + LANES) % LANES, 1)
    count = strength.shape[1]
    atom = lax.broadcasted_iota(jnp.int32, (count, LANES), 0)
    slot = lax.broadcasted_iota(jnp.int32, (count, LANES), 1) + (slab - 1) * ATOM_DEV
    near = jnp.dot(
        jnp.broadcast_to(strength[...], (n.panel, count)),
        (atom == slot).astype(jnp.float32),
        precision=lax.Precision.HIGHEST,
        preferred_element_type=jnp.float32,
    )
    lane = lax.broadcasted_iota(jnp.int32, total.shape, 1)
    total = jnp.where(lane < 3 * ATOM_DEV, total * near, 0.0)
    slot = lax.broadcasted_iota(jnp.int32, (LANES, n.atoms), 1) % SLOTS
    lane = lax.broadcasted_iota(jnp.int32, (LANES, n.atoms), 0)
    return jnp.dot(
        total,
        (slot == lane).astype(jnp.float32),
        precision=lax.Precision.HIGHEST,
        preferred_element_type=jnp.float32,
    )


def by_side(inner, outer, run):
    odd = lax.axis_index("grid") % 2
    pl.when(odd == 0)(functools.partial(run, outer, inner))
    pl.when(odd == 1)(functools.partial(run, inner, outer))


def level_of(n, potential, plane, block, part):
    first = plane * (PLANE // LANES) + block * (BLOCK // LANES) + part * (TILE // LANES)
    return jnp.concatenate(
        [
            jnp.broadcast_to(potential[pl.ds(first + k, 1), :], (n.panel, LANES))
            for k in range(TILE // LANES)
        ],
        axis=1,
    )


def local_part(n, field, potential, sums, emit):
    for chunk in range(len(CHUNKS)):

        def one(block):
            for part in range(BLOCK // TILE):
                starts = [n.start(plane, block, part) for plane in range(n.depth)]
                planes = [field[:, pl.ds(start, TILE)].astype(jnp.float32) for start in starts]
                for plane in range(n.depth):
                    row = aligned(block * n.stride + plane * n.panel, 8)
                    lap = (
                        3.0 * stencil_weights[0] * planes[plane]
                        + stencil_weights[1]
                        * sums[pl.ds(row, n.panel), part * TILE : (part + 1) * TILE]
                        + z_sum(planes, plane, 0)
                    )
                    level = level_of(n, potential, plane, block, part)
                    value = -0.5 * lap + (level - cheb_center) * planes[plane]
                    emit(chunk, (plane, block, part), pl.ds(starts[plane], TILE), value)

        n.each_block(chunk, one)


def lap_beside(n, low, high, starts):
    below = [low[:, pl.ds(start, TILE)].astype(jnp.float32) for start in starts]
    above = [high[:, pl.ds(start, TILE)].astype(jnp.float32) for start in starts]
    return [
        z_sum(below, plane, -n.depth) + z_sum(above, plane, n.depth) for plane in range(n.depth)
    ]


def table_kernel(n, field, entry_ref, table, partial, packed, place):
    rows = n.entries // LANES

    def entry_row(first):
        return jnp.concatenate(
            [entry_ref[first * rows + k : first * rows + k + 1, :] for k in range(rows)], axis=1
        )

    row_at, lane_at = entry_row(0), entry_row(1)
    lane = lax.broadcasted_iota(jnp.int32, (BLOCK, n.entries), 0).astype(jnp.float32)
    place[...] = jnp.where(lane == lane_at, entry_row(2), 0.0).astype(jnp.bfloat16)
    chunk = 4 * n.atoms
    for first in range(0, n.blocks * n.atoms, chunk):
        row = lax.broadcasted_iota(jnp.int32, (chunk, n.entries), 0) + first
        hit = jnp.where(row.astype(jnp.float32) == row_at, 1.0, 0.0).astype(jnp.bfloat16)
        table[first : first + chunk, :] = lax.dot_general(
            hit, place[...], (((1,), (1,)), ((), ())), preferred_element_type=jnp.float32
        ).astype(jnp.bfloat16)
    pack_planes(n, field, (packed,))
    atom_partial(n, (packed,), table, partial)


def first_local_kernel(n, field, packed, potential, taps, out, sums):
    apply_taps(n, (packed,), taps, sums)

    def emit(chunk, tile, cells, value):
        out[:, cells] = value * (1.0 / cheb_half)

    local_part(n, field, potential, sums, emit)


def first_halo_kernel(n, local, inner, outer, table, strength, *refs):
    tables, out, sents = refs[:4], refs[4], refs[5:]
    wide = near_sums(n, tables, strength)
    rows = jnp.where(
        block_diagonal(n.depth, n.panel, SLOTS), jnp.concatenate([wide] * n.depth, axis=0), 0.0
    )
    rows = jnp.concatenate(split(rows), axis=1)

    def run(low, high):
        for chunk in range(len(CHUNKS)):

            def one(block):
                weights = table[pl.ds(aligned(block * n.atoms, 16), n.atoms), :]
                weights = jnp.concatenate([weights, weights], axis=0)
                spread = jnp.dot(rows, weights, preferred_element_type=jnp.float32)
                for part in range(BLOCK // TILE):
                    starts = [n.start(plane, block, part) for plane in range(n.depth)]
                    laps = lap_beside(n, low, high, starts)
                    for plane in range(n.depth):
                        near = spread[
                            plane * n.panel : (plane + 1) * n.panel,
                            part * TILE : (part + 1) * TILE,
                        ]
                        cells = pl.ds(starts[plane], TILE)
                        value = local[:, cells] + (near - 0.5 * laps[plane]) * (1.0 / cheb_half)
                        out[:, cells] = value
                        cells = pl.ds(n.chunk_start(chunk, plane, block, part), TILE)
                        sents[chunk][:, cells] = value.astype(jnp.bfloat16)

            n.each_block(chunk, one)

    by_side(inner, outer, run)


def second_sums_kernel(n, field, table, partial, packed, rest):
    pack_planes(n, field, (packed, rest))
    atom_partial(n, (packed, rest), table, partial)


def second_local_kernel(n, field, initial, packed, rest, potential, taps, *refs):
    *outs, sums = refs
    apply_taps(n, (packed, rest), taps, sums)

    def emit(chunk, tile, cells, value):
        value = value * (2.0 / cheb_half) - initial[:, cells].astype(jnp.float32)
        outs[chunk][:, pl.ds(n.chunk_start(chunk, *tile), TILE)] = value

    local_part(n, field, potential, sums, emit)


def second_halo_kernel(n, chunk, local, inner, outer, out, sent):
    def run(low, high):
        def one(block):
            for part in range(BLOCK // TILE):
                starts = [n.chunk_start(chunk, plane, block, part) for plane in range(n.depth)]
                laps = lap_beside(n, low, high, starts)
                for plane in range(n.depth):
                    cells = pl.ds(starts[plane], TILE)
                    value = local[:, cells] - laps[plane] * (1.0 / cheb_half)
                    out[:, cells] = value
                    sent[:, cells] = value.astype(jnp.bfloat16)

        n.each_block(chunk, one)

    by_side(inner, outer, run)


def atoms_kernel(n, strength, *refs):
    *tables, out = refs
    wide = near_sums(n, tables, strength) * (2.0 / cheb_half)
    out[...] = jnp.concatenate(
        [wide[:, 0:SLOTS], jnp.zeros((n.panel, LANES - SLOTS), jnp.float32)], axis=1
    )


def rotate_kernel(n, columns, rotation_ref, *refs):
    count = len(CHUNKS)
    *refs, table, filtered, rotated, rows_ref = refs
    orbs = len(refs) // (count + 1)
    adds, panels = refs[:orbs], refs[orbs:]
    rows = orbs * n.panel

    @pl.when(pl.program_id(0) == 0)
    def _():
        added = jnp.concatenate([add[...] for add in adds], axis=0)[:, 0:SLOTS]
        both = jnp.dot(
            rotation_ref[...],
            added,
            precision=lax.Precision.HIGHEST,
            preferred_element_type=jnp.float32,
        )
        top = jnp.concatenate([rotation_ref[...], both], axis=1)
        bottom = jnp.concatenate(
            [jnp.zeros((n.panel, rows), jnp.float32), added[0 : n.panel, :]], axis=1
        )
        rows_ref[...] = jnp.concatenate(split(jnp.concatenate([top, bottom], axis=0)), axis=1)

    plane = pl.program_id(0)
    size = columns + n.panel
    matrix = rows_ref[...]
    for chunk, (low, high) in enumerate(CHUNKS):
        for block in range(low, high):
            cut = pl.ds(n.chunk_start(chunk, plane, block), BLOCK)
            parts = [panel[:, cut].astype(jnp.float32) for panel in panels[chunk::count]]
            stack = jnp.concatenate(parts, axis=0).astype(jnp.bfloat16)
            atoms = table[pl.ds(aligned(block * n.atoms + plane * SLOTS, 16), SLOTS), :]
            stack = jnp.concatenate([stack, atoms] * 2, axis=0)
            both = jnp.dot(matrix, stack, preferred_element_type=jnp.float32)
            cells = slice(block * BLOCK, (block + 1) * BLOCK)
            filtered[:, cells] = (parts[0] + both[columns:size, :]).astype(jnp.bfloat16)
            rotated[:, cells] = both[0:columns, :].astype(jnp.bfloat16)


def call(kernel, out_shape, scratch, flops, *operands):
    bytes_accessed = sum(int(np.prod(o.shape)) * o.dtype.itemsize for o in operands)
    return pl.pallas_call(
        kernel,
        out_shape=out_shape,
        in_specs=[pl.BlockSpec(memory_space=pltpu.VMEM)] * len(operands),
        out_specs=jax.tree.map(lambda _: pl.BlockSpec(memory_space=pltpu.VMEM), out_shape),
        scratch_shapes=scratch,
        compiler_params=pltpu.CompilerParams(vmem_limit_bytes=VMEM_LIMIT),
        cost_estimate=pl.CostEstimate(
            flops=flops, bytes_accessed=bytes_accessed, transcendentals=0
        ),
    )(*operands)


def swapped(block, partner):
    count = lax.axis_size("grid")
    pairs = [(i, partner(i)) for i in range(count) if 0 <= partner(i) < count]
    return lax.ppermute(block, "grid", pairs)


def core_partner(i):
    return i ^ 1


def outer_partner(i):
    return i + 1 if i % 2 else i - 1


def exchange_sums(partial, after=None):
    partner = swapped(partial, core_partner)
    both = jnp.concatenate([partial, partner], axis=0)
    if after is not None:
        both, _ = lax.optimization_barrier((both, after))
    far = swapped(both, outer_partner)
    return partial, partner, far, swapped(far, core_partner)


def body(
    orbitals,
    potential,
    projector_atom,
    projector_cell,
    projector_value,
    atom_strength,
    ritz_rotation,
    panel_owner,
):
    panel, cells = orbitals.shape
    n = Sizes(panel, cells, projector_atom.shape[0])
    chunks = range(len(CHUNKS))
    taps = jnp.asarray(plane_taps())
    level = potential.reshape(n.cells // LANES, LANES)
    strength = atom_strength[None, :]

    bf16, f32 = jnp.bfloat16, jnp.float32
    shape = jax.ShapeDtypeStruct
    field = shape((panel, cells), f32)
    fields = [shape((panel, n.chunk_cells(chunk)), f32) for chunk in chunks]
    narrows = [shape((panel, n.chunk_cells(chunk)), bf16) for chunk in chunks]
    sums = shape((panel, LANES), f32)
    packed_shape = shape(((n.blocks + 2) * n.stride, BLOCK), bf16)
    tap_sums = pltpu.VMEM((n.blocks * n.stride, BLOCK), f32)

    inner, outer = swapped(orbitals, core_partner), swapped(orbitals, outer_partner)
    plane, inside = projector_cell // PLANE, projector_cell % PLANE
    slot = projector_atom - (lax.axis_index("grid") - 1) * ATOM_DEV
    row_at = ((inside // BLOCK) * n.depth + plane) * SLOTS + slot
    entries = jnp.concatenate(
        [
            entry.astype(f32).reshape(n.entries // LANES, LANES)
            for entry in (row_at, inside % BLOCK, projector_value)
        ],
        axis=0,
    )
    table, partial, packed = call(
        functools.partial(table_kernel, n),
        (shape((n.blocks * n.atoms, BLOCK), bf16), sums, packed_shape),
        [pltpu.VMEM((BLOCK, n.entries), bf16)],
        4 * 10**9,
        orbitals, entries,
    )
    local = call(
        functools.partial(first_local_kernel, n), field, [tap_sums], 2 * 10**9,
        orbitals, packed, level, taps,
    )
    near = exchange_sums(partial, local)
    step_field, *sents = call(
        functools.partial(first_halo_kernel, n),
        [field] + narrows, [], 10**9,
        local, inner, outer, table, strength, *near,
    )
    halos = [(swapped(sent, core_partner), swapped(sent, outer_partner)) for sent in sents]
    partial, packed, rest = call(
        functools.partial(second_sums_kernel, n),
        (sums, packed_shape, packed_shape), [], 10**9,
        step_field, table,
    )
    near = exchange_sums(partial)
    locals_ = call(
        functools.partial(second_local_kernel, n), fields, [tap_sums], 3 * 10**9,
        step_field, orbitals, packed, rest, level, taps,
    )

    orb_count = lax.axis_size("orb")

    def all_orbs(block):
        return [block] + [
            lax.ppermute(block, "orb", [(i, (i + k) % orb_count) for i in range(orb_count)])
            for k in range(1, orb_count)
        ]

    shares = []
    for chunk in chunks:
        own, sent = call(
            functools.partial(second_halo_kernel, n, chunk),
            (fields[chunk], narrows[chunk]), [], 10**9,
            locals_[chunk], *halos[chunk],
        )
        shares.append([own] + all_orbs(sent)[1:])
    added = call(functools.partial(atoms_kernel, n), sums, [], 10**6, strength, *near)
    adds = all_orbs(added)
    panels = [shares[chunk][k] for k in range(orb_count) for chunk in chunks]
    source = (lax.axis_index("orb") - jnp.arange(orb_count)) % orb_count
    chosen = (panel_owner[None, :] == source[:, None]).astype(f32)
    rotation = jnp.sum(
        chosen[:, :, None, None] * ritz_rotation.astype(f32)[None], axis=1
    )
    columns = ritz_rotation.shape[2]
    rotation = rotation.reshape(orb_count * panel, columns).T
    operands = (rotation, *adds, *panels, table)
    filtered, rotated = pl.pallas_call(
        functools.partial(rotate_kernel, n, columns),
        grid=(n.depth,),
        out_shape=(shape((panel, n.cells), bf16), shape((columns, n.cells), bf16)),
        in_specs=[pl.BlockSpec(memory_space=pltpu.VMEM)] * len(operands),
        out_specs=(
            pl.BlockSpec((panel, PLANE), lambda i: (0, i)),
            pl.BlockSpec((columns, PLANE), lambda i: (0, i)),
        ),
        scratch_shapes=[
            pltpu.VMEM((columns + panel, 2 * (orb_count * panel + SLOTS)), bf16)
        ],
        compiler_params=pltpu.CompilerParams(vmem_limit_bytes=VMEM_LIMIT),
    )(*operands)
    return (filtered, rotated)


def solution(mesh):
    in_specs = (
        P("orb", "grid"),
        P("grid"),
        P("grid"),
        P("grid"),
        P("grid"),
        P(),
        P(None, None, "orb"),
        P(),
    )
    out_specs = (P("orb", "grid"), P("orb", "grid"))
    return jax.shard_map(body, mesh=mesh, in_specs=in_specs, out_specs=out_specs, check_vma=False)
```

time: 80.4 us -> 74.7 us (0.929)
  starting transfers between devices: 18.8 us -> 15.8 us
  other arithmetic: 0.27 us -> 2.92 us
  local copies, waits for them, and re-layouts: 4.11 us -> 1.95 us
  waiting for transfers between devices: 30.1 us -> 28.6 us
    ppermute x2, waiting for transfers between devices: 9.76 us -> 2.25 us  [all_orbs(): lax.ppermute(block, 'orb', [(i, (i + k) % orb_count) for i in range(orb_c...]
    ppermute x12 -> x10, waiting for transfers between devices: 20.4 us -> 26.3 us  [swapped(): return lax.ppermute(block, 'grid', pairs)]
    ppermute x12 -> x10, starting transfers between devices: 18.1 us -> 14.3 us  [swapped(): return lax.ppermute(block, 'grid', pairs)]
    unnamed x26 -> x10, local copies, waits for them, and re-layouts: 3.95 us -> 1.18 us
    pallas_call x7, Pallas kernels: 21.6 us -> 19.3 us  [call(): pl.pallas_call(kernel, out_shape=out_shape, in_specs=[pl.BlockSpec(memory...]
    pallas_call x1, Pallas kernels: 3.37 us -> 4.97 us  [body(): pl.pallas_call(functools.partial(rotate_kernel, n, columns), grid=(n.dept...]
    ppermute x2, starting transfers between devices: 0.63 us -> 1.49 us  [all_orbs(): lax.ppermute(block, 'orb', [(i, (i + k) % orb_count) for i in range(orb_c...]
  transfers between devices with their start and end apart: 14 -> 12, of which waited for: 7 -> 7; matrix products, arithmetic and copies ran while one was open for 1% -> 5% of each run, Pallas kernels for 20% -> 20%
where the time goes in v3:
time: 74.7 us; the launch traced here: 74.2 us
  waiting for transfers between devices  28.6 us (38%)
  Pallas kernels  24.2 us (32%)
  starting transfers between devices  15.8 us (21%)
  other arithmetic  2.92 us (4%)
  local copies, waits for them, and re-layouts  1.95 us (3%)
  between operations  0.75 us (1%)
    ppermute x10, waiting for transfers between devices, swapped(): return lax.ppermute(block, 'grid', pairs)  26.3 us
    pallas_call x7, Pallas kernels, call(): pl.pallas_call(kernel, out_shape=out_shape, in_specs=[pl.BlockSpec(memory...  19.3 us
    ppermute x10, starting transfers between devices, swapped(): return lax.ppermute(block, 'grid', pairs)  14.3 us
    pallas_call x1, Pallas kernels, body(): pl.pallas_call(functools.partial(rotate_kernel, n, columns), grid=(n.dept...  4.97 us
    ppermute x2, waiting for transfers between devices, all_orbs(): lax.ppermute(block, 'orb', [(i, (i + k) % orb_count) for i in range(orb_c...  2.25 us
  transfers between devices with their start and end apart: 12, of which 7 were waited for; matrix products, arithmetic and copies ran while one was open for 5% of the time, Pallas kernels for 20%

profile of v3, /device:TPU:11, one launch (start us, length us, event | category | flops | bytes accessed | tf_op | source)
XLA Modules:
  0.0 74.2 jit_solution(1855837919907812831)
XLA Ops:
  0.6 0.7 collective-permute-start
  1.4 3.1 %collective-permute-start.1 = (bf16[8,55296]{1,0:T(8,128)(2,1)}, bf16[8,55296]{1,0:T(8,128)(2,1)S(1)}, u32[]{:S(2)}, u32[]{:S(2)}) collective-permute-start(bf16[8,55296]{1,0:T(8,128)(2,1)} %initial.1), channel_id=1, source_target_pairs={{2,4},{4,2},{6,8},{8,6},{10,12},{12,10},{14,16},{16,14},{18,20},{2... | collective-permute-start | bytes 2654216 | tf_op jit(solution)/shard_map/ppermute | solution.py:415
  4.4 0.7 %fusion.5 = (f32[12,128]{1,0:T(8,128)S(1)}, f32[12,128]{1,0:T(8,128)S(1)}) fusion(s32[1536]{0:T(1024)} %param.11, s32[1536]{0:T(1024)} %param.12, s32[]{:T(128)S(6)} %mul.35), kind=kLoop, calls=%fused_computation.11 | loop fusion | flops 47616 | bytes 24580 | tf_op jit(solution)/shard_map/reshape | solution.py:467
  5.2 0.7 pad_maximum_fusion.entry_ref
  5.9 0.0 copy-start.1
  5.9 1.2 %copy-done.1 = bf16[8,55296]{1,0:T(8,128)(2,1)S(1)} copy-done((bf16[8,55296]{1,0:T(8,128)(2,1)S(1)}, bf16[8,55296]{1,0:T(8,128)(2,1)}, u32[]{:S(2)}) %copy-start.1) | copy-done | bytes 884760
  7.1 0.0 copy-start
  7.1 0.0 copy-start.2
  7.1 4.6 %shard_map.104 = (bf16[1152,768]{1,0:T(8,128)(2,1)S(1)}, f32[8,128]{1,0:T(8,128)S(1)}, bf16[672,768]{1,0:T(8,128)(2,1)S(1)}) custom-call(bf16[8,55296]{1,0:T(8,128)(2,1)S(1)} %copy-done.1, f32[36,128]{1,0:T(8,128)S(1)} %pad_maximum_fusion.entry_ref), custom_call_target="tpu_custom_call" | custom-call | flops 4000000000 | bytes 903168 | tf_op jit(solution)/shard_map/pallas_call | solution.py:399
  11.7 0.4 collective-permute-start.2
  12.1 0.0 copy-done
  12.1 0.0 copy-done.2
  12.1 0.0 copy-start.3
  12.1 3.1 %shard_map.105.local = f32[8,55296]{1,0:T(8,128)S(1)} custom-call(bf16[8,55296]{1,0:T(8,128)(2,1)S(1)} %copy-done.1, bf16[672,768]{1,0:T(8,128)(2,1)S(1)} %get-tuple-element.13.packed, f32[432,128]{1,0:T(8,128)S(1)} %bitcast.9, bf16[3,768,768]{2,1,0:T(8,128)(2,1)S(1)} %copy-done), custom_call_target="tpu_custom_call" | custom-call | flops 2000000000 | bytes 5677056 | tf_op jit(solution)/shard_map/pallas_call | solution.py:399
  15.2 0.0 collective-permute-done.2.refs_1_
  15.2 3.2 %collective-permute-start.3 = (f32[16,128]{1,0:T(8,128)S(1)}, f32[16,128]{1,0:T(8,128)S(1)}, u32[]{:S(2)}, u32[]{:S(2)}) collective-permute-start(f32[16,128]{1,0:T(8,128)S(1)} %pad_maximum_fusion.1), channel_id=1, source_target_pairs={{2,4},{4,2},{6,8},{8,6},{10,12},{12,10},{14,16},{16,14},{18,20},{2... | collective-permute-start | bytes 24584 | tf_op jit(solution)/shard_map/ppermute | solution.py:415
  18.4 7.2 %collective-permute-done.3.refs_2_ = f32[16,128]{1,0:T(8,128)S(1)} collective-permute-done((f32[16,128]{1,0:T(8,128)S(1)}, f32[16,128]{1,0:T(8,128)S(1)}, u32[]{:S(2)}, u32[]{:S(2)}) %collective-permute-start.3) | collective-permute-done | bytes 8224 | tf_op jit(solution)/shard_map/ppermute | solution.py:415
  25.6 0.0 collective-permute-start.4
  25.6 1.2 %collective-permute-done.4.refs_3_ = f32[16,128]{1,0:T(8,128)S(1)} collective-permute-done((f32[16,128]{1,0:T(8,128)S(1)}, f32[16,128]{1,0:T(8,128)S(1)}, u32[]{:S(2)}, u32[]{:S(2)}) %collective-permute-start.4) | collective-permute-done | bytes 8224 | tf_op jit(solution)/shard_map/ppermute | solution.py:415
  26.8 0.0 collective-permute-done.inner
  26.8 0.0 collective-permute-done.1.outer
  26.8 0.0 copy-done.3
  26.8 2.7 %shard_map.106 = (f32[8,55296]{1,0:T(8,128)S(1)}, bf16[8,55296]{1,0:T(8,128)(2,1)S(1)}) custom-call(f32[8,55296]{1,0:T(8,128)S(1)} %shard_map.105.local, bf16[8,55296]{1,0:T(8,128)(2,1)S(1)} %collective-permute-done.inner, bf16[8,55296]{1,0:T(8,128)(2,1)S(1)} %collective-permute-done.1.outer, bf16[1152,768]{1,0:T(8,128)(2,1)S(1)} %get-tuple-element.14.table.refs_4_, ...), custom_call_target="tpu_custom_call" | custom-call | flops 1000000000 | bytes 5333248 | tf_op jit(solution)/shard_map/pallas_call | solution.py:399
  29.5 3.0 %collective-permute-start.10 = (bf16[8,55296]{1,0:T(8,128)(2,1)S(1)}, bf16[8,55296]{1,0:T(8,128)(2,1)S(1)}, u32[]{:S(2)}, u32[]{:S(2)}) collective-permute-start(bf16[8,55296]{1,0:T(8,128)(2,1)S(1)} %get-tuple-element.21), channel_id=1, source_target_pairs={{2,4},{4,2},{6,8},{8,6},{10,12},{12,10},{14,16},{16,14},{18,20},{2... | collective-permute-start | bytes 2654216 | tf_op jit(solution)/shard_map/ppermute | solution.py:415
  32.5 0.1 collective-permute-start.9
  32.7 1.7 %shard_map.107 = (f32[8,128]{1,0:T(8,128)S(1)}, bf16[672,768]{1,0:T(8,128)(2,1)S(1)}, bf16[672,768]{1,0:T(8,128)(2,1)S(1)}) custom-call(f32[8,55296]{1,0:T(8,128)S(1)} %get-tuple-element.17.field, bf16[1152,768]{1,0:T(8,128)(2,1)S(1)} %get-tuple-element.14.table.refs_4_), custom_call_target="tpu_custom_call" | custom-call | flops 1000000000 | bytes 3538944 | tf_op jit(solution)/shard_map/pallas_call | solution.py:399
  34.4 4.9 %shard_map.109.local = f32[8,55296]{1,0:T(8,128)S(1)} custom-call(f32[8,55296]{1,0:T(8,128)S(1)} %get-tuple-element.17.field, bf16[8,55296]{1,0:T(8,128)(2,1)S(1)} %copy-done.1, bf16[672,768]{1,0:T(8,128)(2,1)S(1)} %get-tuple-element.19.packed, bf16[672,768]{1,0:T(8,128)(2,1)S(1)} %get-tuple-element.20.rest, f32[432,128]{1,0:T(8,128)S(1)} %bitcast.10, ...), custom_call_target="tpu_custom_call" | custom-call | flops 3000000000 | bytes 8478720 | tf_op jit(solution)/shard_map/pallas_call | solution.py:399
  39.3 0.0 copy-start.4
  39.3 14.4 %collective-permute-done.10.outer = bf16[8,55296]{1,0:T(8,128)(2,1)S(1)} collective-permute-done((bf16[8,55296]{1,0:T(8,128)(2,1)S(1)}, bf16[8,55296]{1,0:T(8,128)(2,1)S(1)}, u32[]{:S(2)}, u32[]{:S(2)}) %collective-permute-start.10) | collective-permute-done | bytes 884768 | tf_op jit(solution)/shard_map/ppermute | solution.py:415
  53.7 0.0 collective-permute-done.9.inner
  53.7 2.0 %shard_map.110 = (f32[8,55296]{1,0:T(8,128)S(1)}, bf16[8,55296]{1,0:T(8,128)(2,1)}) custom-call(f32[8,55296]{1,0:T(8,128)S(1)} %shard_map.109.local, bf16[8,55296]{1,0:T(8,128)(2,1)S(1)} %collective-permute-done.9.inner, bf16[8,55296]{1,0:T(8,128)(2,1)S(1)} %collective-permute-done.10.outer), custom_call_target="tpu_custom_call" | custom-call | flops 1000000000 | bytes 3538944 | tf_op jit(solution)/shard_map/pallas_call | solution.py:399
  55.7 0.3 collective-permute-start.11
  56.0 0.0 collective-permute-start.5
  56.0 1.2 %collective-permute-done.5.refs_1_ = f32[8,128]{1,0:T(8,128)S(1)} collective-permute-done((f32[8,128]{1,0:T(8,128)S(1)}, f32[8,128]{1,0:T(8,128)S(1)}, u32[]{:S(2)}, u32[]{:S(2)}) %collective-permute-start.5) | collective-permute-done | bytes 4128 | tf_op jit(solution)/shard_map/ppermute | solution.py:415
  57.2 2.9 %collective-permute-start.6 = (f32[16,128]{1,0:T(8,128)S(1)}, f32[16,128]{1,0:T(8,128)S(1)}, u32[]{:S(2)}, u32[]{:S(2)}) collective-permute-start(f32[16,128]{1,0:T(8,128)S(1)} %pad_maximum_fusion.2), channel_id=1, source_target_pairs={{2,4},{4,2},{6,8},{8,6},{10,12},{12,10},{14,16},{16,14},{18,20},{2... | collective-permute-start | bytes 24584 | tf_op jit(solution)/shard_map/ppermute | solution.py:415
  60.1 2.3 %collective-permute-done.6.refs_2_ = f32[16,128]{1,0:T(8,128)S(1)} collective-permute-done((f32[16,128]{1,0:T(8,128)S(1)}, f32[16,128]{1,0:T(8,128)S(1)}, u32[]{:S(2)}, u32[]{:S(2)}) %collective-permute-start.6) | collective-permute-done | bytes 8224 | tf_op jit(solution)/shard_map/ppermute | solution.py:415
  62.4 0.8 %collective-permute-start.7 = (f32[16,128]{1,0:T(8,128)S(1)}, f32[16,128]{1,0:T(8,128)S(1)}, u32[]{:S(2)}, u32[]{:S(2)}) collective-permute-start(f32[16,128]{1,0:T(8,128)S(1)} %collective-permute-done.6.refs_2_), channel_id=1, source_target_pairs={{0,2},{2,0},{4,6},{6,4},{8,10},{10,8},{12,14},{14,12},{16,18},{18,... | collective-permute-start | bytes 24584 | tf_op jit(solution)/shard_map/ppermute | solution.py:415
  63.2 0.0 copy-done.4
  63.2 0.1 compare_convert_fusion
  63.3 0.7 convert_element_type.17
  64.0 0.1 collective-permute-done.7.refs_3_
  64.0 0.3 shard_map.108.refs_0_
  64.3 1.2 %collective-permute-start.8 = (f32[8,128]{1,0:T(8,128)S(1)}, f32[8,128]{1,0:T(8,128)S(1)}, u32[]{:S(2)}, u32[]{:S(2)}) collective-permute-start(f32[8,128]{1,0:T(8,128)S(1)} %shard_map.108.refs_0_), channel_id=1, source_target_pairs={{0,1},{1,0},{2,3},{3,2},{4,5},{5,4},{6,7},{7,6},{8,9},{9,8},{10,11... | collective-permute-start | bytes 12296 | tf_op jit(solution)/shard_map/ppermute | solution.py:505
  65.5 0.7 multiply_reduce_fusion
  66.2 0.8 %copy.12 = f32[16,16]{0,1:T(8,128)S(1)} copy(f32[16,16]{1,0:T(8,128)} %bitcast.14) | data formatting | bytes 2048 | tf_op jit(solution)/shard_map/reshape | solution.py:526
  67.0 2.2 %collective-permute-done.8.refs_1_ = f32[8,128]{1,0:T(8,128)S(1)} collective-permute-done((f32[8,128]{1,0:T(8,128)S(1)}, f32[8,128]{1,0:T(8,128)S(1)}, u32[]{:S(2)}, u32[]{:S(2)}) %collective-permute-start.8) | collective-permute-done | bytes 4128 | tf_op jit(solution)/shard_map/ppermute | solution.py:505
  69.2 0.0 collective-permute-done.11.refs_3_
  69.2 5.0 %shard_map.111 = (bf16[8,55296]{1,0:T(8,128)(2,1)}, bf16[16,55296]{1,0:T(8,128)(2,1)}) custom-call(f32[16,16]{1,0:T(8,128)S(1)} %bitcast.11, f32[8,128]{1,0:T(8,128)S(1)} %shard_map.108.refs_0_, f32[8,128]{1,0:T(8,128)S(1)} %collective-permute-done.8.refs_1_, f32[8,55296]{1,0:T(8,128)S(1)} %get-tuple-element.22.refs_2_, ...), custom_call_target="tpu_custom_call" | custom-call | tf_op jit(solution)/shard_map/pallas_call | solution.py:528
  (3 shorter events, 0.0 us)
Async XLA Ops:
  0.6 26.1 %collective-permute-start = (bf16[8,55296]{1,0:T(8,128)(2,1)}, bf16[8,55296]{1,0:T(8,128)(2,1)S(1)}, u32[]{:S(2)}, u32[]{:S(2)}) collective-permute-start(bf16[8,55296]{1,0:T(8,128)(2,1)} %initial.1), channel_id=1, source_target_pairs={{0,2},{2,0},{4,6},{6,4},{8,10},{10,8},{12,14},{14,12},{16,18},{18,... | collective-permute-start | bytes 2654216 | tf_op jit(solution)/shard_map/ppermute | solution.py:415
  1.4 25.4 %collective-permute-start.1 = (bf16[8,55296]{1,0:T(8,128)(2,1)}, bf16[8,55296]{1,0:T(8,128)(2,1)S(1)}, u32[]{:S(2)}, u32[]{:S(2)}) collective-permute-start(bf16[8,55296]{1,0:T(8,128)(2,1)} %initial.1), channel_id=1, source_target_pairs={{2,4},{4,2},{6,8},{8,6},{10,12},{12,10},{14,16},{16,14},{18,20},{2... | collective-permute-start | bytes 2654216 | tf_op jit(solution)/shard_map/ppermute | solution.py:415
  5.9 1.2 %copy-start.1 = (bf16[8,55296]{1,0:T(8,128)(2,1)S(1)}, bf16[8,55296]{1,0:T(8,128)(2,1)}, u32[]{:S(2)}) copy-start(bf16[8,55296]{1,0:T(8,128)(2,1)} %initial.1) | copy-start | bytes 2654212
  7.1 5.0 %copy-start = (bf16[3,768,768]{2,1,0:T(8,128)(2,1)S(1)}, bf16[3,768,768]{2,1,0:T(8,128)(2,1)}, u32[]{:S(2)}) copy-start(bf16[3,768,768]{2,1,0:T(8,128)(2,1)} %constant.65.clone.taps) | copy-start | bytes 10616836
  7.1 5.0 %copy-start.2 = (f32[55296]{0:T(1024)S(1)}, f32[55296]{0:T(1024)}, u32[]{:S(2)}) copy-start(f32[55296]{0:T(1024)} %param.10) | copy-start | bytes 663556
  11.7 3.5 %collective-permute-start.2 = (f32[8,128]{1,0:T(8,128)S(1)}, f32[8,128]{1,0:T(8,128)S(1)}, u32[]{:S(2)}, u32[]{:S(2)}) collective-permute-start(f32[8,128]{1,0:T(8,128)S(1)} %get-tuple-element.15.refs_0_), channel_id=1, source_target_pairs={{0,2},{2,0},{4,6},{6,4},{8,10},{10,8},{12,14},{14,12},{16,18},{18,... | collective-permute-start | bytes 12296 | tf_op jit(solution)/shard_map/ppermute | solution.py:415
  12.1 14.7 %copy-start.3 = (f32[64]{0:T(128)S(1)}, f32[64]{0:T(128)}, u32[]{:S(2)}) copy-start(f32[64]{0:T(128)} %param.14) | copy-start | bytes 772
  15.2 10.4 %collective-permute-start.3 = (f32[16,128]{1,0:T(8,128)S(1)}, f32[16,128]{1,0:T(8,128)S(1)}, u32[]{:S(2)}, u32[]{:S(2)}) collective-permute-start(f32[16,128]{1,0:T(8,128)S(1)} %pad_maximum_fusion.1), channel_id=1, source_target_pairs={{2,4},{4,2},{6,8},{8,6},{10,12},{12,10},{14,16},{16,14},{18,20},{2... | collective-permute-start | bytes 24584 | tf_op jit(solution)/shard_map/ppermute | solution.py:415
  25.6 1.2 %collective-permute-start.4 = (f32[16,128]{1,0:T(8,128)S(1)}, f32[16,128]{1,0:T(8,128)S(1)}, u32[]{:S(2)}, u32[]{:S(2)}) collective-permute-start(f32[16,128]{1,0:T(8,128)S(1)} %collective-permute-done.3.refs_2_), channel_id=1, source_target_pairs={{0,2},{2,0},{4,6},{6,4},{8,10},{10,8},{12,14},{14,12},{16,18},{18,... | collective-permute-start | bytes 24584 | tf_op jit(solution)/shard_map/ppermute | solution.py:415
  29.5 24.2 %collective-permute-start.10 = (bf16[8,55296]{1,0:T(8,128)(2,1)S(1)}, bf16[8,55296]{1,0:T(8,128)(2,1)S(1)}, u32[]{:S(2)}, u32[]{:S(2)}) collective-permute-start(bf16[8,55296]{1,0:T(8,128)(2,1)S(1)} %get-tuple-element.21), channel_id=1, source_target_pairs={{2,4},{4,2},{6,8},{8,6},{10,12},{12,10},{14,16},{16,14},{18,20},{2... | collective-permute-start | bytes 2654216 | tf_op jit(solution)/shard_map/ppermute | solution.py:415
  32.5 21.2 %collective-permute-start.9 = (bf16[8,55296]{1,0:T(8,128)(2,1)S(1)}, bf16[8,55296]{1,0:T(8,128)(2,1)S(1)}, u32[]{:S(2)}, u32[]{:S(2)}) collective-permute-start(bf16[8,55296]{1,0:T(8,128)(2,1)S(1)} %get-tuple-element.21), channel_id=1, source_target_pairs={{0,2},{2,0},{4,6},{6,4},{8,10},{10,8},{12,14},{14,12},{16,18},{18,... | collective-permute-start | bytes 2654216 | tf_op jit(solution)/shard_map/ppermute | solution.py:415
  39.3 23.9 %copy-start.4 = (s32[4]{0:T(128)S(1)}, s32[4]{0:T(128)}, u32[]{:S(2)}) copy-start(s32[4]{0:T(128)} %param.16) | copy-start | bytes 52
  55.7 13.5 %collective-permute-start.11 = (bf16[8,55296]{1,0:T(8,128)(2,1)}, bf16[8,55296]{1,0:T(8,128)(2,1)}, u32[]{:S(2)}, u32[]{:S(2)}) collective-permute-start(bf16[8,55296]{1,0:T(8,128)(2,1)} %get-tuple-element.23), channel_id=1, source_target_pairs={{0,1},{1,0},{2,3},{3,2},{4,5},{5,4},{6,7},{7,6},{8,9},{9,8},{10,11... | collective-permute-start | bytes 2654216 | tf_op jit(solution)/shard_map/ppermute | solution.py:505
  56.0 1.2 %collective-permute-start.5 = (f32[8,128]{1,0:T(8,128)S(1)}, f32[8,128]{1,0:T(8,128)S(1)}, u32[]{:S(2)}, u32[]{:S(2)}) collective-permute-start(f32[8,128]{1,0:T(8,128)S(1)} %get-tuple-element.18.refs_0_), channel_id=1, source_target_pairs={{0,2},{2,0},{4,6},{6,4},{8,10},{10,8},{12,14},{14,12},{16,18},{18,... | collective-permute-start | bytes 12296 | tf_op jit(solution)/shard_map/ppermute | solution.py:415
  57.2 5.3 %collective-permute-start.6 = (f32[16,128]{1,0:T(8,128)S(1)}, f32[16,128]{1,0:T(8,128)S(1)}, u32[]{:S(2)}, u32[]{:S(2)}) collective-permute-start(f32[16,128]{1,0:T(8,128)S(1)} %pad_maximum_fusion.2), channel_id=1, source_target_pairs={{2,4},{4,2},{6,8},{8,6},{10,12},{12,10},{14,16},{16,14},{18,20},{2... | collective-permute-start | bytes 24584 | tf_op jit(solution)/shard_map/ppermute | solution.py:415
  62.4 1.6 %collective-permute-start.7 = (f32[16,128]{1,0:T(8,128)S(1)}, f32[16,128]{1,0:T(8,128)S(1)}, u32[]{:S(2)}, u32[]{:S(2)}) collective-permute-start(f32[16,128]{1,0:T(8,128)S(1)} %collective-permute-done.6.refs_2_), channel_id=1, source_target_pairs={{0,2},{2,0},{4,6},{6,4},{8,10},{10,8},{12,14},{14,12},{16,18},{18,... | collective-permute-start | bytes 24584 | tf_op jit(solution)/shard_map/ppermute | solution.py:415
  64.3 4.9 %collective-permute-start.8 = (f32[8,128]{1,0:T(8,128)S(1)}, f32[8,128]{1,0:T(8,128)S(1)}, u32[]{:S(2)}, u32[]{:S(2)}) collective-permute-start(f32[8,128]{1,0:T(8,128)S(1)} %shard_map.108.refs_0_), channel_id=1, source_target_pairs={{0,1},{1,0},{2,3},{3,2},{4,5},{5,4},{6,7},{7,6},{8,9},{9,8},{10,11... | collective-permute-start | bytes 12296 | tf_op jit(solution)/shard_map/ppermute | solution.py:505

commit v4 on v3

--- a/solution.py
+++ b/solution.py
@@ -331,7 +331,7 @@
     local_part(n, field, potential, sums, emit)
 
 
-def second_halo_kernel(n, chunk, local, inner, outer, out, sent):
+def second_halo_kernel(n, chunk, local, inner, outer, out):
     def run(low, high):
         def one(block):
             for part in range(BLOCK // TILE):
@@ -340,8 +340,7 @@
                 for plane in range(n.depth):
                     cells = pl.ds(starts[plane], TILE)
                     value = local[:, cells] - laps[plane] * (1.0 / cheb_half)
-                    out[:, cells] = value
-                    sent[:, cells] = value.astype(jnp.bfloat16)
+                    out[:, cells] = value.astype(jnp.bfloat16)
 
         n.each_block(chunk, one)
 
@@ -356,42 +355,95 @@
     )
 
 
-def rotate_kernel(n, columns, rotation_ref, *refs):
-    count = len(CHUNKS)
-    *refs, table, filtered, rotated, rows_ref = refs
-    orbs = len(refs) // (count + 1)
-    adds, panels = refs[:orbs], refs[orbs:]
-    rows = orbs * n.panel
+def weighted_rows(n, shifts, owner, ritz, added):
+    columns = ritz.shape[1]
+    blocks = []
+    for shift in shifts:
+        source = lax.axis_index("orb") + (lax.axis_size("orb") - shift)
+        source = jnp.where(source >= lax.axis_size("orb"), source - lax.axis_size("orb"), source)
+        total = jnp.zeros((n.panel, columns), jnp.float32)
+        for step in range(ritz.shape[0] // n.panel):
+            rows = ritz[step * n.panel : (step + 1) * n.panel, :].astype(jnp.float32)
+            total = total + jnp.where(owner[step] == source, rows, 0.0)
+        blocks.append(total)
+    weights = jnp.concatenate(blocks, axis=0)
+    eye = lax.broadcasted_iota(jnp.int32, (columns, columns), 0) == lax.broadcasted_iota(
+        jnp.int32, (columns, columns), 1
+    )
+    rotation = lax.dot_general(
+        eye.astype(jnp.float32),
+        weights,
+        (((1,), (1,)), ((), ())),
+        precision=lax.Precision.HIGHEST,
+        preferred_element_type=jnp.float32,
+    )
+    both = jnp.dot(
+        rotation,
+        added[:, 0:SLOTS],
+        precision=lax.Precision.HIGHEST,
+        preferred_element_type=jnp.float32,
+    )
+    return jnp.concatenate([rotation, both], axis=1)
+
+
+def tile_rows(n, panels, table, plane, block):
+    cells = pl.ds(n.start(plane, block), BLOCK)
+    parts = [panel[:, cells].astype(jnp.float32) for panel in panels]
+    stack = parts[0] if len(parts) == 1 else jnp.concatenate(parts, axis=0)
+    atoms = table[pl.ds(aligned(block * n.atoms + plane * SLOTS, 16), SLOTS), :]
+    stack = jnp.concatenate([stack, atoms.astype(jnp.float32)], axis=0).astype(jnp.bfloat16)
+    return parts[0], stack
+
+
+def rotate_own_kernel(n, owner, ritz, added, panel, table, filtered, rotated, rows_ref):
+    columns = ritz.shape[1]
 
     @pl.when(pl.program_id(0) == 0)
     def _():
-        added = jnp.concatenate([add[...] for add in adds], axis=0)[:, 0:SLOTS]
+        top = weighted_rows(n, (0,), owner, ritz, added[...])
+        bottom = jnp.concatenate(
+            [jnp.zeros((n.panel, n.panel), jnp.float32), added[:, 0:SLOTS]], axis=1
+        )
+        rows_ref[...] = jnp.concatenate(split(jnp.concatenate([top, bottom], axis=0)), axis=1)
+
+    plane = pl.program_id(0)
+    matrix = rows_ref[...]
+    for block in range(n.blocks):
+        own, stack = tile_rows(n, (panel,), table, plane, block)
         both = jnp.dot(
-            rotation_ref[...],
-            added,
-            precision=lax.Precision.HIGHEST,
+            matrix,
+            jnp.concatenate([stack, stack], axis=0),
             preferred_element_type=jnp.float32,
         )
-        top = jnp.concatenate([rotation_ref[...], both], axis=1)
-        bottom = jnp.concatenate(
-            [jnp.zeros((n.panel, rows), jnp.float32), added[0 : n.panel, :]], axis=1
+        cells = slice(block * BLOCK, (block + 1) * BLOCK)
+        filtered[:, cells] = (own + both[columns : columns + n.panel, :]).astype(jnp.bfloat16)
+        rotated[:, pl.ds(n.start(plane, block), BLOCK)] = both[0:columns, :]
+
+
+def rotate_rest_kernel(n, count, owner, ritz, *refs):
+    *refs, own, table, rotated, rows_ref = refs
+    adds, panels = refs[:count], refs[count:]
+
+    @pl.when(pl.program_id(0) == 0)
+    def _():
+        added = jnp.concatenate([add[...] for add in adds], axis=0)
+        rows = weighted_rows(n, range(1, count + 1), owner, ritz, added)
+        rows_ref[...] = jnp.concatenate(split(rows), axis=1)
+
+    plane = pl.program_id(0)
+    matrix = rows_ref[...]
+    for block in range(n.blocks):
+        cells = pl.ds(n.start(plane, block), BLOCK)
+        parts = [p[:, block * BLOCK : (block + 1) * BLOCK].astype(jnp.float32) for p in panels]
+        atoms = table[pl.ds(aligned(block * n.atoms + plane * SLOTS, 16), SLOTS), :]
+        parts.append(atoms.astype(jnp.float32))
+        stack = jnp.concatenate(parts, axis=0).astype(jnp.bfloat16)
+        total = own[:, cells] + jnp.dot(
+            matrix,
+            jnp.concatenate([stack, stack], axis=0),
+            preferred_element_type=jnp.float32,
         )
-        rows_ref[...] = jnp.concatenate(split(jnp.concatenate([top, bottom], axis=0)), axis=1)
-
-    plane = pl.program_id(0)
-    size = columns + n.panel
-    matrix = rows_ref[...]
-    for chunk, (low, high) in enumerate(CHUNKS):
-        for block in range(low, high):
-            cut = pl.ds(n.chunk_start(chunk, plane, block), BLOCK)
-            parts = [panel[:, cut].astype(jnp.float32) for panel in panels[chunk::count]]
-            stack = jnp.concatenate(parts, axis=0).astype(jnp.bfloat16)
-            atoms = table[pl.ds(aligned(block * n.atoms + plane * SLOTS, 16), SLOTS), :]
-            stack = jnp.concatenate([stack, atoms] * 2, axis=0)
-            both = jnp.dot(matrix, stack, preferred_element_type=jnp.float32)
-            cells = slice(block * BLOCK, (block + 1) * BLOCK)
-            filtered[:, cells] = (parts[0] + both[columns:size, :]).astype(jnp.bfloat16)
-            rotated[:, cells] = both[0:columns, :].astype(jnp.bfloat16)
+        rotated[:, block * BLOCK : (block + 1) * BLOCK] = total.astype(jnp.bfloat16)
 
 
 def call(kernel, out_shape, scratch, flops, *operands):
@@ -492,7 +544,6 @@
         (sums, packed_shape, packed_shape), [], 10**9,
         step_field, table,
     )
-    near = exchange_sums(partial)
     locals_ = call(
         functools.partial(second_local_kernel, n), fields, [tap_sums], 3 * 10**9,
         step_field, orbitals, packed, rest, level, taps,
@@ -506,39 +557,40 @@
             for k in range(1, orb_count)
         ]
 
-    shares = []
-    for chunk in chunks:
-        own, sent = call(
-            functools.partial(second_halo_kernel, n, chunk),
-            (fields[chunk], narrows[chunk]), [], 10**9,
-            locals_[chunk], *halos[chunk],
-        )
-        shares.append([own] + all_orbs(sent)[1:])
+    near = exchange_sums(partial)
+    held, _ = lax.optimization_barrier((locals_[0], near[2]))
+    share = call(
+        functools.partial(second_halo_kernel, n, 0), narrows[0], [], 10**9,
+        held, *halos[0],
+    )
+    panels = all_orbs(share)
     added = call(functools.partial(atoms_kernel, n), sums, [], 10**6, strength, *near)
     adds = all_orbs(added)
-    panels = [shares[chunk][k] for k in range(orb_count) for chunk in chunks]
-    source = (lax.axis_index("orb") - jnp.arange(orb_count)) % orb_count
-    chosen = (panel_owner[None, :] == source[:, None]).astype(f32)
-    rotation = jnp.sum(
-        chosen[:, :, None, None] * ritz_rotation.astype(f32)[None], axis=1
-    )
     columns = ritz_rotation.shape[2]
-    rotation = rotation.reshape(orb_count * panel, columns).T
-    operands = (rotation, *adds, *panels, table)
+    ritz = ritz_rotation.reshape(-1, columns)
+    smem = pl.BlockSpec(memory_space=pltpu.SMEM)
+    vmem = pl.BlockSpec(memory_space=pltpu.VMEM)
+    plane_of = lambda rows: pl.BlockSpec((rows, PLANE), lambda i: (0, i))
+    params = pltpu.CompilerParams(vmem_limit_bytes=VMEM_LIMIT)
     filtered, rotated = pl.pallas_call(
-        functools.partial(rotate_kernel, n, columns),
+        functools.partial(rotate_own_kernel, n),
         grid=(n.depth,),
-        out_shape=(shape((panel, n.cells), bf16), shape((columns, n.cells), bf16)),
-        in_specs=[pl.BlockSpec(memory_space=pltpu.VMEM)] * len(operands),
-        out_specs=(
-            pl.BlockSpec((panel, PLANE), lambda i: (0, i)),
-            pl.BlockSpec((columns, PLANE), lambda i: (0, i)),
-        ),
-        scratch_shapes=[
-            pltpu.VMEM((columns + panel, 2 * (orb_count * panel + SLOTS)), bf16)
-        ],
-        compiler_params=pltpu.CompilerParams(vmem_limit_bytes=VMEM_LIMIT),
-    )(*operands)
+        out_shape=(shape((panel, n.cells), bf16), shape((columns, n.cells), f32)),
+        in_specs=[smem] + [vmem] * 4,
+        out_specs=(plane_of(panel), vmem),
+        scratch_shapes=[pltpu.VMEM((columns + panel, 2 * (panel + SLOTS)), bf16)],
+        compiler_params=params,
+    )(panel_owner, ritz, adds[0], share, table)
+    rest = orb_count - 1
+    rotated = pl.pallas_call(
+        functools.partial(rotate_rest_kernel, n, rest),
+        grid=(n.depth,),
+        out_shape=shape((columns, n.cells), bf16),
+        in_specs=[smem] + [vmem] * (1 + rest) + [plane_of(panel)] * rest + [vmem] * 2,
+        out_specs=plane_of(columns),
+        scratch_shapes=[pltpu.VMEM((columns, 2 * (rest * panel + SLOTS)), bf16)],
+        compiler_params=params,
+    )(panel_owner, ritz, *adds[1:], *panels[1:], rotated, table)
     return (filtered, rotated)
 
 

time: 74.7 us -> 73.2 us (0.980)
  Pallas kernels: 24.2 us -> 26.8 us
  waiting for transfers between devices: 28.6 us -> 26.7 us
  other arithmetic: 2.92 us -> 1.46 us
  local copies, waits for them, and re-layouts: 1.95 us -> 1.19 us
    ppermute x10, waiting for transfers between devices: 26.3 us -> 20.4 us  [swapped(): return lax.ppermute(block, 'grid', pairs)]
    ppermute x2, waiting for transfers between devices: 2.25 us -> 6.27 us  [all_orbs(): lax.ppermute(block, 'orb', [(i, (i + k) % orb_count) for i in range(orb_c...]
    pallas_call x1 -> x2, Pallas kernels: 4.97 us -> 8.46 us  [the longest x1 4.24 us: body(): pl.pallas_call(functools.partial(rotate_rest_kernel, n, rest), grid=(n.de...]
    pallas_call x7, Pallas kernels: 19.3 us -> 18.3 us  [call(): pl.pallas_call(kernel, out_shape=out_shape, in_specs=[pl.BlockSpec(memory...]
    convert_element_type x2 -> x0, other arithmetic: 0.77 us -> none  [the longest x1 0.7 us: body(): ritz_rotation.astype(f32)[None]]
    reshape x1 -> x0, local copies, waits for them, and re-layouts: 0.77 us -> none  [body(): rotation = rotation.reshape(orb_count * panel, columns).T]
  transfers between devices with their start and end apart: 12 -> 12, of which waited for: 7 -> 6; matrix products, arithmetic and copies ran while one was open for 5% -> 2% of each run, Pallas kernels for 20% -> 26%
where the time goes in v4:
time: 73.2 us; the launch traced here: 72.8 us
  Pallas kernels  26.8 us (37%)
  waiting for transfers between devices  26.7 us (36%)
  starting transfers between devices  16 us (22%)
  other arithmetic  1.46 us (2%)
  local copies, waits for them, and re-layouts  1.19 us (2%)
  between operations  0.75 us (1%)
    ppermute x10, waiting for transfers between devices, swapped(): return lax.ppermute(block, 'grid', pairs)  20.4 us
    pallas_call x7, Pallas kernels, call(): pl.pallas_call(kernel, out_shape=out_shape, in_specs=[pl.BlockSpec(memory...  18.3 us
    ppermute x10, starting transfers between devices, swapped(): return lax.ppermute(block, 'grid', pairs)  14.5 us
    ppermute x2, waiting for transfers between devices, all_orbs(): lax.ppermute(block, 'orb', [(i, (i + k) % orb_count) for i in range(orb_c...  6.27 us
    pallas_call x1, Pallas kernels, body(): pl.pallas_call(functools.partial(rotate_rest_kernel, n, rest), grid=(n.de...  4.24 us
    pallas_call x1, Pallas kernels, body(): pl.pallas_call(functools.partial(rotate_own_kernel, n), grid=(n.depth,),...  4.22 us
    ppermute x2, starting transfers between devices, all_orbs(): lax.ppermute(block, 'orb', [(i, (i + k) % orb_count) for i in range(orb_c...  1.55 us
  transfers between devices with their start and end apart: 12, of which 6 were waited for; matrix products, arithmetic and copies ran while one was open for 2% of the time, Pallas kernels for 26%

profile of v4, /device:TPU:11, one launch (start us, length us, event | category | flops | bytes accessed | tf_op | source)
XLA Modules:
  0.0 72.8 jit_solution(6949808488220848176)
XLA Ops:
  0.6 0.7 %collective-permute-start = (bf16[8,55296]{1,0:T(8,128)(2,1)}, bf16[8,55296]{1,0:T(8,128)(2,1)S(1)}, u32[]{:S(2)}, u32[]{:S(2)}) collective-permute-start(bf16[8,55296]{1,0:T(8,128)(2,1)} %initial.1), channel_id=1, source_target_pairs={{0,2},{2,0},{4,6},{6,4},{8,10},{10,8},{12,14},{14,12},{16,18},{18,... | collective-permute-start | bytes 2654216 | tf_op jit(solution)/shard_map/ppermute | solution.py:467
  1.4 3.1 %collective-permute-start.1 = (bf16[8,55296]{1,0:T(8,128)(2,1)}, bf16[8,55296]{1,0:T(8,128)(2,1)S(1)}, u32[]{:S(2)}, u32[]{:S(2)}) collective-permute-start(bf16[8,55296]{1,0:T(8,128)(2,1)} %initial.1), channel_id=1, source_target_pairs={{2,4},{4,2},{6,8},{8,6},{10,12},{12,10},{14,16},{16,14},{18,20},{2... | collective-permute-start | bytes 2654216 | tf_op jit(solution)/shard_map/ppermute | solution.py:467
  4.4 0.7 %fusion.5 = (f32[12,128]{1,0:T(8,128)S(1)}, f32[12,128]{1,0:T(8,128)S(1)}) fusion(s32[1536]{0:T(1024)} %param.11, s32[1536]{0:T(1024)} %param.12, s32[]{:T(128)S(6)} %mul.19), kind=kLoop, calls=%fused_computation.10 | loop fusion | flops 47616 | bytes 24580 | tf_op jit(solution)/shard_map/reshape | solution.py:519
  5.2 0.7 pad_maximum_fusion.entry_ref
  5.9 0.0 copy-start.1
  5.9 1.2 %copy-done.1 = bf16[8,55296]{1,0:T(8,128)(2,1)S(1)} copy-done((bf16[8,55296]{1,0:T(8,128)(2,1)S(1)}, bf16[8,55296]{1,0:T(8,128)(2,1)}, u32[]{:S(2)}) %copy-start.1) | copy-done | bytes 884760
  7.1 0.0 copy-start
  7.1 0.0 copy-start.2
  7.1 4.6 %shard_map.104 = (bf16[1152,768]{1,0:T(8,128)(2,1)S(1)}, f32[8,128]{1,0:T(8,128)S(1)}, bf16[672,768]{1,0:T(8,128)(2,1)S(1)}) custom-call(bf16[8,55296]{1,0:T(8,128)(2,1)S(1)} %copy-done.1, f32[36,128]{1,0:T(8,128)S(1)} %pad_maximum_fusion.entry_ref), custom_call_target="tpu_custom_call" | custom-call | flops 4000000000 | bytes 903168 | tf_op jit(solution)/shard_map/pallas_call | solution.py:451
  11.7 0.4 collective-permute-start.2
  12.1 0.0 copy-done
  12.1 0.0 copy-done.2
  12.1 0.0 copy-start.4
  12.1 3.1 %shard_map.105.local = f32[8,55296]{1,0:T(8,128)S(1)} custom-call(bf16[8,55296]{1,0:T(8,128)(2,1)S(1)} %copy-done.1, bf16[672,768]{1,0:T(8,128)(2,1)S(1)} %get-tuple-element.14.packed, f32[432,128]{1,0:T(8,128)S(1)} %bitcast.8, bf16[3,768,768]{2,1,0:T(8,128)(2,1)S(1)} %copy-done), custom_call_target="tpu_custom_call" | custom-call | flops 2000000000 | bytes 5677056 | tf_op jit(solution)/shard_map/pallas_call | solution.py:451
  15.2 0.0 collective-permute-done.2.refs_1_
  15.2 3.2 %collective-permute-start.3 = (f32[16,128]{1,0:T(8,128)S(1)}, f32[16,128]{1,0:T(8,128)S(1)}, u32[]{:S(2)}, u32[]{:S(2)}) collective-permute-start(f32[16,128]{1,0:T(8,128)S(1)} %pad_maximum_fusion.1), channel_id=1, source_target_pairs={{2,4},{4,2},{6,8},{8,6},{10,12},{12,10},{14,16},{16,14},{18,20},{2... | collective-permute-start | bytes 24584 | tf_op jit(solution)/shard_map/ppermute | solution.py:467
  18.4 7.2 %collective-permute-done.3.refs_2_ = f32[16,128]{1,0:T(8,128)S(1)} collective-permute-done((f32[16,128]{1,0:T(8,128)S(1)}, f32[16,128]{1,0:T(8,128)S(1)}, u32[]{:S(2)}, u32[]{:S(2)}) %collective-permute-start.3) | collective-permute-done | bytes 8224 | tf_op jit(solution)/shard_map/ppermute | solution.py:467
  25.6 0.0 collective-permute-start.4
  25.6 1.2 %collective-permute-done.4.refs_3_ = f32[16,128]{1,0:T(8,128)S(1)} collective-permute-done((f32[16,128]{1,0:T(8,128)S(1)}, f32[16,128]{1,0:T(8,128)S(1)}, u32[]{:S(2)}, u32[]{:S(2)}) %collective-permute-start.4) | collective-permute-done | bytes 8224 | tf_op jit(solution)/shard_map/ppermute | solution.py:467
  26.8 0.0 collective-permute-done.inner
  26.8 0.0 collective-permute-done.1.outer
  26.8 0.0 copy-done.4
  26.8 2.7 %shard_map.106 = (f32[8,55296]{1,0:T(8,128)S(1)}, bf16[8,55296]{1,0:T(8,128)(2,1)S(1)}) custom-call(f32[8,55296]{1,0:T(8,128)S(1)} %shard_map.105.local, bf16[8,55296]{1,0:T(8,128)(2,1)S(1)} %collective-permute-done.inner, bf16[8,55296]{1,0:T(8,128)(2,1)S(1)} %collective-permute-done.1.outer, bf16[1152,768]{1,0:T(8,128)(2,1)S(1)} %get-tuple-element.15.table.refs_3_, ...), custom_call_target="tpu_custom_call" | custom-call | flops 1000000000 | bytes 5333248 | tf_op jit(solution)/shard_map/pallas_call | solution.py:451
  29.5 0.2 collective-permute-start.8
  29.7 3.1 %collective-permute-start.9 = (bf16[8,55296]{1,0:T(8,128)(2,1)S(1)}, bf16[8,55296]{1,0:T(8,128)(2,1)S(1)}, u32[]{:S(2)}, u32[]{:S(2)}) collective-permute-start(bf16[8,55296]{1,0:T(8,128)(2,1)S(1)} %get-tuple-element.23), channel_id=1, source_target_pairs={{2,4},{4,2},{6,8},{8,6},{10,12},{12,10},{14,16},{16,14},{18,20},{2... | collective-permute-start | bytes 2654216 | tf_op jit(solution)/shard_map/ppermute | solution.py:467
  32.8 1.7 %shard_map.107 = (f32[8,128]{1,0:T(8,128)S(1)}, bf16[672,768]{1,0:T(8,128)(2,1)S(1)}, bf16[672,768]{1,0:T(8,128)(2,1)S(1)}) custom-call(f32[8,55296]{1,0:T(8,128)S(1)} %get-tuple-element.18.field, bf16[1152,768]{1,0:T(8,128)(2,1)S(1)} %get-tuple-element.15.table.refs_3_), custom_call_target="tpu_custom_call" | custom-call | flops 1000000000 | bytes 3538944 | tf_op jit(solution)/shard_map/pallas_call | solution.py:451
  34.5 0.3 collective-permute-start.5
  34.8 1.0 %collective-permute-done.5.refs_1_ = f32[8,128]{1,0:T(8,128)S(1)} collective-permute-done((f32[8,128]{1,0:T(8,128)S(1)}, f32[8,128]{1,0:T(8,128)S(1)}, u32[]{:S(2)}, u32[]{:S(2)}) %collective-permute-start.5) | collective-permute-done | bytes 4128 | tf_op jit(solution)/shard_map/ppermute | solution.py:467
  35.7 3.5 %collective-permute-start.6 = (f32[16,128]{1,0:T(8,128)S(1)}, f32[16,128]{1,0:T(8,128)S(1)}, u32[]{:S(2)}, u32[]{:S(2)}) collective-permute-start(f32[16,128]{1,0:T(8,128)S(1)} %pad_maximum_fusion.2), channel_id=1, source_target_pairs={{2,4},{4,2},{6,8},{8,6},{10,12},{12,10},{14,16},{16,14},{18,20},{2... | collective-permute-start | bytes 24584 | tf_op jit(solution)/shard_map/ppermute | solution.py:467
  39.3 4.8 %shard_map.109.local = f32[8,55296]{1,0:T(8,128)S(1)} custom-call(f32[8,55296]{1,0:T(8,128)S(1)} %get-tuple-element.18.field, bf16[8,55296]{1,0:T(8,128)(2,1)S(1)} %copy-done.1, bf16[672,768]{1,0:T(8,128)(2,1)S(1)} %get-tuple-element.20.packed, bf16[672,768]{1,0:T(8,128)(2,1)S(1)} %get-tuple-element.21.rest, f32[432,128]{1,0:T(8,128)S(1)} %bitcast.9, ...), custom_call_target="tpu_custom_call" | custom-call | flops 3000000000 | bytes 8478720 | tf_op jit(solution)/shard_map/pallas_call | solution.py:451
  44.1 0.0 copy-start.3
  44.1 0.0 copy-start.5
  44.1 9.9 %collective-permute-done.6.refs_2_ = f32[16,128]{1,0:T(8,128)S(1)} collective-permute-done((f32[16,128]{1,0:T(8,128)S(1)}, f32[16,128]{1,0:T(8,128)S(1)}, u32[]{:S(2)}, u32[]{:S(2)}) %collective-permute-start.6) | collective-permute-done | bytes 8224 | tf_op jit(solution)/shard_map/ppermute | solution.py:467
  54.0 0.0 collective-permute-done.8.inner
  54.0 0.0 collective-permute-done.9.outer
  54.0 1.1 %shard_map.110.panel = bf16[8,55296]{1,0:T(8,128)(2,1)S(1)} custom-call(f32[8,55296]{1,0:T(8,128)S(1)} %shard_map.109.local, bf16[8,55296]{1,0:T(8,128)(2,1)S(1)} %collective-permute-done.8.inner, bf16[8,55296]{1,0:T(8,128)(2,1)S(1)} %collective-permute-done.9.outer), custom_call_target="tpu_custom_call" | custom-call | flops 1000000000 | bytes 3538944 | tf_op jit(solution)/shard_map/pallas_call | solution.py:451
  55.1 0.3 collective-permute-start.11
  55.4 0.0 collective-permute-start.7
  55.4 1.2 %collective-permute-done.7.refs_3_ = f32[16,128]{1,0:T(8,128)S(1)} collective-permute-done((f32[16,128]{1,0:T(8,128)S(1)}, f32[16,128]{1,0:T(8,128)S(1)}, u32[]{:S(2)}, u32[]{:S(2)}) %collective-permute-start.7) | collective-permute-done | bytes 8224 | tf_op jit(solution)/shard_map/ppermute | solution.py:467
  56.6 0.3 shard_map.108.added
  56.9 1.2 %collective-permute-start.10 = (f32[8,128]{1,0:T(8,128)S(1)}, f32[8,128]{1,0:T(8,128)S(1)}, u32[]{:S(2)}, u32[]{:S(2)}) collective-permute-start(f32[8,128]{1,0:T(8,128)S(1)} %shard_map.108.added), channel_id=1, source_target_pairs={{0,1},{1,0},{2,3},{3,2},{4,5},{5,4},{6,7},{7,6},{8,9},{9,8},{10,11... | collective-permute-start | bytes 12296 | tf_op jit(solution)/shard_map/ppermute | solution.py:556
  58.1 0.0 copy-done.3
  58.1 0.0 copy-done.5
  58.1 4.2 %shard_map.111 = (bf16[8,55296]{1,0:T(8,128)(2,1)}, f32[16,55296]{1,0:T(8,128)S(1)}) custom-call(s32[4]{0:T(128)S(1)} %copy-done.5, bf16[32,16]{1,0:T(8,128)(2,1)S(1)} %bitcast.10, f32[8,128]{1,0:T(8,128)S(1)} %shard_map.108.added, bf16[8,55296]{1,0:T(8,128)(2,1)S(1)} %shard_map.110.panel, bf16[1152,768]{1,0:T(8,128)(2,1)S(1)} %get-tuple-element.15.table.refs_3_), custom_call_target="tpu_custom_call" | custom-call | tf_op jit(solution)/shard_map/pallas_call | solution.py:575
  62.3 6.3 %collective-permute-done.10.refs_0_ = f32[8,128]{1,0:T(8,128)S(1)} collective-permute-done((f32[8,128]{1,0:T(8,128)S(1)}, f32[8,128]{1,0:T(8,128)S(1)}, u32[]{:S(2)}, u32[]{:S(2)}) %collective-permute-start.10) | collective-permute-done | bytes 4128 | tf_op jit(solution)/shard_map/ppermute | solution.py:556
  68.6 0.0 collective-permute-done.11.refs_1_
  68.6 4.2 %shard_map.112 = bf16[16,55296]{1,0:T(8,128)(2,1)} custom-call(s32[4]{0:T(128)S(1)} %copy-done.5, bf16[32,16]{1,0:T(8,128)(2,1)S(1)} %bitcast.11, f32[8,128]{1,0:T(8,128)S(1)} %collective-permute-done.10.refs_0_, bf16[8,55296]{1,0:T(8,128)(2,1)S(1)} %collective-permute-done.11.refs_1_, f32[16,55296]{1,0:T(8,128)S(1)} %get-tuple-element.25.refs_2_, ...), custom_call_target="tpu_custom_call" | custom-call | tf_op jit(solution)/shard_map/pallas_call | solution.py:585
  (2 shorter events, 0.0 us)
Async XLA Ops:
  0.6 26.1 %collective-permute-start = (bf16[8,55296]{1,0:T(8,128)(2,1)}, bf16[8,55296]{1,0:T(8,128)(2,1)S(1)}, u32[]{:S(2)}, u32[]{:S(2)}) collective-permute-start(bf16[8,55296]{1,0:T(8,128)(2,1)} %initial.1), channel_id=1, source_target_pairs={{0,2},{2,0},{4,6},{6,4},{8,10},{10,8},{12,14},{14,12},{16,18},{18,... | collective-permute-start | bytes 2654216 | tf_op jit(solution)/shard_map/ppermute | solution.py:467
  1.4 25.4 %collective-permute-start.1 = (bf16[8,55296]{1,0:T(8,128)(2,1)}, bf16[8,55296]{1,0:T(8,128)(2,1)S(1)}, u32[]{:S(2)}, u32[]{:S(2)}) collective-permute-start(bf16[8,55296]{1,0:T(8,128)(2,1)} %initial.1), channel_id=1, source_target_pairs={{2,4},{4,2},{6,8},{8,6},{10,12},{12,10},{14,16},{16,14},{18,20},{2... | collective-permute-start | bytes 2654216 | tf_op jit(solution)/shard_map/ppermute | solution.py:467
  5.9 1.2 %copy-start.1 = (bf16[8,55296]{1,0:T(8,128)(2,1)S(1)}, bf16[8,55296]{1,0:T(8,128)(2,1)}, u32[]{:S(2)}) copy-start(bf16[8,55296]{1,0:T(8,128)(2,1)} %initial.1) | copy-start | bytes 2654212
  7.1 5.0 %copy-start = (bf16[3,768,768]{2,1,0:T(8,128)(2,1)S(1)}, bf16[3,768,768]{2,1,0:T(8,128)(2,1)}, u32[]{:S(2)}) copy-start(bf16[3,768,768]{2,1,0:T(8,128)(2,1)} %constant.48.clone.taps) | copy-start | bytes 10616836
  7.1 5.0 %copy-start.2 = (f32[55296]{0:T(1024)S(1)}, f32[55296]{0:T(1024)}, u32[]{:S(2)}) copy-start(f32[55296]{0:T(1024)} %param.10) | copy-start | bytes 663556
  11.7 3.5 %collective-permute-start.2 = (f32[8,128]{1,0:T(8,128)S(1)}, f32[8,128]{1,0:T(8,128)S(1)}, u32[]{:S(2)}, u32[]{:S(2)}) collective-permute-start(f32[8,128]{1,0:T(8,128)S(1)} %get-tuple-element.16.refs_0_), channel_id=1, source_target_pairs={{0,2},{2,0},{4,6},{6,4},{8,10},{10,8},{12,14},{14,12},{16,18},{18,... | collective-permute-start | bytes 12296 | tf_op jit(solution)/shard_map/ppermute | solution.py:467
  12.1 14.7 %copy-start.4 = (f32[64]{0:T(128)S(1)}, f32[64]{0:T(128)}, u32[]{:S(2)}) copy-start(f32[64]{0:T(128)} %param.14) | copy-start | bytes 772
  15.2 10.4 %collective-permute-start.3 = (f32[16,128]{1,0:T(8,128)S(1)}, f32[16,128]{1,0:T(8,128)S(1)}, u32[]{:S(2)}, u32[]{:S(2)}) collective-permute-start(f32[16,128]{1,0:T(8,128)S(1)} %pad_maximum_fusion.1), channel_id=1, source_target_pairs={{2,4},{4,2},{6,8},{8,6},{10,12},{12,10},{14,16},{16,14},{18,20},{2... | collective-permute-start | bytes 24584 | tf_op jit(solution)/shard_map/ppermute | solution.py:467
  25.6 1.2 %collective-permute-start.4 = (f32[16,128]{1,0:T(8,128)S(1)}, f32[16,128]{1,0:T(8,128)S(1)}, u32[]{:S(2)}, u32[]{:S(2)}) collective-permute-start(f32[16,128]{1,0:T(8,128)S(1)} %collective-permute-done.3.refs_2_), channel_id=1, source_target_pairs={{0,2},{2,0},{4,6},{6,4},{8,10},{10,8},{12,14},{14,12},{16,18},{18,... | collective-permute-start | bytes 24584 | tf_op jit(solution)/shard_map/ppermute | solution.py:467
  29.5 24.5 %collective-permute-start.8 = (bf16[8,55296]{1,0:T(8,128)(2,1)S(1)}, bf16[8,55296]{1,0:T(8,128)(2,1)S(1)}, u32[]{:S(2)}, u32[]{:S(2)}) collective-permute-start(bf16[8,55296]{1,0:T(8,128)(2,1)S(1)} %get-tuple-element.23), channel_id=1, source_target_pairs={{0,2},{2,0},{4,6},{6,4},{8,10},{10,8},{12,14},{14,12},{16,18},{18,... | collective-permute-start | bytes 2654216 | tf_op jit(solution)/shard_map/ppermute | solution.py:467
  29.7 24.3 %collective-permute-start.9 = (bf16[8,55296]{1,0:T(8,128)(2,1)S(1)}, bf16[8,55296]{1,0:T(8,128)(2,1)S(1)}, u32[]{:S(2)}, u32[]{:S(2)}) collective-permute-start(bf16[8,55296]{1,0:T(8,128)(2,1)S(1)} %get-tuple-element.23), channel_id=1, source_target_pairs={{2,4},{4,2},{6,8},{8,6},{10,12},{12,10},{14,16},{16,14},{18,20},{2... | collective-permute-start | bytes 2654216 | tf_op jit(solution)/shard_map/ppermute | solution.py:467
  34.5 1.2 %collective-permute-start.5 = (f32[8,128]{1,0:T(8,128)S(1)}, f32[8,128]{1,0:T(8,128)S(1)}, u32[]{:S(2)}, u32[]{:S(2)}) collective-permute-start(f32[8,128]{1,0:T(8,128)S(1)} %get-tuple-element.19.refs_0_), channel_id=1, source_target_pairs={{0,2},{2,0},{4,6},{6,4},{8,10},{10,8},{12,14},{14,12},{16,18},{18,... | collective-permute-start | bytes 12296 | tf_op jit(solution)/shard_map/ppermute | solution.py:467
  35.7 18.2 %collective-permute-start.6 = (f32[16,128]{1,0:T(8,128)S(1)}, f32[16,128]{1,0:T(8,128)S(1)}, u32[]{:S(2)}, u32[]{:S(2)}) collective-permute-start(f32[16,128]{1,0:T(8,128)S(1)} %pad_maximum_fusion.2), channel_id=1, source_target_pairs={{2,4},{4,2},{6,8},{8,6},{10,12},{12,10},{14,16},{16,14},{18,20},{2... | collective-permute-start | bytes 24584 | tf_op jit(solution)/shard_map/ppermute | solution.py:467
  44.1 14.0 %copy-start.3 = (bf16[4,8,16]{2,1,0:T(8,128)(2,1)S(1)}, bf16[4,8,16]{2,1,0:T(8,128)(2,1)}, u32[]{:S(2)}) copy-start(bf16[4,8,16]{2,1,0:T(8,128)(2,1)} %param.15) | copy-start | bytes 3076
  44.1 14.0 %copy-start.5 = (s32[4]{0:T(128)S(1)}, s32[4]{0:T(128)}, u32[]{:S(2)}) copy-start(s32[4]{0:T(128)} %owner.3) | copy-start | bytes 52
  55.1 13.5 %collective-permute-start.11 = (bf16[8,55296]{1,0:T(8,128)(2,1)S(1)}, bf16[8,55296]{1,0:T(8,128)(2,1)S(1)}, u32[]{:S(2)}, u32[]{:S(2)}) collective-permute-start(bf16[8,55296]{1,0:T(8,128)(2,1)S(1)} %shard_map.110.panel), channel_id=1, source_target_pairs={{0,1},{1,0},{2,3},{3,2},{4,5},{5,4},{6,7},{7,6},{8,9},{9,8},{10,11... | collective-permute-start | bytes 2654216 | tf_op jit(solution)/shard_map/ppermute | solution.py:556
  55.4 1.2 %collective-permute-start.7 = (f32[16,128]{1,0:T(8,128)S(1)}, f32[16,128]{1,0:T(8,128)S(1)}, u32[]{:S(2)}, u32[]{:S(2)}) collective-permute-start(f32[16,128]{1,0:T(8,128)S(1)} %collective-permute-done.6.refs_2_), channel_id=1, source_target_pairs={{0,2},{2,0},{4,6},{6,4},{8,10},{10,8},{12,14},{14,12},{16,18},{18,... | collective-permute-start | bytes 24584 | tf_op jit(solution)/shard_map/ppermute | solution.py:467
  56.9 11.7 %collective-permute-start.10 = (f32[8,128]{1,0:T(8,128)S(1)}, f32[8,128]{1,0:T(8,128)S(1)}, u32[]{:S(2)}, u32[]{:S(2)}) collective-permute-start(f32[8,128]{1,0:T(8,128)S(1)} %shard_map.108.added), channel_id=1, source_target_pairs={{0,1},{1,0},{2,3},{3,2},{4,5},{5,4},{6,7},{7,6},{8,9},{9,8},{10,11... | collective-permute-start | bytes 12296 | tf_op jit(solution)/shard_map/ppermute | solution.py:556

commit v5 on v4

--- a/solution.py
+++ b/solution.py
@@ -106,7 +106,7 @@
             one(block)
             return carry
 
-        lax.fori_loop(*CHUNKS[chunk], step, None)
+        lax.fori_loop(*CHUNKS[chunk], step, None, unroll=2)
 
 
 def pack_planes(n, source, targets):
@@ -159,14 +159,12 @@
     folded = total[0 : n.panel, :]
     for plane in range(1, n.depth):
         folded = folded + total[plane * n.panel : (plane + 1) * n.panel, :]
-    slot = lax.broadcasted_iota(jnp.int32, (n.atoms, LANES), 0) % SLOTS
-    lane = lax.broadcasted_iota(jnp.int32, (n.atoms, LANES), 1)
-    out[...] = jnp.dot(
-        folded,
-        (slot == lane).astype(jnp.float32),
-        precision=lax.Precision.HIGHEST,
-        preferred_element_type=jnp.float32,
-    )
+    wide = jnp.concatenate([folded, jnp.zeros((n.panel, LANES - n.atoms), jnp.float32)], axis=1)
+    total = wide
+    for plane in range(1, n.depth):
+        total = total + pltpu.roll(wide, LANES - plane * SLOTS, 1)
+    lane = lax.broadcasted_iota(jnp.int32, total.shape, 1)
+    out[...] = jnp.where(lane < SLOTS, total, 0.0)
 
 
 def near_sums(n, tables, strength):
@@ -183,24 +181,20 @@
     ):
         total = total + pltpu.roll(table, (offset * ATOM_DEV + LANES) % LANES, 1)
     count = strength.shape[1]
-    atom = lax.broadcasted_iota(jnp.int32, (count, LANES), 0)
-    slot = lax.broadcasted_iota(jnp.int32, (count, LANES), 1) + (slab - 1) * ATOM_DEV
-    near = jnp.dot(
-        jnp.broadcast_to(strength[...], (n.panel, count)),
-        (atom == slot).astype(jnp.float32),
-        precision=lax.Precision.HIGHEST,
-        preferred_element_type=jnp.float32,
-    )
+    near = strength[...]
+    if count < LANES:
+        near = jnp.concatenate([near, jnp.zeros((1, LANES - count), jnp.float32)], axis=1)
+    near = jnp.broadcast_to(near, total.shape)
+    near = pltpu.roll(near, (ATOM_DEV - slab * ATOM_DEV + LANES) % LANES, 1)
     lane = lax.broadcasted_iota(jnp.int32, total.shape, 1)
-    total = jnp.where(lane < 3 * ATOM_DEV, total * near, 0.0)
-    slot = lax.broadcasted_iota(jnp.int32, (LANES, n.atoms), 1) % SLOTS
-    lane = lax.broadcasted_iota(jnp.int32, (LANES, n.atoms), 0)
-    return jnp.dot(
-        total,
-        (slot == lane).astype(jnp.float32),
-        precision=lax.Precision.HIGHEST,
-        preferred_element_type=jnp.float32,
-    )
+    return jnp.where(lane < 3 * ATOM_DEV, total * near, 0.0)
+
+
+def on_planes(n, sums):
+    wide = sums
+    for plane in range(1, n.depth):
+        wide = wide + pltpu.roll(sums, plane * SLOTS, 1)
+    return wide[:, 0 : n.atoms]
 
 
 def by_side(inner, outer, run):
@@ -283,7 +277,7 @@
 
 def first_halo_kernel(n, local, inner, outer, table, strength, *refs):
     tables, out, sents = refs[:4], refs[4], refs[5:]
-    wide = near_sums(n, tables, strength)
+    wide = on_planes(n, near_sums(n, tables, strength))
     rows = jnp.where(
         block_diagonal(n.depth, n.panel, SLOTS), jnp.concatenate([wide] * n.depth, axis=0), 0.0
     )
@@ -349,13 +343,10 @@
 
 def atoms_kernel(n, strength, *refs):
     *tables, out = refs
-    wide = near_sums(n, tables, strength) * (2.0 / cheb_half)
-    out[...] = jnp.concatenate(
-        [wide[:, 0:SLOTS], jnp.zeros((n.panel, LANES - SLOTS), jnp.float32)], axis=1
-    )
-
-
-def weighted_rows(n, shifts, owner, ritz, added):
+    out[...] = near_sums(n, tables, strength) * (2.0 / cheb_half)
+
+
+def rotation_rows(n, shifts, owner, ritz):
     columns = ritz.shape[1]
     blocks = []
     for shift in shifts:
@@ -370,13 +361,16 @@
     eye = lax.broadcasted_iota(jnp.int32, (columns, columns), 0) == lax.broadcasted_iota(
         jnp.int32, (columns, columns), 1
     )
-    rotation = lax.dot_general(
+    return lax.dot_general(
         eye.astype(jnp.float32),
         weights,
         (((1,), (1,)), ((), ())),
         precision=lax.Precision.HIGHEST,
         preferred_element_type=jnp.float32,
     )
+
+
+def with_slots(rotation, added):
     both = jnp.dot(
         rotation,
         added[:, 0:SLOTS],
@@ -395,12 +389,16 @@
     return parts[0], stack
 
 
-def rotate_own_kernel(n, owner, ritz, added, panel, table, filtered, rotated, rows_ref):
+def rotate_own_kernel(
+    n, orbs, owner, ritz, added, panel, table, filtered, rotated, rest, rows_ref
+):
     columns = ritz.shape[1]
 
     @pl.when(pl.program_id(0) == 0)
     def _():
-        top = weighted_rows(n, (0,), owner, ritz, added[...])
+        rotation = rotation_rows(n, range(orbs), owner, ritz)
+        rest[...] = rotation[:, n.panel :]
+        top = with_slots(rotation[:, 0 : n.panel], added[...])
         bottom = jnp.concatenate(
             [jnp.zeros((n.panel, n.panel), jnp.float32), added[:, 0:SLOTS]], axis=1
         )
@@ -420,15 +418,14 @@
         rotated[:, pl.ds(n.start(plane, block), BLOCK)] = both[0:columns, :]
 
 
-def rotate_rest_kernel(n, count, owner, ritz, *refs):
+def rotate_rest_kernel(n, count, rotation, *refs):
     *refs, own, table, rotated, rows_ref = refs
     adds, panels = refs[:count], refs[count:]
 
     @pl.when(pl.program_id(0) == 0)
     def _():
         added = jnp.concatenate([add[...] for add in adds], axis=0)
-        rows = weighted_rows(n, range(1, count + 1), owner, ritz, added)
-        rows_ref[...] = jnp.concatenate(split(rows), axis=1)
+        rows_ref[...] = jnp.concatenate(split(with_slots(rotation[...], added)), axis=1)
 
     plane = pl.program_id(0)
     matrix = rows_ref[...]
@@ -510,7 +507,8 @@
     packed_shape = shape(((n.blocks + 2) * n.stride, BLOCK), bf16)
     tap_sums = pltpu.VMEM((n.blocks * n.stride, BLOCK), f32)
 
-    inner, outer = swapped(orbitals, core_partner), swapped(orbitals, outer_partner)
+    outer = swapped(orbitals, outer_partner)
+    inner = swapped(orbitals, core_partner)
     plane, inside = projector_cell // PLANE, projector_cell % PLANE
     slot = projector_atom - (lax.axis_index("grid") - 1) * ATOM_DEV
     row_at = ((inside // BLOCK) * n.depth + plane) * SLOTS + slot
@@ -538,7 +536,8 @@
         [field] + narrows, [], 10**9,
         local, inner, outer, table, strength, *near,
     )
-    halos = [(swapped(sent, core_partner), swapped(sent, outer_partner)) for sent in sents]
+    outers = [swapped(sent, outer_partner) for sent in sents]
+    halos = [(swapped(sent, core_partner), outer) for sent, outer in zip(sents, outers)]
     partial, packed, rest = call(
         functools.partial(second_sums_kernel, n),
         (sums, packed_shape, packed_shape), [], 10**9,
@@ -572,25 +571,29 @@
     vmem = pl.BlockSpec(memory_space=pltpu.VMEM)
     plane_of = lambda rows: pl.BlockSpec((rows, PLANE), lambda i: (0, i))
     params = pltpu.CompilerParams(vmem_limit_bytes=VMEM_LIMIT)
-    filtered, rotated = pl.pallas_call(
-        functools.partial(rotate_own_kernel, n),
+    rest = orb_count - 1
+    filtered, rotated, rotation = pl.pallas_call(
+        functools.partial(rotate_own_kernel, n, orb_count),
         grid=(n.depth,),
-        out_shape=(shape((panel, n.cells), bf16), shape((columns, n.cells), f32)),
+        out_shape=(
+            shape((panel, n.cells), bf16),
+            shape((columns, n.cells), f32),
+            shape((columns, rest * panel), f32),
+        ),
         in_specs=[smem] + [vmem] * 4,
-        out_specs=(plane_of(panel), vmem),
+        out_specs=(plane_of(panel), vmem, vmem),
         scratch_shapes=[pltpu.VMEM((columns + panel, 2 * (panel + SLOTS)), bf16)],
         compiler_params=params,
     )(panel_owner, ritz, adds[0], share, table)
-    rest = orb_count - 1
     rotated = pl.pallas_call(
         functools.partial(rotate_rest_kernel, n, rest),
         grid=(n.depth,),
         out_shape=shape((columns, n.cells), bf16),
-        in_specs=[smem] + [vmem] * (1 + rest) + [plane_of(panel)] * rest + [vmem] * 2,
+        in_specs=[vmem] * (1 + rest) + [plane_of(panel)] * rest + [vmem] * 2,
         out_specs=plane_of(columns),
         scratch_shapes=[pltpu.VMEM((columns, 2 * (rest * panel + SLOTS)), bf16)],
         compiler_params=params,
-    )(panel_owner, ritz, *adds[1:], *panels[1:], rotated, table)
+    )(rotation, *adds[1:], *panels[1:], rotated, table)
     return (filtered, rotated)
 
 

time: 73.2 us -> 71.7 us (0.980)
  Pallas kernels: 26.8 us -> 24.9 us
    pallas_call x7, Pallas kernels: 18.3 us -> 17.2 us  [call(): pl.pallas_call(kernel, out_shape=out_shape, in_specs=[pl.BlockSpec(memory...]
    pallas_call x1, Pallas kernels: 4.24 us -> 3.48 us  [body(): pl.pallas_call(functools.partial(rotate_rest_kernel, n, rest), grid=(n.de...]
where the time goes in v5:
time: 71.7 us; the launch traced here: 71.4 us
  waiting for transfers between devices  27.2 us (38%)
  Pallas kernels  24.9 us (35%)
  starting transfers between devices  15.9 us (22%)
  other arithmetic  1.46 us (2%)
  local copies, waits for them, and re-layouts  1.19 us (2%)
  between operations  0.75 us (1%)
    ppermute x10, waiting for transfers between devices, swapped(): return lax.ppermute(block, 'grid', pairs)  20.7 us
    pallas_call x7, Pallas kernels, call(): pl.pallas_call(kernel, out_shape=out_shape, in_specs=[pl.BlockSpec(memory...  17.2 us
    ppermute x10, starting transfers between devices, swapped(): return lax.ppermute(block, 'grid', pairs)  14.4 us
    ppermute x2, waiting for transfers between devices, all_orbs(): lax.ppermute(block, 'orb', [(i, (i + k) % orb_count) for i in range(orb_c...  6.45 us
    pallas_call x1, Pallas kernels, body(): pl.pallas_call(functools.partial(rotate_own_kernel, n, orb_count), grid=(...  4.22 us
    pallas_call x1, Pallas kernels, body(): pl.pallas_call(functools.partial(rotate_rest_kernel, n, rest), grid=(n.de...  3.48 us
    ppermute x2, starting transfers between devices, all_orbs(): lax.ppermute(block, 'orb', [(i, (i + k) % orb_count) for i in range(orb_c...  1.53 us
  transfers between devices with their start and end apart: 12, of which 6 were waited for; matrix products, arithmetic and copies ran while one was open for 2% of the time, Pallas kernels for 26%

profile of v5, /device:TPU:11, one launch (start us, length us, event | category | flops | bytes accessed | tf_op | source)
XLA Modules:
  0.0 71.4 jit_solution(12546040347073113258)
XLA Ops:
  0.6 0.7 %collective-permute-start = (bf16[8,55296]{1,0:T(8,128)(2,1)}, bf16[8,55296]{1,0:T(8,128)(2,1)S(1)}, u32[]{:S(2)}, u32[]{:S(2)}) collective-permute-start(bf16[8,55296]{1,0:T(8,128)(2,1)} %initial.1), channel_id=1, source_target_pairs={{0,2},{2,0},{4,6},{6,4},{8,10},{10,8},{12,14},{14,12},{16,18},{18,... | collective-permute-start | bytes 2654216 | tf_op jit(solution)/shard_map/ppermute | solution.py:464
  1.4 3.1 %collective-permute-start.1 = (bf16[8,55296]{1,0:T(8,128)(2,1)}, bf16[8,55296]{1,0:T(8,128)(2,1)S(1)}, u32[]{:S(2)}, u32[]{:S(2)}) collective-permute-start(bf16[8,55296]{1,0:T(8,128)(2,1)} %initial.1), channel_id=1, source_target_pairs={{2,4},{4,2},{6,8},{8,6},{10,12},{12,10},{14,16},{16,14},{18,20},{2... | collective-permute-start | bytes 2654216 | tf_op jit(solution)/shard_map/ppermute | solution.py:464
  4.4 0.7 %fusion.5 = (f32[12,128]{1,0:T(8,128)S(1)}, f32[12,128]{1,0:T(8,128)S(1)}) fusion(s32[1536]{0:T(1024)} %param.11, s32[1536]{0:T(1024)} %param.12, s32[]{:T(128)S(6)} %mul.19), kind=kLoop, calls=%fused_computation.10 | loop fusion | flops 47616 | bytes 24580 | tf_op jit(solution)/shard_map/reshape | solution.py:517
  5.2 0.7 pad_maximum_fusion.entry_ref
  5.9 0.0 copy-start.1
  5.9 1.2 %copy-done.1 = bf16[8,55296]{1,0:T(8,128)(2,1)S(1)} copy-done((bf16[8,55296]{1,0:T(8,128)(2,1)S(1)}, bf16[8,55296]{1,0:T(8,128)(2,1)}, u32[]{:S(2)}) %copy-start.1) | copy-done | bytes 884760
  7.1 0.0 copy-start
  7.1 0.0 copy-start.2
  7.1 4.5 %shard_map.104 = (bf16[1152,768]{1,0:T(8,128)(2,1)S(1)}, f32[8,128]{1,0:T(8,128)S(1)}, bf16[672,768]{1,0:T(8,128)(2,1)S(1)}) custom-call(bf16[8,55296]{1,0:T(8,128)(2,1)S(1)} %copy-done.1, f32[36,128]{1,0:T(8,128)S(1)} %pad_maximum_fusion.entry_ref), custom_call_target="tpu_custom_call" | custom-call | flops 4000000000 | bytes 903168 | tf_op jit(solution)/shard_map/pallas_call | solution.py:448
  11.6 0.4 collective-permute-start.2
  12.0 0.0 copy-done
  12.0 0.0 copy-done.2
  12.0 0.0 copy-start.4
  12.0 3.0 %shard_map.105.local = f32[8,55296]{1,0:T(8,128)S(1)} custom-call(bf16[8,55296]{1,0:T(8,128)(2,1)S(1)} %copy-done.1, bf16[672,768]{1,0:T(8,128)(2,1)S(1)} %get-tuple-element.15.packed, f32[432,128]{1,0:T(8,128)S(1)} %bitcast.8, bf16[3,768,768]{2,1,0:T(8,128)(2,1)S(1)} %copy-done), custom_call_target="tpu_custom_call" | custom-call | flops 2000000000 | bytes 5677056 | tf_op jit(solution)/shard_map/pallas_call | solution.py:448
  15.0 0.0 collective-permute-done.2.refs_1_
  15.1 3.2 %collective-permute-start.3 = (f32[16,128]{1,0:T(8,128)S(1)}, f32[16,128]{1,0:T(8,128)S(1)}, u32[]{:S(2)}, u32[]{:S(2)}) collective-permute-start(f32[16,128]{1,0:T(8,128)S(1)} %pad_maximum_fusion.1), channel_id=1, source_target_pairs={{2,4},{4,2},{6,8},{8,6},{10,12},{12,10},{14,16},{16,14},{18,20},{2... | collective-permute-start | bytes 24584 | tf_op jit(solution)/shard_map/ppermute | solution.py:464
  18.2 7.4 %collective-permute-done.3.refs_2_ = f32[16,128]{1,0:T(8,128)S(1)} collective-permute-done((f32[16,128]{1,0:T(8,128)S(1)}, f32[16,128]{1,0:T(8,128)S(1)}, u32[]{:S(2)}, u32[]{:S(2)}) %collective-permute-start.3) | collective-permute-done | bytes 8224 | tf_op jit(solution)/shard_map/ppermute | solution.py:464
  25.6 0.0 collective-permute-start.4
  25.6 1.2 %collective-permute-done.4.refs_3_ = f32[16,128]{1,0:T(8,128)S(1)} collective-permute-done((f32[16,128]{1,0:T(8,128)S(1)}, f32[16,128]{1,0:T(8,128)S(1)}, u32[]{:S(2)}, u32[]{:S(2)}) %collective-permute-start.4) | collective-permute-done | bytes 8224 | tf_op jit(solution)/shard_map/ppermute | solution.py:464
  26.8 0.0 collective-permute-done.inner
  26.8 0.0 collective-permute-done.1.outer
  26.8 0.0 copy-done.4
  26.8 2.0 %shard_map.106 = (f32[8,55296]{1,0:T(8,128)S(1)}, bf16[8,55296]{1,0:T(8,128)(2,1)S(1)}) custom-call(f32[8,55296]{1,0:T(8,128)S(1)} %shard_map.105.local, bf16[8,55296]{1,0:T(8,128)(2,1)S(1)} %collective-permute-done.inner, bf16[8,55296]{1,0:T(8,128)(2,1)S(1)} %collective-permute-done.1.outer, bf16[1152,768]{1,0:T(8,128)(2,1)S(1)} %get-tuple-element.16.table.refs_3_, ...), custom_call_target="tpu_custom_call" | custom-call | flops 1000000000 | bytes 5333248 | tf_op jit(solution)/shard_map/pallas_call | solution.py:448
  28.8 0.2 collective-permute-start.8
  29.1 3.0 %collective-permute-start.9 = (bf16[8,55296]{1,0:T(8,128)(2,1)S(1)}, bf16[8,55296]{1,0:T(8,128)(2,1)S(1)}, u32[]{:S(2)}, u32[]{:S(2)}) collective-permute-start(bf16[8,55296]{1,0:T(8,128)(2,1)S(1)} %get-tuple-element.24), channel_id=1, source_target_pairs={{2,4},{4,2},{6,8},{8,6},{10,12},{12,10},{14,16},{16,14},{18,20},{2... | collective-permute-start | bytes 2654216 | tf_op jit(solution)/shard_map/ppermute | solution.py:464
  32.1 1.7 %shard_map.107 = (f32[8,128]{1,0:T(8,128)S(1)}, bf16[672,768]{1,0:T(8,128)(2,1)S(1)}, bf16[672,768]{1,0:T(8,128)(2,1)S(1)}) custom-call(f32[8,55296]{1,0:T(8,128)S(1)} %get-tuple-element.19.field, bf16[1152,768]{1,0:T(8,128)(2,1)S(1)} %get-tuple-element.16.table.refs_3_), custom_call_target="tpu_custom_call" | custom-call | flops 1000000000 | bytes 3538944 | tf_op jit(solution)/shard_map/pallas_call | solution.py:448
  33.8 0.3 collective-permute-start.5
  34.0 0.9 %collective-permute-done.5.refs_1_ = f32[8,128]{1,0:T(8,128)S(1)} collective-permute-done((f32[8,128]{1,0:T(8,128)S(1)}, f32[8,128]{1,0:T(8,128)S(1)}, u32[]{:S(2)}, u32[]{:S(2)}) %collective-permute-start.5) | collective-permute-done | bytes 4128 | tf_op jit(solution)/shard_map/ppermute | solution.py:464
  35.0 3.5 %collective-permute-start.6 = (f32[16,128]{1,0:T(8,128)S(1)}, f32[16,128]{1,0:T(8,128)S(1)}, u32[]{:S(2)}, u32[]{:S(2)}) collective-permute-start(f32[16,128]{1,0:T(8,128)S(1)} %pad_maximum_fusion.2), channel_id=1, source_target_pairs={{2,4},{4,2},{6,8},{8,6},{10,12},{12,10},{14,16},{16,14},{18,20},{2... | collective-permute-start | bytes 24584 | tf_op jit(solution)/shard_map/ppermute | solution.py:464
  38.5 4.7 %shard_map.109.local = f32[8,55296]{1,0:T(8,128)S(1)} custom-call(f32[8,55296]{1,0:T(8,128)S(1)} %get-tuple-element.19.field, bf16[8,55296]{1,0:T(8,128)(2,1)S(1)} %copy-done.1, bf16[672,768]{1,0:T(8,128)(2,1)S(1)} %get-tuple-element.21.packed, bf16[672,768]{1,0:T(8,128)(2,1)S(1)} %get-tuple-element.22.rest, f32[432,128]{1,0:T(8,128)S(1)} %bitcast.9, ...), custom_call_target="tpu_custom_call" | custom-call | flops 3000000000 | bytes 8478720 | tf_op jit(solution)/shard_map/pallas_call | solution.py:448
  43.2 0.0 copy-start.3
  43.2 0.0 copy-start.5
  43.3 10.1 %collective-permute-done.6.refs_2_ = f32[16,128]{1,0:T(8,128)S(1)} collective-permute-done((f32[16,128]{1,0:T(8,128)S(1)}, f32[16,128]{1,0:T(8,128)S(1)}, u32[]{:S(2)}, u32[]{:S(2)}) %collective-permute-start.6) | collective-permute-done | bytes 8224 | tf_op jit(solution)/shard_map/ppermute | solution.py:464
  53.4 0.0 collective-permute-done.8.inner
  53.4 0.0 collective-permute-done.9.outer
  53.4 1.0 %shard_map.110.panel = bf16[8,55296]{1,0:T(8,128)(2,1)S(1)} custom-call(f32[8,55296]{1,0:T(8,128)S(1)} %shard_map.109.local, bf16[8,55296]{1,0:T(8,128)(2,1)S(1)} %collective-permute-done.8.inner, bf16[8,55296]{1,0:T(8,128)(2,1)S(1)} %collective-permute-done.9.outer), custom_call_target="tpu_custom_call" | custom-call | flops 1000000000 | bytes 3538944 | tf_op jit(solution)/shard_map/pallas_call | solution.py:448
  54.4 0.3 collective-permute-start.11
  54.7 0.0 collective-permute-start.7
  54.7 1.2 %collective-permute-done.7.refs_3_ = f32[16,128]{1,0:T(8,128)S(1)} collective-permute-done((f32[16,128]{1,0:T(8,128)S(1)}, f32[16,128]{1,0:T(8,128)S(1)}, u32[]{:S(2)}, u32[]{:S(2)}) %collective-permute-start.7) | collective-permute-done | bytes 8224 | tf_op jit(solution)/shard_map/ppermute | solution.py:464
  55.9 0.1 shard_map.108.added
  56.0 1.2 %collective-permute-start.10 = (f32[8,128]{1,0:T(8,128)S(1)}, f32[8,128]{1,0:T(8,128)S(1)}, u32[]{:S(2)}, u32[]{:S(2)}) collective-permute-start(f32[8,128]{1,0:T(8,128)S(1)} %shard_map.108.added), channel_id=1, source_target_pairs={{0,1},{1,0},{2,3},{3,2},{4,5},{5,4},{6,7},{7,6},{8,9},{9,8},{10,11... | collective-permute-start | bytes 12296 | tf_op jit(solution)/shard_map/ppermute | solution.py:555
  57.2 0.0 copy-done.3
  57.2 0.0 copy-done.5
  57.2 4.2 %shard_map.111 = (bf16[8,55296]{1,0:T(8,128)(2,1)}, f32[16,55296]{1,0:T(8,128)S(1)}, f32[16,8]{1,0:T(8,128)S(1)}) custom-call(s32[4]{0:T(128)S(1)} %copy-done.5, bf16[32,16]{1,0:T(8,128)(2,1)S(1)} %bitcast.10, f32[8,128]{1,0:T(8,128)S(1)} %shard_map.108.added, bf16[8,55296]{1,0:T(8,128)(2,1)S(1)} %shard_map.110.panel, ...), custom_call_target="tpu_custom_call" | custom-call | tf_op jit(solution)/shard_map/pallas_call | solution.py:575
  61.4 6.5 %collective-permute-done.10.refs_0_ = f32[8,128]{1,0:T(8,128)S(1)} collective-permute-done((f32[8,128]{1,0:T(8,128)S(1)}, f32[8,128]{1,0:T(8,128)S(1)}, u32[]{:S(2)}, u32[]{:S(2)}) %collective-permute-start.10) | collective-permute-done | bytes 4128 | tf_op jit(solution)/shard_map/ppermute | solution.py:555
  67.9 0.0 collective-permute-done.11.refs_1_
  67.9 3.5 %shard_map.112 = bf16[16,55296]{1,0:T(8,128)(2,1)} custom-call(f32[16,8]{1,0:T(8,128)S(1)} %get-tuple-element.26.rotation, f32[8,128]{1,0:T(8,128)S(1)} %collective-permute-done.10.refs_0_, bf16[8,55296]{1,0:T(8,128)(2,1)S(1)} %collective-permute-done.11.refs_1_, f32[16,55296]{1,0:T(8,128)S(1)} %get-tuple-element.27.refs_2_, ...), custom_call_target="tpu_custom_call" | custom-call | tf_op jit(solution)/shard_map/pallas_call | solution.py:588
  (2 shorter events, 0.0 us)
Async XLA Ops:
  0.6 26.1 %collective-permute-start = (bf16[8,55296]{1,0:T(8,128)(2,1)}, bf16[8,55296]{1,0:T(8,128)(2,1)S(1)}, u32[]{:S(2)}, u32[]{:S(2)}) collective-permute-start(bf16[8,55296]{1,0:T(8,128)(2,1)} %initial.1), channel_id=1, source_target_pairs={{0,2},{2,0},{4,6},{6,4},{8,10},{10,8},{12,14},{14,12},{16,18},{18,... | collective-permute-start | bytes 2654216 | tf_op jit(solution)/shard_map/ppermute | solution.py:464
  1.4 25.4 %collective-permute-start.1 = (bf16[8,55296]{1,0:T(8,128)(2,1)}, bf16[8,55296]{1,0:T(8,128)(2,1)S(1)}, u32[]{:S(2)}, u32[]{:S(2)}) collective-permute-start(bf16[8,55296]{1,0:T(8,128)(2,1)} %initial.1), channel_id=1, source_target_pairs={{2,4},{4,2},{6,8},{8,6},{10,12},{12,10},{14,16},{16,14},{18,20},{2... | collective-permute-start | bytes 2654216 | tf_op jit(solution)/shard_map/ppermute | solution.py:464
  5.9 1.2 %copy-start.1 = (bf16[8,55296]{1,0:T(8,128)(2,1)S(1)}, bf16[8,55296]{1,0:T(8,128)(2,1)}, u32[]{:S(2)}) copy-start(bf16[8,55296]{1,0:T(8,128)(2,1)} %initial.1) | copy-start | bytes 2654212
  7.1 4.9 %copy-start = (bf16[3,768,768]{2,1,0:T(8,128)(2,1)S(1)}, bf16[3,768,768]{2,1,0:T(8,128)(2,1)}, u32[]{:S(2)}) copy-start(bf16[3,768,768]{2,1,0:T(8,128)(2,1)} %constant.48.clone.taps) | copy-start | bytes 10616836
  7.1 4.9 %copy-start.2 = (f32[55296]{0:T(1024)S(1)}, f32[55296]{0:T(1024)}, u32[]{:S(2)}) copy-start(f32[55296]{0:T(1024)} %param.10) | copy-start | bytes 663556
  11.6 3.4 %collective-permute-start.2 = (f32[8,128]{1,0:T(8,128)S(1)}, f32[8,128]{1,0:T(8,128)S(1)}, u32[]{:S(2)}, u32[]{:S(2)}) collective-permute-start(f32[8,128]{1,0:T(8,128)S(1)} %get-tuple-element.17.refs_0_), channel_id=1, source_target_pairs={{0,2},{2,0},{4,6},{6,4},{8,10},{10,8},{12,14},{14,12},{16,18},{18,... | collective-permute-start | bytes 12296 | tf_op jit(solution)/shard_map/ppermute | solution.py:464
  12.0 14.8 %copy-start.4 = (f32[64]{0:T(128)S(1)}, f32[64]{0:T(128)}, u32[]{:S(2)}) copy-start(f32[64]{0:T(128)} %param.14) | copy-start | bytes 772
  15.1 10.5 %collective-permute-start.3 = (f32[16,128]{1,0:T(8,128)S(1)}, f32[16,128]{1,0:T(8,128)S(1)}, u32[]{:S(2)}, u32[]{:S(2)}) collective-permute-start(f32[16,128]{1,0:T(8,128)S(1)} %pad_maximum_fusion.1), channel_id=1, source_target_pairs={{2,4},{4,2},{6,8},{8,6},{10,12},{12,10},{14,16},{16,14},{18,20},{2... | collective-permute-start | bytes 24584 | tf_op jit(solution)/shard_map/ppermute | solution.py:464
  25.6 1.2 %collective-permute-start.4 = (f32[16,128]{1,0:T(8,128)S(1)}, f32[16,128]{1,0:T(8,128)S(1)}, u32[]{:S(2)}, u32[]{:S(2)}) collective-permute-start(f32[16,128]{1,0:T(8,128)S(1)} %collective-permute-done.3.refs_2_), channel_id=1, source_target_pairs={{0,2},{2,0},{4,6},{6,4},{8,10},{10,8},{12,14},{14,12},{16,18},{18,... | collective-permute-start | bytes 24584 | tf_op jit(solution)/shard_map/ppermute | solution.py:464
  28.8 24.5 %collective-permute-start.8 = (bf16[8,55296]{1,0:T(8,128)(2,1)S(1)}, bf16[8,55296]{1,0:T(8,128)(2,1)S(1)}, u32[]{:S(2)}, u32[]{:S(2)}) collective-permute-start(bf16[8,55296]{1,0:T(8,128)(2,1)S(1)} %get-tuple-element.24), channel_id=1, source_target_pairs={{0,2},{2,0},{4,6},{6,4},{8,10},{10,8},{12,14},{14,12},{16,18},{18,... | collective-permute-start | bytes 2654216 | tf_op jit(solution)/shard_map/ppermute | solution.py:464
  29.1 24.3 %collective-permute-start.9 = (bf16[8,55296]{1,0:T(8,128)(2,1)S(1)}, bf16[8,55296]{1,0:T(8,128)(2,1)S(1)}, u32[]{:S(2)}, u32[]{:S(2)}) collective-permute-start(bf16[8,55296]{1,0:T(8,128)(2,1)S(1)} %get-tuple-element.24), channel_id=1, source_target_pairs={{2,4},{4,2},{6,8},{8,6},{10,12},{12,10},{14,16},{16,14},{18,20},{2... | collective-permute-start | bytes 2654216 | tf_op jit(solution)/shard_map/ppermute | solution.py:464
  33.8 1.2 %collective-permute-start.5 = (f32[8,128]{1,0:T(8,128)S(1)}, f32[8,128]{1,0:T(8,128)S(1)}, u32[]{:S(2)}, u32[]{:S(2)}) collective-permute-start(f32[8,128]{1,0:T(8,128)S(1)} %get-tuple-element.20.refs_0_), channel_id=1, source_target_pairs={{0,2},{2,0},{4,6},{6,4},{8,10},{10,8},{12,14},{14,12},{16,18},{18,... | collective-permute-start | bytes 12296 | tf_op jit(solution)/shard_map/ppermute | solution.py:464
  35.0 18.4 %collective-permute-start.6 = (f32[16,128]{1,0:T(8,128)S(1)}, f32[16,128]{1,0:T(8,128)S(1)}, u32[]{:S(2)}, u32[]{:S(2)}) collective-permute-start(f32[16,128]{1,0:T(8,128)S(1)} %pad_maximum_fusion.2), channel_id=1, source_target_pairs={{2,4},{4,2},{6,8},{8,6},{10,12},{12,10},{14,16},{16,14},{18,20},{2... | collective-permute-start | bytes 24584 | tf_op jit(solution)/shard_map/ppermute | solution.py:464
  43.2 14.0 %copy-start.3 = (bf16[4,8,16]{2,1,0:T(8,128)(2,1)S(1)}, bf16[4,8,16]{2,1,0:T(8,128)(2,1)}, u32[]{:S(2)}) copy-start(bf16[4,8,16]{2,1,0:T(8,128)(2,1)} %param.15) | copy-start | bytes 3076
  43.2 14.0 %copy-start.5 = (s32[4]{0:T(128)S(1)}, s32[4]{0:T(128)}, u32[]{:S(2)}) copy-start(s32[4]{0:T(128)} %owner.1) | copy-start | bytes 52
  54.4 13.5 %collective-permute-start.11 = (bf16[8,55296]{1,0:T(8,128)(2,1)S(1)}, bf16[8,55296]{1,0:T(8,128)(2,1)S(1)}, u32[]{:S(2)}, u32[]{:S(2)}) collective-permute-start(bf16[8,55296]{1,0:T(8,128)(2,1)S(1)} %shard_map.110.panel), channel_id=1, source_target_pairs={{0,1},{1,0},{2,3},{3,2},{4,5},{5,4},{6,7},{7,6},{8,9},{9,8},{10,11... | collective-permute-start | bytes 2654216 | tf_op jit(solution)/shard_map/ppermute | solution.py:555
  54.7 1.2 %collective-permute-start.7 = (f32[16,128]{1,0:T(8,128)S(1)}, f32[16,128]{1,0:T(8,128)S(1)}, u32[]{:S(2)}, u32[]{:S(2)}) collective-permute-start(f32[16,128]{1,0:T(8,128)S(1)} %collective-permute-done.6.refs_2_), channel_id=1, source_target_pairs={{0,2},{2,0},{4,6},{6,4},{8,10},{10,8},{12,14},{14,12},{16,18},{18,... | collective-permute-start | bytes 24584 | tf_op jit(solution)/shard_map/ppermute | solution.py:464
  56.0 11.9 %collective-permute-start.10 = (f32[8,128]{1,0:T(8,128)S(1)}, f32[8,128]{1,0:T(8,128)S(1)}, u32[]{:S(2)}, u32[]{:S(2)}) collective-permute-start(f32[8,128]{1,0:T(8,128)S(1)} %shard_map.108.added), channel_id=1, source_target_pairs={{0,1},{1,0},{2,3},{3,2},{4,5},{5,4},{6,7},{7,6},{8,9},{9,8},{10,11... | collective-permute-start | bytes 12296 | tf_op jit(solution)/shard_map/ppermute | solution.py:555

commit v6 on v5

--- a/solution.py
+++ b/solution.py
@@ -15,6 +15,7 @@
 PLANE = NX * NY
 BLOCK_ROWS = 8
 BLOCK = BLOCK_ROWS * NX
+STEP_PLANES = 3
 SLOTS = 16
 TILE = 256
 LANES = 128
@@ -348,13 +349,14 @@
 
 def rotation_rows(n, shifts, owner, ritz):
     columns = ritz.shape[1]
+    steps = ritz[...].astype(jnp.float32)
     blocks = []
     for shift in shifts:
         source = lax.axis_index("orb") + (lax.axis_size("orb") - shift)
         source = jnp.where(source >= lax.axis_size("orb"), source - lax.axis_size("orb"), source)
         total = jnp.zeros((n.panel, columns), jnp.float32)
         for step in range(ritz.shape[0] // n.panel):
-            rows = ritz[step * n.panel : (step + 1) * n.panel, :].astype(jnp.float32)
+            rows = steps[step * n.panel : (step + 1) * n.panel, :]
             total = total + jnp.where(owner[step] == source, rows, 0.0)
         blocks.append(total)
     weights = jnp.concatenate(blocks, axis=0)
@@ -380,13 +382,10 @@
     return jnp.concatenate([rotation, both], axis=1)
 
 
-def tile_rows(n, panels, table, plane, block):
-    cells = pl.ds(n.start(plane, block), BLOCK)
-    parts = [panel[:, cells].astype(jnp.float32) for panel in panels]
-    stack = parts[0] if len(parts) == 1 else jnp.concatenate(parts, axis=0)
+def twice(parts, table, n, plane, block):
     atoms = table[pl.ds(aligned(block * n.atoms + plane * SLOTS, 16), SLOTS), :]
-    stack = jnp.concatenate([stack, atoms.astype(jnp.float32)], axis=0).astype(jnp.bfloat16)
-    return parts[0], stack
+    parts = parts + [atoms.astype(jnp.float32)]
+    return jnp.concatenate(parts * 2, axis=0).astype(jnp.bfloat16)
 
 
 def rotate_own_kernel(
@@ -404,16 +403,16 @@
         )
         rows_ref[...] = jnp.concatenate(split(jnp.concatenate([top, bottom], axis=0)), axis=1)
 
-    plane = pl.program_id(0)
     matrix = rows_ref[...]
-    for block in range(n.blocks):
-        own, stack = tile_rows(n, (panel,), table, plane, block)
+    for at in range(STEP_PLANES * n.blocks):
+        plane, block = pl.program_id(0) * STEP_PLANES + at // n.blocks, at % n.blocks
+        own = panel[:, pl.ds(n.start(plane, block), BLOCK)].astype(jnp.float32)
         both = jnp.dot(
             matrix,
-            jnp.concatenate([stack, stack], axis=0),
+            twice([own], table, n, plane, block),
             preferred_element_type=jnp.float32,
         )
-        cells = slice(block * BLOCK, (block + 1) * BLOCK)
+        cells = slice(at * BLOCK, (at + 1) * BLOCK)
         filtered[:, cells] = (own + both[columns : columns + n.panel, :]).astype(jnp.bfloat16)
         rotated[:, pl.ds(n.start(plane, block), BLOCK)] = both[0:columns, :]
 
@@ -427,20 +426,17 @@
         added = jnp.concatenate([add[...] for add in adds], axis=0)
         rows_ref[...] = jnp.concatenate(split(with_slots(rotation[...], added)), axis=1)
 
-    plane = pl.program_id(0)
     matrix = rows_ref[...]
-    for block in range(n.blocks):
+    for at in range(STEP_PLANES * n.blocks):
+        plane, block = pl.program_id(0) * STEP_PLANES + at // n.blocks, at % n.blocks
         cells = pl.ds(n.start(plane, block), BLOCK)
-        parts = [p[:, block * BLOCK : (block + 1) * BLOCK].astype(jnp.float32) for p in panels]
-        atoms = table[pl.ds(aligned(block * n.atoms + plane * SLOTS, 16), SLOTS), :]
-        parts.append(atoms.astype(jnp.float32))
-        stack = jnp.concatenate(parts, axis=0).astype(jnp.bfloat16)
+        parts = [p[:, at * BLOCK : (at + 1) * BLOCK].astype(jnp.float32) for p in panels]
         total = own[:, cells] + jnp.dot(
             matrix,
-            jnp.concatenate([stack, stack], axis=0),
+            twice(parts, table, n, plane, block),
             preferred_element_type=jnp.float32,
         )
-        rotated[:, block * BLOCK : (block + 1) * BLOCK] = total.astype(jnp.bfloat16)
+        rotated[:, at * BLOCK : (at + 1) * BLOCK] = total.astype(jnp.bfloat16)
 
 
 def call(kernel, out_shape, scratch, flops, *operands):
@@ -569,28 +565,28 @@
     ritz = ritz_rotation.reshape(-1, columns)
     smem = pl.BlockSpec(memory_space=pltpu.SMEM)
     vmem = pl.BlockSpec(memory_space=pltpu.VMEM)
-    plane_of = lambda rows: pl.BlockSpec((rows, PLANE), lambda i: (0, i))
+    planes_of = lambda rows: pl.BlockSpec((rows, STEP_PLANES * PLANE), lambda i: (0, i))
     params = pltpu.CompilerParams(vmem_limit_bytes=VMEM_LIMIT)
     rest = orb_count - 1
     filtered, rotated, rotation = pl.pallas_call(
         functools.partial(rotate_own_kernel, n, orb_count),
-        grid=(n.depth,),
+        grid=(n.depth // STEP_PLANES,),
         out_shape=(
             shape((panel, n.cells), bf16),
             shape((columns, n.cells), f32),
             shape((columns, rest * panel), f32),
         ),
         in_specs=[smem] + [vmem] * 4,
-        out_specs=(plane_of(panel), vmem, vmem),
+        out_specs=(planes_of(panel), vmem, vmem),
         scratch_shapes=[pltpu.VMEM((columns + panel, 2 * (panel + SLOTS)), bf16)],
         compiler_params=params,
     )(panel_owner, ritz, adds[0], share, table)
     rotated = pl.pallas_call(
         functools.partial(rotate_rest_kernel, n, rest),
-        grid=(n.depth,),
+        grid=(n.depth // STEP_PLANES,),
         out_shape=shape((columns, n.cells), bf16),
-        in_specs=[vmem] * (1 + rest) + [plane_of(panel)] * rest + [vmem] * 2,
-        out_specs=plane_of(columns),
+        in_specs=[vmem] * (1 + rest) + [planes_of(panel)] * rest + [vmem] * 2,
+        out_specs=planes_of(columns),
         scratch_shapes=[pltpu.VMEM((columns, 2 * (rest * panel + SLOTS)), bf16)],
         compiler_params=params,
     )(rotation, *adds[1:], *panels[1:], rotated, table)

time: 71.7 us -> 70.5 us (0.983)
  Pallas kernels: 24.9 us -> 22.4 us
  waiting for transfers between devices: 27.2 us -> 28.4 us
    pallas_call x1, Pallas kernels: 3.48 us -> 2.22 us  [body(): pl.pallas_call(functools.partial(rotate_rest_kernel, n, rest), grid=(n.de...]
    ppermute x2, waiting for transfers between devices: 6.45 us -> 7.69 us  [all_orbs(): lax.ppermute(block, 'orb', [(i, (i + k) % orb_count) for i in range(orb_c...]
    pallas_call x1, Pallas kernels: 4.22 us -> 2.98 us  [body(): pl.pallas_call(functools.partial(rotate_own_kernel, n, orb_count), grid=(...]
  transfers between devices with their start and end apart: 12 -> 12, of which waited for: 6 -> 6; matrix products, arithmetic and copies ran while one was open for 2% -> 2% of each run, Pallas kernels for 26% -> 24%
where the time goes in v6:
time: 70.5 us; the launch traced here: 70.1 us
  waiting for transfers between devices  28.4 us (40%)
  Pallas kernels  22.4 us (32%)
  starting transfers between devices  15.9 us (23%)
  other arithmetic  1.46 us (2%)
  local copies, waits for them, and re-layouts  1.19 us (2%)
  between operations  0.75 us (1%)
    ppermute x10, waiting for transfers between devices, swapped(): return lax.ppermute(block, 'grid', pairs)  20.7 us
    pallas_call x7, Pallas kernels, call(): pl.pallas_call(kernel, out_shape=out_shape, in_specs=[pl.BlockSpec(memory...  17.2 us
    ppermute x10, starting transfers between devices, swapped(): return lax.ppermute(block, 'grid', pairs)  14.4 us
    ppermute x2, waiting for transfers between devices, all_orbs(): lax.ppermute(block, 'orb', [(i, (i + k) % orb_count) for i in range(orb_c...  7.69 us
    pallas_call x1, Pallas kernels, body(): pl.pallas_call(functools.partial(rotate_own_kernel, n, orb_count), grid=(...  2.98 us
    pallas_call x1, Pallas kernels, body(): pl.pallas_call(functools.partial(rotate_rest_kernel, n, rest), grid=(n.de...  2.22 us
    ppermute x2, starting transfers between devices, all_orbs(): lax.ppermute(block, 'orb', [(i, (i + k) % orb_count) for i in range(orb_c...  1.53 us
  transfers between devices with their start and end apart: 12, of which 6 were waited for; matrix products, arithmetic and copies ran while one was open for 2% of the time, Pallas kernels for 24%

profile of v6, /device:TPU:11, one launch (start us, length us, event | category | flops | bytes accessed | tf_op | source)
XLA Modules:
  0.0 70.1 jit_solution(8952030508600172794)
XLA Ops:
  0.6 0.7 %collective-permute-start = (bf16[8,55296]{1,0:T(8,128)(2,1)}, bf16[8,55296]{1,0:T(8,128)(2,1)S(1)}, u32[]{:S(2)}, u32[]{:S(2)}) collective-permute-start(bf16[8,55296]{1,0:T(8,128)(2,1)} %initial.1), channel_id=1, source_target_pairs={{0,2},{2,0},{4,6},{6,4},{8,10},{10,8},{12,14},{14,12},{16,18},{18,... | collective-permute-start | bytes 2654216 | tf_op jit(solution)/shard_map/ppermute | solution.py:460
  1.4 3.1 %collective-permute-start.1 = (bf16[8,55296]{1,0:T(8,128)(2,1)}, bf16[8,55296]{1,0:T(8,128)(2,1)S(1)}, u32[]{:S(2)}, u32[]{:S(2)}) collective-permute-start(bf16[8,55296]{1,0:T(8,128)(2,1)} %initial.1), channel_id=1, source_target_pairs={{2,4},{4,2},{6,8},{8,6},{10,12},{12,10},{14,16},{16,14},{18,20},{2... | collective-permute-start | bytes 2654216 | tf_op jit(solution)/shard_map/ppermute | solution.py:460
  4.4 0.7 %fusion.5 = (f32[12,128]{1,0:T(8,128)S(1)}, f32[12,128]{1,0:T(8,128)S(1)}) fusion(s32[1536]{0:T(1024)} %param.11, s32[1536]{0:T(1024)} %param.12, s32[]{:T(128)S(6)} %mul.19), kind=kLoop, calls=%fused_computation.10 | loop fusion | flops 47616 | bytes 24580 | tf_op jit(solution)/shard_map/reshape | solution.py:513
  5.2 0.7 %pad_maximum_fusion.entry_ref = f32[36,128]{1,0:T(8,128)S(1)} fusion(f32[12,128]{1,0:T(8,128)} %bitcast.13, f32[12,128]{1,0:T(8,128)S(1)} %get-tuple-element.29, f32[12,128]{1,0:T(8,128)S(1)} %get-tuple-element.28), kind=kLoop, calls=%fused_computation | loop fusion | flops 9216 | bytes 36864 | tf_op jit(solution)/shard_map/concatenate | solution.py:511
  5.9 0.0 copy-start.1
  5.9 1.2 %copy-done.1 = bf16[8,55296]{1,0:T(8,128)(2,1)S(1)} copy-done((bf16[8,55296]{1,0:T(8,128)(2,1)S(1)}, bf16[8,55296]{1,0:T(8,128)(2,1)}, u32[]{:S(2)}) %copy-start.1) | copy-done | bytes 884760
  7.1 0.0 copy-start
  7.1 0.0 copy-start.2
  7.1 4.5 %shard_map.104 = (bf16[1152,768]{1,0:T(8,128)(2,1)S(1)}, f32[8,128]{1,0:T(8,128)S(1)}, bf16[672,768]{1,0:T(8,128)(2,1)S(1)}) custom-call(bf16[8,55296]{1,0:T(8,128)(2,1)S(1)} %copy-done.1, f32[36,128]{1,0:T(8,128)S(1)} %pad_maximum_fusion.entry_ref), custom_call_target="tpu_custom_call" | custom-call | flops 4000000000 | bytes 903168 | tf_op jit(solution)/shard_map/pallas_call | solution.py:444
  11.6 0.4 collective-permute-start.2
  12.0 0.0 copy-done
  12.0 0.0 copy-done.2
  12.0 0.0 copy-start.4
  12.0 3.0 %shard_map.105.local = f32[8,55296]{1,0:T(8,128)S(1)} custom-call(bf16[8,55296]{1,0:T(8,128)(2,1)S(1)} %copy-done.1, bf16[672,768]{1,0:T(8,128)(2,1)S(1)} %get-tuple-element.15.packed, f32[432,128]{1,0:T(8,128)S(1)} %bitcast.8, bf16[3,768,768]{2,1,0:T(8,128)(2,1)S(1)} %copy-done), custom_call_target="tpu_custom_call" | custom-call | flops 2000000000 | bytes 5677056 | tf_op jit(solution)/shard_map/pallas_call | solution.py:444
  15.0 0.0 collective-permute-done.2.refs_1_
  15.1 3.2 %collective-permute-start.3 = (f32[16,128]{1,0:T(8,128)S(1)}, f32[16,128]{1,0:T(8,128)S(1)}, u32[]{:S(2)}, u32[]{:S(2)}) collective-permute-start(f32[16,128]{1,0:T(8,128)S(1)} %pad_maximum_fusion.1), channel_id=1, source_target_pairs={{2,4},{4,2},{6,8},{8,6},{10,12},{12,10},{14,16},{16,14},{18,20},{2... | collective-permute-start | bytes 24584 | tf_op jit(solution)/shard_map/ppermute | solution.py:460
  18.2 7.4 %collective-permute-done.3.refs_2_ = f32[16,128]{1,0:T(8,128)S(1)} collective-permute-done((f32[16,128]{1,0:T(8,128)S(1)}, f32[16,128]{1,0:T(8,128)S(1)}, u32[]{:S(2)}, u32[]{:S(2)}) %collective-permute-start.3) | collective-permute-done | bytes 8224 | tf_op jit(solution)/shard_map/ppermute | solution.py:460
  25.6 0.0 collective-permute-start.4
  25.6 1.2 %collective-permute-done.4.refs_3_ = f32[16,128]{1,0:T(8,128)S(1)} collective-permute-done((f32[16,128]{1,0:T(8,128)S(1)}, f32[16,128]{1,0:T(8,128)S(1)}, u32[]{:S(2)}, u32[]{:S(2)}) %collective-permute-start.4) | collective-permute-done | bytes 8224 | tf_op jit(solution)/shard_map/ppermute | solution.py:460
  26.8 0.0 collective-permute-done.inner
  26.8 0.0 collective-permute-done.1.outer
  26.8 0.0 copy-done.4
  26.8 2.0 %shard_map.106 = (f32[8,55296]{1,0:T(8,128)S(1)}, bf16[8,55296]{1,0:T(8,128)(2,1)S(1)}) custom-call(f32[8,55296]{1,0:T(8,128)S(1)} %shard_map.105.local, bf16[8,55296]{1,0:T(8,128)(2,1)S(1)} %collective-permute-done.inner, bf16[8,55296]{1,0:T(8,128)(2,1)S(1)} %collective-permute-done.1.outer, bf16[1152,768]{1,0:T(8,128)(2,1)S(1)} %get-tuple-element.16.table.refs_3_, ...), custom_call_target="tpu_custom_call" | custom-call | flops 1000000000 | bytes 5333248 | tf_op jit(solution)/shard_map/pallas_call | solution.py:444
  28.8 0.2 collective-permute-start.8
  29.1 3.0 %collective-permute-start.9 = (bf16[8,55296]{1,0:T(8,128)(2,1)S(1)}, bf16[8,55296]{1,0:T(8,128)(2,1)S(1)}, u32[]{:S(2)}, u32[]{:S(2)}) collective-permute-start(bf16[8,55296]{1,0:T(8,128)(2,1)S(1)} %get-tuple-element.24), channel_id=1, source_target_pairs={{2,4},{4,2},{6,8},{8,6},{10,12},{12,10},{14,16},{16,14},{18,20},{2... | collective-permute-start | bytes 2654216 | tf_op jit(solution)/shard_map/ppermute | solution.py:460
  32.1 1.7 %shard_map.107 = (f32[8,128]{1,0:T(8,128)S(1)}, bf16[672,768]{1,0:T(8,128)(2,1)S(1)}, bf16[672,768]{1,0:T(8,128)(2,1)S(1)}) custom-call(f32[8,55296]{1,0:T(8,128)S(1)} %get-tuple-element.19.field, bf16[1152,768]{1,0:T(8,128)(2,1)S(1)} %get-tuple-element.16.table.refs_3_), custom_call_target="tpu_custom_call" | custom-call | flops 1000000000 | bytes 3538944 | tf_op jit(solution)/shard_map/pallas_call | solution.py:444
  33.8 0.3 collective-permute-start.5
  34.0 0.9 %collective-permute-done.5.refs_1_ = f32[8,128]{1,0:T(8,128)S(1)} collective-permute-done((f32[8,128]{1,0:T(8,128)S(1)}, f32[8,128]{1,0:T(8,128)S(1)}, u32[]{:S(2)}, u32[]{:S(2)}) %collective-permute-start.5) | collective-permute-done | bytes 4128 | tf_op jit(solution)/shard_map/ppermute | solution.py:460
  35.0 3.5 %collective-permute-start.6 = (f32[16,128]{1,0:T(8,128)S(1)}, f32[16,128]{1,0:T(8,128)S(1)}, u32[]{:S(2)}, u32[]{:S(2)}) collective-permute-start(f32[16,128]{1,0:T(8,128)S(1)} %pad_maximum_fusion.2), channel_id=1, source_target_pairs={{2,4},{4,2},{6,8},{8,6},{10,12},{12,10},{14,16},{16,14},{18,20},{2... | collective-permute-start | bytes 24584 | tf_op jit(solution)/shard_map/ppermute | solution.py:460
  38.5 4.7 %shard_map.109.local = f32[8,55296]{1,0:T(8,128)S(1)} custom-call(f32[8,55296]{1,0:T(8,128)S(1)} %get-tuple-element.19.field, bf16[8,55296]{1,0:T(8,128)(2,1)S(1)} %copy-done.1, bf16[672,768]{1,0:T(8,128)(2,1)S(1)} %get-tuple-element.21.packed, bf16[672,768]{1,0:T(8,128)(2,1)S(1)} %get-tuple-element.22.rest, f32[432,128]{1,0:T(8,128)S(1)} %bitcast.9, ...), custom_call_target="tpu_custom_call" | custom-call | flops 3000000000 | bytes 8478720 | tf_op jit(solution)/shard_map/pallas_call | solution.py:444
  43.2 0.0 copy-start.3
  43.2 0.0 copy-start.5
  43.3 10.1 %collective-permute-done.6.refs_2_ = f32[16,128]{1,0:T(8,128)S(1)} collective-permute-done((f32[16,128]{1,0:T(8,128)S(1)}, f32[16,128]{1,0:T(8,128)S(1)}, u32[]{:S(2)}, u32[]{:S(2)}) %collective-permute-start.6) | collective-permute-done | bytes 8224 | tf_op jit(solution)/shard_map/ppermute | solution.py:460
  53.4 0.0 collective-permute-done.8.inner
  53.4 0.0 collective-permute-done.9.outer
  53.4 1.0 %shard_map.110.panel = bf16[8,55296]{1,0:T(8,128)(2,1)S(1)} custom-call(f32[8,55296]{1,0:T(8,128)S(1)} %shard_map.109.local, bf16[8,55296]{1,0:T(8,128)(2,1)S(1)} %collective-permute-done.8.inner, bf16[8,55296]{1,0:T(8,128)(2,1)S(1)} %collective-permute-done.9.outer), custom_call_target="tpu_custom_call" | custom-call | flops 1000000000 | bytes 3538944 | tf_op jit(solution)/shard_map/pallas_call | solution.py:444
  54.4 0.3 collective-permute-start.11
  54.7 0.0 collective-permute-start.7
  54.7 1.2 %collective-permute-done.7.refs_3_ = f32[16,128]{1,0:T(8,128)S(1)} collective-permute-done((f32[16,128]{1,0:T(8,128)S(1)}, f32[16,128]{1,0:T(8,128)S(1)}, u32[]{:S(2)}, u32[]{:S(2)}) %collective-permute-start.7) | collective-permute-done | bytes 8224 | tf_op jit(solution)/shard_map/ppermute | solution.py:460
  55.9 0.1 shard_map.108.added
  56.0 1.2 %collective-permute-start.10 = (f32[8,128]{1,0:T(8,128)S(1)}, f32[8,128]{1,0:T(8,128)S(1)}, u32[]{:S(2)}, u32[]{:S(2)}) collective-permute-start(f32[8,128]{1,0:T(8,128)S(1)} %shard_map.108.added), channel_id=1, source_target_pairs={{0,1},{1,0},{2,3},{3,2},{4,5},{5,4},{6,7},{7,6},{8,9},{9,8},{10,11... | collective-permute-start | bytes 12296 | tf_op jit(solution)/shard_map/ppermute | solution.py:551
  57.2 0.0 copy-done.3
  57.2 0.0 copy-done.5
  57.2 3.0 %shard_map.111 = (bf16[8,55296]{1,0:T(8,128)(2,1)}, f32[16,55296]{1,0:T(8,128)S(1)}, f32[16,8]{1,0:T(8,128)S(1)}) custom-call(s32[4]{0:T(128)S(1)} %copy-done.5, bf16[32,16]{1,0:T(8,128)(2,1)S(1)} %bitcast.10, f32[8,128]{1,0:T(8,128)S(1)} %shard_map.108.added, bf16[8,55296]{1,0:T(8,128)(2,1)S(1)} %shard_map.110.panel, ...), custom_call_target="tpu_custom_call" | custom-call | tf_op jit(solution)/shard_map/pallas_call | solution.py:571
  60.2 7.7 %collective-permute-done.10.refs_0_ = f32[8,128]{1,0:T(8,128)S(1)} collective-permute-done((f32[8,128]{1,0:T(8,128)S(1)}, f32[8,128]{1,0:T(8,128)S(1)}, u32[]{:S(2)}, u32[]{:S(2)}) %collective-permute-start.10) | collective-permute-done | bytes 4128 | tf_op jit(solution)/shard_map/ppermute | solution.py:551
  67.9 0.0 collective-permute-done.11.refs_1_
  67.9 2.2 %shard_map.112 = bf16[16,55296]{1,0:T(8,128)(2,1)} custom-call(f32[16,8]{1,0:T(8,128)S(1)} %get-tuple-element.26.rotation, f32[8,128]{1,0:T(8,128)S(1)} %collective-permute-done.10.refs_0_, bf16[8,55296]{1,0:T(8,128)(2,1)S(1)} %collective-permute-done.11.refs_1_, f32[16,55296]{1,0:T(8,128)S(1)} %get-tuple-element.27.refs_2_, ...), custom_call_target="tpu_custom_call" | custom-call | tf_op jit(solution)/shard_map/pallas_call | solution.py:584
  (2 shorter events, 0.0 us)
Async XLA Ops:
  0.6 26.1 %collective-permute-start = (bf16[8,55296]{1,0:T(8,128)(2,1)}, bf16[8,55296]{1,0:T(8,128)(2,1)S(1)}, u32[]{:S(2)}, u32[]{:S(2)}) collective-permute-start(bf16[8,55296]{1,0:T(8,128)(2,1)} %initial.1), channel_id=1, source_target_pairs={{0,2},{2,0},{4,6},{6,4},{8,10},{10,8},{12,14},{14,12},{16,18},{18,... | collective-permute-start | bytes 2654216 | tf_op jit(solution)/shard_map/ppermute | solution.py:460
  1.4 25.4 %collective-permute-start.1 = (bf16[8,55296]{1,0:T(8,128)(2,1)}, bf16[8,55296]{1,0:T(8,128)(2,1)S(1)}, u32[]{:S(2)}, u32[]{:S(2)}) collective-permute-start(bf16[8,55296]{1,0:T(8,128)(2,1)} %initial.1), channel_id=1, source_target_pairs={{2,4},{4,2},{6,8},{8,6},{10,12},{12,10},{14,16},{16,14},{18,20},{2... | collective-permute-start | bytes 2654216 | tf_op jit(solution)/shard_map/ppermute | solution.py:460
  5.9 1.2 %copy-start.1 = (bf16[8,55296]{1,0:T(8,128)(2,1)S(1)}, bf16[8,55296]{1,0:T(8,128)(2,1)}, u32[]{:S(2)}) copy-start(bf16[8,55296]{1,0:T(8,128)(2,1)} %initial.1) | copy-start | bytes 2654212
  7.1 4.9 %copy-start = (bf16[3,768,768]{2,1,0:T(8,128)(2,1)S(1)}, bf16[3,768,768]{2,1,0:T(8,128)(2,1)}, u32[]{:S(2)}) copy-start(bf16[3,768,768]{2,1,0:T(8,128)(2,1)} %constant.48.clone.taps) | copy-start | bytes 10616836
  7.1 4.9 %copy-start.2 = (f32[55296]{0:T(1024)S(1)}, f32[55296]{0:T(1024)}, u32[]{:S(2)}) copy-start(f32[55296]{0:T(1024)} %param.10) | copy-start | bytes 663556
  11.6 3.4 %collective-permute-start.2 = (f32[8,128]{1,0:T(8,128)S(1)}, f32[8,128]{1,0:T(8,128)S(1)}, u32[]{:S(2)}, u32[]{:S(2)}) collective-permute-start(f32[8,128]{1,0:T(8,128)S(1)} %get-tuple-element.17.refs_0_), channel_id=1, source_target_pairs={{0,2},{2,0},{4,6},{6,4},{8,10},{10,8},{12,14},{14,12},{16,18},{18,... | collective-permute-start | bytes 12296 | tf_op jit(solution)/shard_map/ppermute | solution.py:460
  12.0 14.8 %copy-start.4 = (f32[64]{0:T(128)S(1)}, f32[64]{0:T(128)}, u32[]{:S(2)}) copy-start(f32[64]{0:T(128)} %param.14) | copy-start | bytes 772
  15.1 10.5 %collective-permute-start.3 = (f32[16,128]{1,0:T(8,128)S(1)}, f32[16,128]{1,0:T(8,128)S(1)}, u32[]{:S(2)}, u32[]{:S(2)}) collective-permute-start(f32[16,128]{1,0:T(8,128)S(1)} %pad_maximum_fusion.1), channel_id=1, source_target_pairs={{2,4},{4,2},{6,8},{8,6},{10,12},{12,10},{14,16},{16,14},{18,20},{2... | collective-permute-start | bytes 24584 | tf_op jit(solution)/shard_map/ppermute | solution.py:460
  25.6 1.2 %collective-permute-start.4 = (f32[16,128]{1,0:T(8,128)S(1)}, f32[16,128]{1,0:T(8,128)S(1)}, u32[]{:S(2)}, u32[]{:S(2)}) collective-permute-start(f32[16,128]{1,0:T(8,128)S(1)} %collective-permute-done.3.refs_2_), channel_id=1, source_target_pairs={{0,2},{2,0},{4,6},{6,4},{8,10},{10,8},{12,14},{14,12},{16,18},{18,... | collective-permute-start | bytes 24584 | tf_op jit(solution)/shard_map/ppermute | solution.py:460
  28.8 24.5 %collective-permute-start.8 = (bf16[8,55296]{1,0:T(8,128)(2,1)S(1)}, bf16[8,55296]{1,0:T(8,128)(2,1)S(1)}, u32[]{:S(2)}, u32[]{:S(2)}) collective-permute-start(bf16[8,55296]{1,0:T(8,128)(2,1)S(1)} %get-tuple-element.24), channel_id=1, source_target_pairs={{0,2},{2,0},{4,6},{6,4},{8,10},{10,8},{12,14},{14,12},{16,18},{18,... | collective-permute-start | bytes 2654216 | tf_op jit(solution)/shard_map/ppermute | solution.py:460
  29.1 24.3 %collective-permute-start.9 = (bf16[8,55296]{1,0:T(8,128)(2,1)S(1)}, bf16[8,55296]{1,0:T(8,128)(2,1)S(1)}, u32[]{:S(2)}, u32[]{:S(2)}) collective-permute-start(bf16[8,55296]{1,0:T(8,128)(2,1)S(1)} %get-tuple-element.24), channel_id=1, source_target_pairs={{2,4},{4,2},{6,8},{8,6},{10,12},{12,10},{14,16},{16,14},{18,20},{2... | collective-permute-start | bytes 2654216 | tf_op jit(solution)/shard_map/ppermute | solution.py:460
  33.8 1.2 %collective-permute-start.5 = (f32[8,128]{1,0:T(8,128)S(1)}, f32[8,128]{1,0:T(8,128)S(1)}, u32[]{:S(2)}, u32[]{:S(2)}) collective-permute-start(f32[8,128]{1,0:T(8,128)S(1)} %get-tuple-element.20.refs_0_), channel_id=1, source_target_pairs={{0,2},{2,0},{4,6},{6,4},{8,10},{10,8},{12,14},{14,12},{16,18},{18,... | collective-permute-start | bytes 12296 | tf_op jit(solution)/shard_map/ppermute | solution.py:460
  35.0 18.4 %collective-permute-start.6 = (f32[16,128]{1,0:T(8,128)S(1)}, f32[16,128]{1,0:T(8,128)S(1)}, u32[]{:S(2)}, u32[]{:S(2)}) collective-permute-start(f32[16,128]{1,0:T(8,128)S(1)} %pad_maximum_fusion.2), channel_id=1, source_target_pairs={{2,4},{4,2},{6,8},{8,6},{10,12},{12,10},{14,16},{16,14},{18,20},{2... | collective-permute-start | bytes 24584 | tf_op jit(solution)/shard_map/ppermute | solution.py:460
  43.2 14.0 %copy-start.3 = (bf16[4,8,16]{2,1,0:T(8,128)(2,1)S(1)}, bf16[4,8,16]{2,1,0:T(8,128)(2,1)}, u32[]{:S(2)}) copy-start(bf16[4,8,16]{2,1,0:T(8,128)(2,1)} %param.15) | copy-start | bytes 3076
  43.2 14.0 %copy-start.5 = (s32[4]{0:T(128)S(1)}, s32[4]{0:T(128)}, u32[]{:S(2)}) copy-start(s32[4]{0:T(128)} %owner.1) | copy-start | bytes 52
  54.4 13.5 %collective-permute-start.11 = (bf16[8,55296]{1,0:T(8,128)(2,1)S(1)}, bf16[8,55296]{1,0:T(8,128)(2,1)S(1)}, u32[]{:S(2)}, u32[]{:S(2)}) collective-permute-start(bf16[8,55296]{1,0:T(8,128)(2,1)S(1)} %shard_map.110.panel), channel_id=1, source_target_pairs={{0,1},{1,0},{2,3},{3,2},{4,5},{5,4},{6,7},{7,6},{8,9},{9,8},{10,11... | collective-permute-start | bytes 2654216 | tf_op jit(solution)/shard_map/ppermute | solution.py:551
  54.7 1.2 %collective-permute-start.7 = (f32[16,128]{1,0:T(8,128)S(1)}, f32[16,128]{1,0:T(8,128)S(1)}, u32[]{:S(2)}, u32[]{:S(2)}) collective-permute-start(f32[16,128]{1,0:T(8,128)S(1)} %collective-permute-done.6.refs_2_), channel_id=1, source_target_pairs={{0,2},{2,0},{4,6},{6,4},{8,10},{10,8},{12,14},{14,12},{16,18},{18,... | collective-permute-start | bytes 24584 | tf_op jit(solution)/shard_map/ppermute | solution.py:460
  56.0 11.9 %collective-permute-start.10 = (f32[8,128]{1,0:T(8,128)S(1)}, f32[8,128]{1,0:T(8,128)S(1)}, u32[]{:S(2)}, u32[]{:S(2)}) collective-permute-start(f32[8,128]{1,0:T(8,128)S(1)} %shard_map.108.added), channel_id=1, source_target_pairs={{0,1},{1,0},{2,3},{3,2},{4,5},{5,4},{6,7},{7,6},{8,9},{9,8},{10,11... | collective-permute-start | bytes 12296 | tf_op jit(solution)/shard_map/ppermute | solution.py:551

commit v7 on v6

--- a/solution.py
+++ b/solution.py
@@ -107,7 +107,7 @@
             one(block)
             return carry
 
-        lax.fori_loop(*CHUNKS[chunk], step, None, unroll=2)
+        lax.fori_loop(*CHUNKS[chunk], step, None, unroll=4)
 
 
 def pack_planes(n, source, targets):

time: 70.5 us -> 70.3 us (level)
  no operation moved by 1% of the time
where the time goes in v7:
time: 70.3 us; the launch traced here: 69.9 us
  waiting for transfers between devices  28.5 us (41%)
  Pallas kernels  22.1 us (31%)
  starting transfers between devices  15.9 us (23%)
  other arithmetic  1.46 us (2%)
  local copies, waits for them, and re-layouts  1.19 us (2%)
  between operations  0.75 us (1%)
    ppermute x10, waiting for transfers between devices, swapped(): return lax.ppermute(block, 'grid', pairs)  20.8 us
    pallas_call x7, Pallas kernels, call(): pl.pallas_call(kernel, out_shape=out_shape, in_specs=[pl.BlockSpec(memory...  16.9 us
    ppermute x10, starting transfers between devices, swapped(): return lax.ppermute(block, 'grid', pairs)  14.4 us
    ppermute x2, waiting for transfers between devices, all_orbs(): lax.ppermute(block, 'orb', [(i, (i + k) % orb_count) for i in range(orb_c...  7.69 us
    pallas_call x1, Pallas kernels, body(): pl.pallas_call(functools.partial(rotate_own_kernel, n, orb_count), grid=(...  2.98 us
    pallas_call x1, Pallas kernels, body(): pl.pallas_call(functools.partial(rotate_rest_kernel, n, rest), grid=(n.de...  2.21 us
    ppermute x2, starting transfers between devices, all_orbs(): lax.ppermute(block, 'orb', [(i, (i + k) % orb_count) for i in range(orb_c...  1.53 us
  transfers between devices with their start and end apart: 12, of which 6 were waited for; matrix products, arithmetic and copies ran while one was open for 2% of the time, Pallas kernels for 24%

profile of v7, /device:TPU:11, one launch (start us, length us, event | category | flops | bytes accessed | tf_op | source)
XLA Modules:
  0.0 69.9 jit_solution(8438595551056725642)
XLA Ops:
  0.6 0.7 %collective-permute-start = (bf16[8,55296]{1,0:T(8,128)(2,1)}, bf16[8,55296]{1,0:T(8,128)(2,1)S(1)}, u32[]{:S(2)}, u32[]{:S(2)}) collective-permute-start(bf16[8,55296]{1,0:T(8,128)(2,1)} %initial.1), channel_id=1, source_target_pairs={{0,2},{2,0},{4,6},{6,4},{8,10},{10,8},{12,14},{14,12},{16,18},{18,... | collective-permute-start | bytes 2654216 | tf_op jit(solution)/shard_map/ppermute | solution.py:460
  1.4 3.1 %collective-permute-start.1 = (bf16[8,55296]{1,0:T(8,128)(2,1)}, bf16[8,55296]{1,0:T(8,128)(2,1)S(1)}, u32[]{:S(2)}, u32[]{:S(2)}) collective-permute-start(bf16[8,55296]{1,0:T(8,128)(2,1)} %initial.1), channel_id=1, source_target_pairs={{2,4},{4,2},{6,8},{8,6},{10,12},{12,10},{14,16},{16,14},{18,20},{2... | collective-permute-start | bytes 2654216 | tf_op jit(solution)/shard_map/ppermute | solution.py:460
  4.4 0.7 %fusion.5 = (f32[12,128]{1,0:T(8,128)S(1)}, f32[12,128]{1,0:T(8,128)S(1)}) fusion(s32[1536]{0:T(1024)} %param.11, s32[1536]{0:T(1024)} %param.12, s32[]{:T(128)S(6)} %mul.19), kind=kLoop, calls=%fused_computation.10 | loop fusion | flops 47616 | bytes 24580 | tf_op jit(solution)/shard_map/reshape | solution.py:513
  5.2 0.7 %pad_maximum_fusion.entry_ref = f32[36,128]{1,0:T(8,128)S(1)} fusion(f32[12,128]{1,0:T(8,128)} %bitcast.13, f32[12,128]{1,0:T(8,128)S(1)} %get-tuple-element.29, f32[12,128]{1,0:T(8,128)S(1)} %get-tuple-element.28), kind=kLoop, calls=%fused_computation | loop fusion | flops 9216 | bytes 36864 | tf_op jit(solution)/shard_map/concatenate | solution.py:511
  5.9 0.0 copy-start.1
  5.9 1.2 %copy-done.1 = bf16[8,55296]{1,0:T(8,128)(2,1)S(1)} copy-done((bf16[8,55296]{1,0:T(8,128)(2,1)S(1)}, bf16[8,55296]{1,0:T(8,128)(2,1)}, u32[]{:S(2)}) %copy-start.1) | copy-done | bytes 884760
  7.1 0.0 copy-start
  7.1 0.0 copy-start.2
  7.1 4.5 %shard_map.104 = (bf16[1152,768]{1,0:T(8,128)(2,1)S(1)}, f32[8,128]{1,0:T(8,128)S(1)}, bf16[672,768]{1,0:T(8,128)(2,1)S(1)}) custom-call(bf16[8,55296]{1,0:T(8,128)(2,1)S(1)} %copy-done.1, f32[36,128]{1,0:T(8,128)S(1)} %pad_maximum_fusion.entry_ref), custom_call_target="tpu_custom_call" | custom-call | flops 4000000000 | bytes 903168 | tf_op jit(solution)/shard_map/pallas_call | solution.py:444
  11.6 0.4 collective-permute-start.2
  12.0 0.0 copy-done
  12.0 0.0 copy-done.2
  12.0 0.0 copy-start.4
  12.0 3.0 %shard_map.105.local = f32[8,55296]{1,0:T(8,128)S(1)} custom-call(bf16[8,55296]{1,0:T(8,128)(2,1)S(1)} %copy-done.1, bf16[672,768]{1,0:T(8,128)(2,1)S(1)} %get-tuple-element.15.packed, f32[432,128]{1,0:T(8,128)S(1)} %bitcast.8, bf16[3,768,768]{2,1,0:T(8,128)(2,1)S(1)} %copy-done), custom_call_target="tpu_custom_call" | custom-call | flops 2000000000 | bytes 5677056 | tf_op jit(solution)/shard_map/pallas_call | solution.py:444
  15.0 0.0 collective-permute-done.2.refs_1_
  15.0 3.2 %collective-permute-start.3 = (f32[16,128]{1,0:T(8,128)S(1)}, f32[16,128]{1,0:T(8,128)S(1)}, u32[]{:S(2)}, u32[]{:S(2)}) collective-permute-start(f32[16,128]{1,0:T(8,128)S(1)} %pad_maximum_fusion.1), channel_id=1, source_target_pairs={{2,4},{4,2},{6,8},{8,6},{10,12},{12,10},{14,16},{16,14},{18,20},{2... | collective-permute-start | bytes 24584 | tf_op jit(solution)/shard_map/ppermute | solution.py:460
  18.2 7.4 %collective-permute-done.3.refs_2_ = f32[16,128]{1,0:T(8,128)S(1)} collective-permute-done((f32[16,128]{1,0:T(8,128)S(1)}, f32[16,128]{1,0:T(8,128)S(1)}, u32[]{:S(2)}, u32[]{:S(2)}) %collective-permute-start.3) | collective-permute-done | bytes 8224 | tf_op jit(solution)/shard_map/ppermute | solution.py:460
  25.6 0.0 collective-permute-start.4
  25.6 1.2 %collective-permute-done.4.refs_3_ = f32[16,128]{1,0:T(8,128)S(1)} collective-permute-done((f32[16,128]{1,0:T(8,128)S(1)}, f32[16,128]{1,0:T(8,128)S(1)}, u32[]{:S(2)}, u32[]{:S(2)}) %collective-permute-start.4) | collective-permute-done | bytes 8224 | tf_op jit(solution)/shard_map/ppermute | solution.py:460
  26.8 0.0 collective-permute-done.inner
  26.8 0.0 collective-permute-done.1.outer
  26.8 0.0 copy-done.4
  26.8 1.9 %shard_map.106 = (f32[8,55296]{1,0:T(8,128)S(1)}, bf16[8,55296]{1,0:T(8,128)(2,1)S(1)}) custom-call(f32[8,55296]{1,0:T(8,128)S(1)} %shard_map.105.local, bf16[8,55296]{1,0:T(8,128)(2,1)S(1)} %collective-permute-done.inner, bf16[8,55296]{1,0:T(8,128)(2,1)S(1)} %collective-permute-done.1.outer, bf16[1152,768]{1,0:T(8,128)(2,1)S(1)} %get-tuple-element.16.table.refs_3_, ...), custom_call_target="tpu_custom_call" | custom-call | flops 1000000000 | bytes 5333248 | tf_op jit(solution)/shard_map/pallas_call | solution.py:444
  28.6 0.2 collective-permute-start.8
  28.9 3.0 %collective-permute-start.9 = (bf16[8,55296]{1,0:T(8,128)(2,1)S(1)}, bf16[8,55296]{1,0:T(8,128)(2,1)S(1)}, u32[]{:S(2)}, u32[]{:S(2)}) collective-permute-start(bf16[8,55296]{1,0:T(8,128)(2,1)S(1)} %get-tuple-element.24), channel_id=1, source_target_pairs={{2,4},{4,2},{6,8},{8,6},{10,12},{12,10},{14,16},{16,14},{18,20},{2... | collective-permute-start | bytes 2654216 | tf_op jit(solution)/shard_map/ppermute | solution.py:460
  31.9 1.7 %shard_map.107 = (f32[8,128]{1,0:T(8,128)S(1)}, bf16[672,768]{1,0:T(8,128)(2,1)S(1)}, bf16[672,768]{1,0:T(8,128)(2,1)S(1)}) custom-call(f32[8,55296]{1,0:T(8,128)S(1)} %get-tuple-element.19.field, bf16[1152,768]{1,0:T(8,128)(2,1)S(1)} %get-tuple-element.16.table.refs_3_), custom_call_target="tpu_custom_call" | custom-call | flops 1000000000 | bytes 3538944 | tf_op jit(solution)/shard_map/pallas_call | solution.py:444
  33.6 0.3 collective-permute-start.5
  33.9 0.9 %collective-permute-done.5.refs_1_ = f32[8,128]{1,0:T(8,128)S(1)} collective-permute-done((f32[8,128]{1,0:T(8,128)S(1)}, f32[8,128]{1,0:T(8,128)S(1)}, u32[]{:S(2)}, u32[]{:S(2)}) %collective-permute-start.5) | collective-permute-done | bytes 4128 | tf_op jit(solution)/shard_map/ppermute | solution.py:460
  34.8 3.5 %collective-permute-start.6 = (f32[16,128]{1,0:T(8,128)S(1)}, f32[16,128]{1,0:T(8,128)S(1)}, u32[]{:S(2)}, u32[]{:S(2)}) collective-permute-start(f32[16,128]{1,0:T(8,128)S(1)} %pad_maximum_fusion.2), channel_id=1, source_target_pairs={{2,4},{4,2},{6,8},{8,6},{10,12},{12,10},{14,16},{16,14},{18,20},{2... | collective-permute-start | bytes 24584 | tf_op jit(solution)/shard_map/ppermute | solution.py:460
  38.3 4.7 %shard_map.109.local = f32[8,55296]{1,0:T(8,128)S(1)} custom-call(f32[8,55296]{1,0:T(8,128)S(1)} %get-tuple-element.19.field, bf16[8,55296]{1,0:T(8,128)(2,1)S(1)} %copy-done.1, bf16[672,768]{1,0:T(8,128)(2,1)S(1)} %get-tuple-element.21.packed, bf16[672,768]{1,0:T(8,128)(2,1)S(1)} %get-tuple-element.22.rest, f32[432,128]{1,0:T(8,128)S(1)} %bitcast.9, ...), custom_call_target="tpu_custom_call" | custom-call | flops 3000000000 | bytes 8478720 | tf_op jit(solution)/shard_map/pallas_call | solution.py:444
  43.0 0.0 copy-start.3
  43.0 0.0 copy-start.5
  43.0 10.2 %collective-permute-done.6.refs_2_ = f32[16,128]{1,0:T(8,128)S(1)} collective-permute-done((f32[16,128]{1,0:T(8,128)S(1)}, f32[16,128]{1,0:T(8,128)S(1)}, u32[]{:S(2)}, u32[]{:S(2)}) %collective-permute-start.6) | collective-permute-done | bytes 8224 | tf_op jit(solution)/shard_map/ppermute | solution.py:460
  53.2 0.0 collective-permute-done.8.inner
  53.2 0.0 collective-permute-done.9.outer
  53.2 1.1 %shard_map.110.panel = bf16[8,55296]{1,0:T(8,128)(2,1)S(1)} custom-call(f32[8,55296]{1,0:T(8,128)S(1)} %shard_map.109.local, bf16[8,55296]{1,0:T(8,128)(2,1)S(1)} %collective-permute-done.8.inner, bf16[8,55296]{1,0:T(8,128)(2,1)S(1)} %collective-permute-done.9.outer), custom_call_target="tpu_custom_call" | custom-call | flops 1000000000 | bytes 3538944 | tf_op jit(solution)/shard_map/pallas_call | solution.py:444
  54.3 0.3 collective-permute-start.11
  54.6 0.0 collective-permute-start.7
  54.6 1.2 %collective-permute-done.7.refs_3_ = f32[16,128]{1,0:T(8,128)S(1)} collective-permute-done((f32[16,128]{1,0:T(8,128)S(1)}, f32[16,128]{1,0:T(8,128)S(1)}, u32[]{:S(2)}, u32[]{:S(2)}) %collective-permute-start.7) | collective-permute-done | bytes 8224 | tf_op jit(solution)/shard_map/ppermute | solution.py:460
  55.8 0.1 shard_map.108.added
  55.8 1.2 %collective-permute-start.10 = (f32[8,128]{1,0:T(8,128)S(1)}, f32[8,128]{1,0:T(8,128)S(1)}, u32[]{:S(2)}, u32[]{:S(2)}) collective-permute-start(f32[8,128]{1,0:T(8,128)S(1)} %shard_map.108.added), channel_id=1, source_target_pairs={{0,1},{1,0},{2,3},{3,2},{4,5},{5,4},{6,7},{7,6},{8,9},{9,8},{10,11... | collective-permute-start | bytes 12296 | tf_op jit(solution)/shard_map/ppermute | solution.py:551
  57.1 0.0 copy-done.3
  57.1 0.0 copy-done.5
  57.1 3.0 %shard_map.111 = (bf16[8,55296]{1,0:T(8,128)(2,1)}, f32[16,55296]{1,0:T(8,128)S(1)}, f32[16,8]{1,0:T(8,128)S(1)}) custom-call(s32[4]{0:T(128)S(1)} %copy-done.5, bf16[32,16]{1,0:T(8,128)(2,1)S(1)} %bitcast.10, f32[8,128]{1,0:T(8,128)S(1)} %shard_map.108.added, bf16[8,55296]{1,0:T(8,128)(2,1)S(1)} %shard_map.110.panel, ...), custom_call_target="tpu_custom_call" | custom-call | tf_op jit(solution)/shard_map/pallas_call | solution.py:571
  60.0 7.7 %collective-permute-done.10.refs_0_ = f32[8,128]{1,0:T(8,128)S(1)} collective-permute-done((f32[8,128]{1,0:T(8,128)S(1)}, f32[8,128]{1,0:T(8,128)S(1)}, u32[]{:S(2)}, u32[]{:S(2)}) %collective-permute-start.10) | collective-permute-done | bytes 4128 | tf_op jit(solution)/shard_map/ppermute | solution.py:551
  67.7 0.0 collective-permute-done.11.refs_1_
  67.7 2.2 %shard_map.112 = bf16[16,55296]{1,0:T(8,128)(2,1)} custom-call(f32[16,8]{1,0:T(8,128)S(1)} %get-tuple-element.26.rotation, f32[8,128]{1,0:T(8,128)S(1)} %collective-permute-done.10.refs_0_, bf16[8,55296]{1,0:T(8,128)(2,1)S(1)} %collective-permute-done.11.refs_1_, f32[16,55296]{1,0:T(8,128)S(1)} %get-tuple-element.27.refs_2_, ...), custom_call_target="tpu_custom_call" | custom-call | tf_op jit(solution)/shard_map/pallas_call | solution.py:584
  (2 shorter events, 0.0 us)
Async XLA Ops:
  0.6 26.1 %collective-permute-start = (bf16[8,55296]{1,0:T(8,128)(2,1)}, bf16[8,55296]{1,0:T(8,128)(2,1)S(1)}, u32[]{:S(2)}, u32[]{:S(2)}) collective-permute-start(bf16[8,55296]{1,0:T(8,128)(2,1)} %initial.1), channel_id=1, source_target_pairs={{0,2},{2,0},{4,6},{6,4},{8,10},{10,8},{12,14},{14,12},{16,18},{18,... | collective-permute-start | bytes 2654216 | tf_op jit(solution)/shard_map/ppermute | solution.py:460
  1.4 25.4 %collective-permute-start.1 = (bf16[8,55296]{1,0:T(8,128)(2,1)}, bf16[8,55296]{1,0:T(8,128)(2,1)S(1)}, u32[]{:S(2)}, u32[]{:S(2)}) collective-permute-start(bf16[8,55296]{1,0:T(8,128)(2,1)} %initial.1), channel_id=1, source_target_pairs={{2,4},{4,2},{6,8},{8,6},{10,12},{12,10},{14,16},{16,14},{18,20},{2... | collective-permute-start | bytes 2654216 | tf_op jit(solution)/shard_map/ppermute | solution.py:460
  5.9 1.2 %copy-start.1 = (bf16[8,55296]{1,0:T(8,128)(2,1)S(1)}, bf16[8,55296]{1,0:T(8,128)(2,1)}, u32[]{:S(2)}) copy-start(bf16[8,55296]{1,0:T(8,128)(2,1)} %initial.1) | copy-start | bytes 2654212
  7.1 4.9 %copy-start = (bf16[3,768,768]{2,1,0:T(8,128)(2,1)S(1)}, bf16[3,768,768]{2,1,0:T(8,128)(2,1)}, u32[]{:S(2)}) copy-start(bf16[3,768,768]{2,1,0:T(8,128)(2,1)} %constant.48.clone.taps) | copy-start | bytes 10616836
  7.1 4.9 %copy-start.2 = (f32[55296]{0:T(1024)S(1)}, f32[55296]{0:T(1024)}, u32[]{:S(2)}) copy-start(f32[55296]{0:T(1024)} %param.10) | copy-start | bytes 663556
  11.6 3.4 %collective-permute-start.2 = (f32[8,128]{1,0:T(8,128)S(1)}, f32[8,128]{1,0:T(8,128)S(1)}, u32[]{:S(2)}, u32[]{:S(2)}) collective-permute-start(f32[8,128]{1,0:T(8,128)S(1)} %get-tuple-element.17.refs_0_), channel_id=1, source_target_pairs={{0,2},{2,0},{4,6},{6,4},{8,10},{10,8},{12,14},{14,12},{16,18},{18,... | collective-permute-start | bytes 12296 | tf_op jit(solution)/shard_map/ppermute | solution.py:460
  12.0 14.8 %copy-start.4 = (f32[64]{0:T(128)S(1)}, f32[64]{0:T(128)}, u32[]{:S(2)}) copy-start(f32[64]{0:T(128)} %param.14) | copy-start | bytes 772
  15.0 10.6 %collective-permute-start.3 = (f32[16,128]{1,0:T(8,128)S(1)}, f32[16,128]{1,0:T(8,128)S(1)}, u32[]{:S(2)}, u32[]{:S(2)}) collective-permute-start(f32[16,128]{1,0:T(8,128)S(1)} %pad_maximum_fusion.1), channel_id=1, source_target_pairs={{2,4},{4,2},{6,8},{8,6},{10,12},{12,10},{14,16},{16,14},{18,20},{2... | collective-permute-start | bytes 24584 | tf_op jit(solution)/shard_map/ppermute | solution.py:460
  25.6 1.2 %collective-permute-start.4 = (f32[16,128]{1,0:T(8,128)S(1)}, f32[16,128]{1,0:T(8,128)S(1)}, u32[]{:S(2)}, u32[]{:S(2)}) collective-permute-start(f32[16,128]{1,0:T(8,128)S(1)} %collective-permute-done.3.refs_2_), channel_id=1, source_target_pairs={{0,2},{2,0},{4,6},{6,4},{8,10},{10,8},{12,14},{14,12},{16,18},{18,... | collective-permute-start | bytes 24584 | tf_op jit(solution)/shard_map/ppermute | solution.py:460
  28.6 24.5 %collective-permute-start.8 = (bf16[8,55296]{1,0:T(8,128)(2,1)S(1)}, bf16[8,55296]{1,0:T(8,128)(2,1)S(1)}, u32[]{:S(2)}, u32[]{:S(2)}) collective-permute-start(bf16[8,55296]{1,0:T(8,128)(2,1)S(1)} %get-tuple-element.24), channel_id=1, source_target_pairs={{0,2},{2,0},{4,6},{6,4},{8,10},{10,8},{12,14},{14,12},{16,18},{18,... | collective-permute-start | bytes 2654216 | tf_op jit(solution)/shard_map/ppermute | solution.py:460
  28.9 24.3 %collective-permute-start.9 = (bf16[8,55296]{1,0:T(8,128)(2,1)S(1)}, bf16[8,55296]{1,0:T(8,128)(2,1)S(1)}, u32[]{:S(2)}, u32[]{:S(2)}) collective-permute-start(bf16[8,55296]{1,0:T(8,128)(2,1)S(1)} %get-tuple-element.24), channel_id=1, source_target_pairs={{2,4},{4,2},{6,8},{8,6},{10,12},{12,10},{14,16},{16,14},{18,20},{2... | collective-permute-start | bytes 2654216 | tf_op jit(solution)/shard_map/ppermute | solution.py:460
  33.6 1.2 %collective-permute-start.5 = (f32[8,128]{1,0:T(8,128)S(1)}, f32[8,128]{1,0:T(8,128)S(1)}, u32[]{:S(2)}, u32[]{:S(2)}) collective-permute-start(f32[8,128]{1,0:T(8,128)S(1)} %get-tuple-element.20.refs_0_), channel_id=1, source_target_pairs={{0,2},{2,0},{4,6},{6,4},{8,10},{10,8},{12,14},{14,12},{16,18},{18,... | collective-permute-start | bytes 12296 | tf_op jit(solution)/shard_map/ppermute | solution.py:460
  34.8 18.4 %collective-permute-start.6 = (f32[16,128]{1,0:T(8,128)S(1)}, f32[16,128]{1,0:T(8,128)S(1)}, u32[]{:S(2)}, u32[]{:S(2)}) collective-permute-start(f32[16,128]{1,0:T(8,128)S(1)} %pad_maximum_fusion.2), channel_id=1, source_target_pairs={{2,4},{4,2},{6,8},{8,6},{10,12},{12,10},{14,16},{16,14},{18,20},{2... | collective-permute-start | bytes 24584 | tf_op jit(solution)/shard_map/ppermute | solution.py:460
  43.0 14.1 %copy-start.3 = (bf16[4,8,16]{2,1,0:T(8,128)(2,1)S(1)}, bf16[4,8,16]{2,1,0:T(8,128)(2,1)}, u32[]{:S(2)}) copy-start(bf16[4,8,16]{2,1,0:T(8,128)(2,1)} %param.15) | copy-start | bytes 3076
  43.0 14.0 %copy-start.5 = (s32[4]{0:T(128)S(1)}, s32[4]{0:T(128)}, u32[]{:S(2)}) copy-start(s32[4]{0:T(128)} %owner.1) | copy-start | bytes 52
  54.3 13.5 %collective-permute-start.11 = (bf16[8,55296]{1,0:T(8,128)(2,1)S(1)}, bf16[8,55296]{1,0:T(8,128)(2,1)S(1)}, u32[]{:S(2)}, u32[]{:S(2)}) collective-permute-start(bf16[8,55296]{1,0:T(8,128)(2,1)S(1)} %shard_map.110.panel), channel_id=1, source_target_pairs={{0,1},{1,0},{2,3},{3,2},{4,5},{5,4},{6,7},{7,6},{8,9},{9,8},{10,11... | collective-permute-start | bytes 2654216 | tf_op jit(solution)/shard_map/ppermute | solution.py:551
  54.6 1.2 %collective-permute-start.7 = (f32[16,128]{1,0:T(8,128)S(1)}, f32[16,128]{1,0:T(8,128)S(1)}, u32[]{:S(2)}, u32[]{:S(2)}) collective-permute-start(f32[16,128]{1,0:T(8,128)S(1)} %collective-permute-done.6.refs_2_), channel_id=1, source_target_pairs={{0,2},{2,0},{4,6},{6,4},{8,10},{10,8},{12,14},{14,12},{16,18},{18,... | collective-permute-start | bytes 24584 | tf_op jit(solution)/shard_map/ppermute | solution.py:460
  55.8 11.9 %collective-permute-start.10 = (f32[8,128]{1,0:T(8,128)S(1)}, f32[8,128]{1,0:T(8,128)S(1)}, u32[]{:S(2)}, u32[]{:S(2)}) collective-permute-start(f32[8,128]{1,0:T(8,128)S(1)} %shard_map.108.added), channel_id=1, source_target_pairs={{0,1},{1,0},{2,3},{3,2},{4,5},{5,4},{6,7},{7,6},{8,9},{9,8},{10,11... | collective-permute-start | bytes 12296 | tf_op jit(solution)/shard_map/ppermute | solution.py:551

commit v8 on v7

--- a/solution.py
+++ b/solution.py
@@ -128,7 +128,7 @@
                 target[pl.ds(row, 2 * n.panel), :] = part
         return carry
 
-    lax.fori_loop(0, n.blocks, one, None)
+    lax.fori_loop(0, n.blocks, one, None, unroll=4)
 
 
 def apply_taps(n, packs, taps, out):

time: 70.3 us -> 70.3 us (level)
  no operation moved by 1% of the time
where the time goes in v8:
time: 70.3 us; the launch traced here: 69.9 us
  waiting for transfers between devices  28.5 us (41%)
  Pallas kernels  22.1 us (31%)
  starting transfers between devices  15.9 us (23%)
  other arithmetic  1.46 us (2%)
  local copies, waits for them, and re-layouts  1.19 us (2%)
  between operations  0.75 us (1%)
    ppermute x10, waiting for transfers between devices, swapped(): return lax.ppermute(block, 'grid', pairs)  20.8 us
    pallas_call x7, Pallas kernels, call(): pl.pallas_call(kernel, out_shape=out_shape, in_specs=[pl.BlockSpec(memory...  16.9 us
    ppermute x10, starting transfers between devices, swapped(): return lax.ppermute(block, 'grid', pairs)  14.4 us
    ppermute x2, waiting for transfers between devices, all_orbs(): lax.ppermute(block, 'orb', [(i, (i + k) % orb_count) for i in range(orb_c...  7.69 us
    pallas_call x1, Pallas kernels, body(): pl.pallas_call(functools.partial(rotate_own_kernel, n, orb_count), grid=(...  2.98 us
    pallas_call x1, Pallas kernels, body(): pl.pallas_call(functools.partial(rotate_rest_kernel, n, rest), grid=(n.de...  2.21 us
    ppermute x2, starting transfers between devices, all_orbs(): lax.ppermute(block, 'orb', [(i, (i + k) % orb_count) for i in range(orb_c...  1.53 us
  transfers between devices with their start and end apart: 12, of which 6 were waited for; matrix products, arithmetic and copies ran while one was open for 2% of the time, Pallas kernels for 24%

profile of v8, /device:TPU:11, one launch (start us, length us, event | category | flops | bytes accessed | tf_op | source)
XLA Modules:
  0.0 69.9 jit_solution(10222917954453898090)
XLA Ops:
  0.6 0.7 %collective-permute-start = (bf16[8,55296]{1,0:T(8,128)(2,1)}, bf16[8,55296]{1,0:T(8,128)(2,1)S(1)}, u32[]{:S(2)}, u32[]{:S(2)}) collective-permute-start(bf16[8,55296]{1,0:T(8,128)(2,1)} %initial.1), channel_id=1, source_target_pairs={{0,2},{2,0},{4,6},{6,4},{8,10},{10,8},{12,14},{14,12},{16,18},{18,... | collective-permute-start | bytes 2654216 | tf_op jit(solution)/shard_map/ppermute | solution.py:460
  1.4 3.1 %collective-permute-start.1 = (bf16[8,55296]{1,0:T(8,128)(2,1)}, bf16[8,55296]{1,0:T(8,128)(2,1)S(1)}, u32[]{:S(2)}, u32[]{:S(2)}) collective-permute-start(bf16[8,55296]{1,0:T(8,128)(2,1)} %initial.1), channel_id=1, source_target_pairs={{2,4},{4,2},{6,8},{8,6},{10,12},{12,10},{14,16},{16,14},{18,20},{2... | collective-permute-start | bytes 2654216 | tf_op jit(solution)/shard_map/ppermute | solution.py:460
  4.4 0.7 %fusion.5 = (f32[12,128]{1,0:T(8,128)S(1)}, f32[12,128]{1,0:T(8,128)S(1)}) fusion(s32[1536]{0:T(1024)} %param.11, s32[1536]{0:T(1024)} %param.12, s32[]{:T(128)S(6)} %mul.19), kind=kLoop, calls=%fused_computation.10 | loop fusion | flops 47616 | bytes 24580 | tf_op jit(solution)/shard_map/reshape | solution.py:513
  5.2 0.7 %pad_maximum_fusion.entry_ref = f32[36,128]{1,0:T(8,128)S(1)} fusion(f32[12,128]{1,0:T(8,128)} %bitcast.13, f32[12,128]{1,0:T(8,128)S(1)} %get-tuple-element.29, f32[12,128]{1,0:T(8,128)S(1)} %get-tuple-element.28), kind=kLoop, calls=%fused_computation | loop fusion | flops 9216 | bytes 36864 | tf_op jit(solution)/shard_map/concatenate | solution.py:511
  5.9 0.0 copy-start.1
  5.9 1.2 %copy-done.1 = bf16[8,55296]{1,0:T(8,128)(2,1)S(1)} copy-done((bf16[8,55296]{1,0:T(8,128)(2,1)S(1)}, bf16[8,55296]{1,0:T(8,128)(2,1)}, u32[]{:S(2)}) %copy-start.1) | copy-done | bytes 884760
  7.1 0.0 copy-start
  7.1 0.0 copy-start.2
  7.1 4.6 %shard_map.104 = (bf16[1152,768]{1,0:T(8,128)(2,1)S(1)}, f32[8,128]{1,0:T(8,128)S(1)}, bf16[672,768]{1,0:T(8,128)(2,1)S(1)}) custom-call(bf16[8,55296]{1,0:T(8,128)(2,1)S(1)} %copy-done.1, f32[36,128]{1,0:T(8,128)S(1)} %pad_maximum_fusion.entry_ref), custom_call_target="tpu_custom_call" | custom-call | flops 4000000000 | bytes 903168 | tf_op jit(solution)/shard_map/pallas_call | solution.py:444
  11.6 0.4 collective-permute-start.2
  12.0 0.0 copy-done
  12.0 0.0 copy-done.2
  12.0 0.0 copy-start.4
  12.0 3.0 %shard_map.105.local = f32[8,55296]{1,0:T(8,128)S(1)} custom-call(bf16[8,55296]{1,0:T(8,128)(2,1)S(1)} %copy-done.1, bf16[672,768]{1,0:T(8,128)(2,1)S(1)} %get-tuple-element.15.packed, f32[432,128]{1,0:T(8,128)S(1)} %bitcast.8, bf16[3,768,768]{2,1,0:T(8,128)(2,1)S(1)} %copy-done), custom_call_target="tpu_custom_call" | custom-call | flops 2000000000 | bytes 5677056 | tf_op jit(solution)/shard_map/pallas_call | solution.py:444
  15.0 0.0 collective-permute-done.2.refs_1_
  15.0 3.2 %collective-permute-start.3 = (f32[16,128]{1,0:T(8,128)S(1)}, f32[16,128]{1,0:T(8,128)S(1)}, u32[]{:S(2)}, u32[]{:S(2)}) collective-permute-start(f32[16,128]{1,0:T(8,128)S(1)} %pad_maximum_fusion.1), channel_id=1, source_target_pairs={{2,4},{4,2},{6,8},{8,6},{10,12},{12,10},{14,16},{16,14},{18,20},{2... | collective-permute-start | bytes 24584 | tf_op jit(solution)/shard_map/ppermute | solution.py:460
  18.2 7.4 %collective-permute-done.3.refs_2_ = f32[16,128]{1,0:T(8,128)S(1)} collective-permute-done((f32[16,128]{1,0:T(8,128)S(1)}, f32[16,128]{1,0:T(8,128)S(1)}, u32[]{:S(2)}, u32[]{:S(2)}) %collective-permute-start.3) | collective-permute-done | bytes 8224 | tf_op jit(solution)/shard_map/ppermute | solution.py:460
  25.6 0.0 collective-permute-start.4
  25.6 1.2 %collective-permute-done.4.refs_3_ = f32[16,128]{1,0:T(8,128)S(1)} collective-permute-done((f32[16,128]{1,0:T(8,128)S(1)}, f32[16,128]{1,0:T(8,128)S(1)}, u32[]{:S(2)}, u32[]{:S(2)}) %collective-permute-start.4) | collective-permute-done | bytes 8224 | tf_op jit(solution)/shard_map/ppermute | solution.py:460
  26.8 0.0 collective-permute-done.inner
  26.8 0.0 collective-permute-done.1.outer
  26.8 0.0 copy-done.4
  26.8 1.9 %shard_map.106 = (f32[8,55296]{1,0:T(8,128)S(1)}, bf16[8,55296]{1,0:T(8,128)(2,1)S(1)}) custom-call(f32[8,55296]{1,0:T(8,128)S(1)} %shard_map.105.local, bf16[8,55296]{1,0:T(8,128)(2,1)S(1)} %collective-permute-done.inner, bf16[8,55296]{1,0:T(8,128)(2,1)S(1)} %collective-permute-done.1.outer, bf16[1152,768]{1,0:T(8,128)(2,1)S(1)} %get-tuple-element.16.table.refs_3_, ...), custom_call_target="tpu_custom_call" | custom-call | flops 1000000000 | bytes 5333248 | tf_op jit(solution)/shard_map/pallas_call | solution.py:444
  28.6 0.2 collective-permute-start.8
  28.9 3.0 %collective-permute-start.9 = (bf16[8,55296]{1,0:T(8,128)(2,1)S(1)}, bf16[8,55296]{1,0:T(8,128)(2,1)S(1)}, u32[]{:S(2)}, u32[]{:S(2)}) collective-permute-start(bf16[8,55296]{1,0:T(8,128)(2,1)S(1)} %get-tuple-element.24), channel_id=1, source_target_pairs={{2,4},{4,2},{6,8},{8,6},{10,12},{12,10},{14,16},{16,14},{18,20},{2... | collective-permute-start | bytes 2654216 | tf_op jit(solution)/shard_map/ppermute | solution.py:460
  31.9 1.7 %shard_map.107 = (f32[8,128]{1,0:T(8,128)S(1)}, bf16[672,768]{1,0:T(8,128)(2,1)S(1)}, bf16[672,768]{1,0:T(8,128)(2,1)S(1)}) custom-call(f32[8,55296]{1,0:T(8,128)S(1)} %get-tuple-element.19.field, bf16[1152,768]{1,0:T(8,128)(2,1)S(1)} %get-tuple-element.16.table.refs_3_), custom_call_target="tpu_custom_call" | custom-call | flops 1000000000 | bytes 3538944 | tf_op jit(solution)/shard_map/pallas_call | solution.py:444
  33.6 0.3 collective-permute-start.5
  33.9 0.9 %collective-permute-done.5.refs_1_ = f32[8,128]{1,0:T(8,128)S(1)} collective-permute-done((f32[8,128]{1,0:T(8,128)S(1)}, f32[8,128]{1,0:T(8,128)S(1)}, u32[]{:S(2)}, u32[]{:S(2)}) %collective-permute-start.5) | collective-permute-done | bytes 4128 | tf_op jit(solution)/shard_map/ppermute | solution.py:460
  34.8 3.5 %collective-permute-start.6 = (f32[16,128]{1,0:T(8,128)S(1)}, f32[16,128]{1,0:T(8,128)S(1)}, u32[]{:S(2)}, u32[]{:S(2)}) collective-permute-start(f32[16,128]{1,0:T(8,128)S(1)} %pad_maximum_fusion.2), channel_id=1, source_target_pairs={{2,4},{4,2},{6,8},{8,6},{10,12},{12,10},{14,16},{16,14},{18,20},{2... | collective-permute-start | bytes 24584 | tf_op jit(solution)/shard_map/ppermute | solution.py:460
  38.3 4.7 %shard_map.109.local = f32[8,55296]{1,0:T(8,128)S(1)} custom-call(f32[8,55296]{1,0:T(8,128)S(1)} %get-tuple-element.19.field, bf16[8,55296]{1,0:T(8,128)(2,1)S(1)} %copy-done.1, bf16[672,768]{1,0:T(8,128)(2,1)S(1)} %get-tuple-element.21.packed, bf16[672,768]{1,0:T(8,128)(2,1)S(1)} %get-tuple-element.22.rest, f32[432,128]{1,0:T(8,128)S(1)} %bitcast.9, ...), custom_call_target="tpu_custom_call" | custom-call | flops 3000000000 | bytes 8478720 | tf_op jit(solution)/shard_map/pallas_call | solution.py:444
  43.0 0.0 copy-start.3
  43.0 0.0 copy-start.5
  43.0 10.1 %collective-permute-done.6.refs_2_ = f32[16,128]{1,0:T(8,128)S(1)} collective-permute-done((f32[16,128]{1,0:T(8,128)S(1)}, f32[16,128]{1,0:T(8,128)S(1)}, u32[]{:S(2)}, u32[]{:S(2)}) %collective-permute-start.6) | collective-permute-done | bytes 8224 | tf_op jit(solution)/shard_map/ppermute | solution.py:460
  53.2 0.0 collective-permute-done.8.inner
  53.2 0.0 collective-permute-done.9.outer
  53.2 1.1 %shard_map.110.panel = bf16[8,55296]{1,0:T(8,128)(2,1)S(1)} custom-call(f32[8,55296]{1,0:T(8,128)S(1)} %shard_map.109.local, bf16[8,55296]{1,0:T(8,128)(2,1)S(1)} %collective-permute-done.8.inner, bf16[8,55296]{1,0:T(8,128)(2,1)S(1)} %collective-permute-done.9.outer), custom_call_target="tpu_custom_call" | custom-call | flops 1000000000 | bytes 3538944 | tf_op jit(solution)/shard_map/pallas_call | solution.py:444
  54.3 0.3 collective-permute-start.11
  54.6 0.0 collective-permute-start.7
  54.6 1.2 %collective-permute-done.7.refs_3_ = f32[16,128]{1,0:T(8,128)S(1)} collective-permute-done((f32[16,128]{1,0:T(8,128)S(1)}, f32[16,128]{1,0:T(8,128)S(1)}, u32[]{:S(2)}, u32[]{:S(2)}) %collective-permute-start.7) | collective-permute-done | bytes 8224 | tf_op jit(solution)/shard_map/ppermute | solution.py:460
  55.8 0.1 shard_map.108.added
  55.8 1.2 %collective-permute-start.10 = (f32[8,128]{1,0:T(8,128)S(1)}, f32[8,128]{1,0:T(8,128)S(1)}, u32[]{:S(2)}, u32[]{:S(2)}) collective-permute-start(f32[8,128]{1,0:T(8,128)S(1)} %shard_map.108.added), channel_id=1, source_target_pairs={{0,1},{1,0},{2,3},{3,2},{4,5},{5,4},{6,7},{7,6},{8,9},{9,8},{10,11... | collective-permute-start | bytes 12296 | tf_op jit(solution)/shard_map/ppermute | solution.py:551
  57.1 0.0 copy-done.3
  57.1 0.0 copy-done.5
  57.1 3.0 %shard_map.111 = (bf16[8,55296]{1,0:T(8,128)(2,1)}, f32[16,55296]{1,0:T(8,128)S(1)}, f32[16,8]{1,0:T(8,128)S(1)}) custom-call(s32[4]{0:T(128)S(1)} %copy-done.5, bf16[32,16]{1,0:T(8,128)(2,1)S(1)} %bitcast.10, f32[8,128]{1,0:T(8,128)S(1)} %shard_map.108.added, bf16[8,55296]{1,0:T(8,128)(2,1)S(1)} %shard_map.110.panel, ...), custom_call_target="tpu_custom_call" | custom-call | tf_op jit(solution)/shard_map/pallas_call | solution.py:571
  60.0 7.7 %collective-permute-done.10.refs_0_ = f32[8,128]{1,0:T(8,128)S(1)} collective-permute-done((f32[8,128]{1,0:T(8,128)S(1)}, f32[8,128]{1,0:T(8,128)S(1)}, u32[]{:S(2)}, u32[]{:S(2)}) %collective-permute-start.10) | collective-permute-done | bytes 4128 | tf_op jit(solution)/shard_map/ppermute | solution.py:551
  67.7 0.0 collective-permute-done.11.refs_1_
  67.7 2.2 %shard_map.112 = bf16[16,55296]{1,0:T(8,128)(2,1)} custom-call(f32[16,8]{1,0:T(8,128)S(1)} %get-tuple-element.26.rotation, f32[8,128]{1,0:T(8,128)S(1)} %collective-permute-done.10.refs_0_, bf16[8,55296]{1,0:T(8,128)(2,1)S(1)} %collective-permute-done.11.refs_1_, f32[16,55296]{1,0:T(8,128)S(1)} %get-tuple-element.27.refs_2_, ...), custom_call_target="tpu_custom_call" | custom-call | tf_op jit(solution)/shard_map/pallas_call | solution.py:584
  (2 shorter events, 0.0 us)
Async XLA Ops:
  0.6 26.1 %collective-permute-start = (bf16[8,55296]{1,0:T(8,128)(2,1)}, bf16[8,55296]{1,0:T(8,128)(2,1)S(1)}, u32[]{:S(2)}, u32[]{:S(2)}) collective-permute-start(bf16[8,55296]{1,0:T(8,128)(2,1)} %initial.1), channel_id=1, source_target_pairs={{0,2},{2,0},{4,6},{6,4},{8,10},{10,8},{12,14},{14,12},{16,18},{18,... | collective-permute-start | bytes 2654216 | tf_op jit(solution)/shard_map/ppermute | solution.py:460
  1.4 25.4 %collective-permute-start.1 = (bf16[8,55296]{1,0:T(8,128)(2,1)}, bf16[8,55296]{1,0:T(8,128)(2,1)S(1)}, u32[]{:S(2)}, u32[]{:S(2)}) collective-permute-start(bf16[8,55296]{1,0:T(8,128)(2,1)} %initial.1), channel_id=1, source_target_pairs={{2,4},{4,2},{6,8},{8,6},{10,12},{12,10},{14,16},{16,14},{18,20},{2... | collective-permute-start | bytes 2654216 | tf_op jit(solution)/shard_map/ppermute | solution.py:460
  5.9 1.2 %copy-start.1 = (bf16[8,55296]{1,0:T(8,128)(2,1)S(1)}, bf16[8,55296]{1,0:T(8,128)(2,1)}, u32[]{:S(2)}) copy-start(bf16[8,55296]{1,0:T(8,128)(2,1)} %initial.1) | copy-start | bytes 2654212
  7.1 5.0 %copy-start = (bf16[3,768,768]{2,1,0:T(8,128)(2,1)S(1)}, bf16[3,768,768]{2,1,0:T(8,128)(2,1)}, u32[]{:S(2)}) copy-start(bf16[3,768,768]{2,1,0:T(8,128)(2,1)} %constant.48.clone.taps) | copy-start | bytes 10616836
  7.1 5.0 %copy-start.2 = (f32[55296]{0:T(1024)S(1)}, f32[55296]{0:T(1024)}, u32[]{:S(2)}) copy-start(f32[55296]{0:T(1024)} %param.10) | copy-start | bytes 663556
  11.6 3.4 %collective-permute-start.2 = (f32[8,128]{1,0:T(8,128)S(1)}, f32[8,128]{1,0:T(8,128)S(1)}, u32[]{:S(2)}, u32[]{:S(2)}) collective-permute-start(f32[8,128]{1,0:T(8,128)S(1)} %get-tuple-element.17.refs_0_), channel_id=1, source_target_pairs={{0,2},{2,0},{4,6},{6,4},{8,10},{10,8},{12,14},{14,12},{16,18},{18,... | collective-permute-start | bytes 12296 | tf_op jit(solution)/shard_map/ppermute | solution.py:460
  12.0 14.8 %copy-start.4 = (f32[64]{0:T(128)S(1)}, f32[64]{0:T(128)}, u32[]{:S(2)}) copy-start(f32[64]{0:T(128)} %param.14) | copy-start | bytes 772
  15.0 10.6 %collective-permute-start.3 = (f32[16,128]{1,0:T(8,128)S(1)}, f32[16,128]{1,0:T(8,128)S(1)}, u32[]{:S(2)}, u32[]{:S(2)}) collective-permute-start(f32[16,128]{1,0:T(8,128)S(1)} %pad_maximum_fusion.1), channel_id=1, source_target_pairs={{2,4},{4,2},{6,8},{8,6},{10,12},{12,10},{14,16},{16,14},{18,20},{2... | collective-permute-start | bytes 24584 | tf_op jit(solution)/shard_map/ppermute | solution.py:460
  25.6 1.2 %collective-permute-start.4 = (f32[16,128]{1,0:T(8,128)S(1)}, f32[16,128]{1,0:T(8,128)S(1)}, u32[]{:S(2)}, u32[]{:S(2)}) collective-permute-start(f32[16,128]{1,0:T(8,128)S(1)} %collective-permute-done.3.refs_2_), channel_id=1, source_target_pairs={{0,2},{2,0},{4,6},{6,4},{8,10},{10,8},{12,14},{14,12},{16,18},{18,... | collective-permute-start | bytes 24584 | tf_op jit(solution)/shard_map/ppermute | solution.py:460
  28.6 24.5 %collective-permute-start.8 = (bf16[8,55296]{1,0:T(8,128)(2,1)S(1)}, bf16[8,55296]{1,0:T(8,128)(2,1)S(1)}, u32[]{:S(2)}, u32[]{:S(2)}) collective-permute-start(bf16[8,55296]{1,0:T(8,128)(2,1)S(1)} %get-tuple-element.24), channel_id=1, source_target_pairs={{0,2},{2,0},{4,6},{6,4},{8,10},{10,8},{12,14},{14,12},{16,18},{18,... | collective-permute-start | bytes 2654216 | tf_op jit(solution)/shard_map/ppermute | solution.py:460
  28.9 24.3 %collective-permute-start.9 = (bf16[8,55296]{1,0:T(8,128)(2,1)S(1)}, bf16[8,55296]{1,0:T(8,128)(2,1)S(1)}, u32[]{:S(2)}, u32[]{:S(2)}) collective-permute-start(bf16[8,55296]{1,0:T(8,128)(2,1)S(1)} %get-tuple-element.24), channel_id=1, source_target_pairs={{2,4},{4,2},{6,8},{8,6},{10,12},{12,10},{14,16},{16,14},{18,20},{2... | collective-permute-start | bytes 2654216 | tf_op jit(solution)/shard_map/ppermute | solution.py:460
  33.6 1.2 %collective-permute-start.5 = (f32[8,128]{1,0:T(8,128)S(1)}, f32[8,128]{1,0:T(8,128)S(1)}, u32[]{:S(2)}, u32[]{:S(2)}) collective-permute-start(f32[8,128]{1,0:T(8,128)S(1)} %get-tuple-element.20.refs_0_), channel_id=1, source_target_pairs={{0,2},{2,0},{4,6},{6,4},{8,10},{10,8},{12,14},{14,12},{16,18},{18,... | collective-permute-start | bytes 12296 | tf_op jit(solution)/shard_map/ppermute | solution.py:460
  34.8 18.4 %collective-permute-start.6 = (f32[16,128]{1,0:T(8,128)S(1)}, f32[16,128]{1,0:T(8,128)S(1)}, u32[]{:S(2)}, u32[]{:S(2)}) collective-permute-start(f32[16,128]{1,0:T(8,128)S(1)} %pad_maximum_fusion.2), channel_id=1, source_target_pairs={{2,4},{4,2},{6,8},{8,6},{10,12},{12,10},{14,16},{16,14},{18,20},{2... | collective-permute-start | bytes 24584 | tf_op jit(solution)/shard_map/ppermute | solution.py:460
  43.0 14.0 %copy-start.3 = (bf16[4,8,16]{2,1,0:T(8,128)(2,1)S(1)}, bf16[4,8,16]{2,1,0:T(8,128)(2,1)}, u32[]{:S(2)}) copy-start(bf16[4,8,16]{2,1,0:T(8,128)(2,1)} %param.15) | copy-start | bytes 3076
  43.0 14.0 %copy-start.5 = (s32[4]{0:T(128)S(1)}, s32[4]{0:T(128)}, u32[]{:S(2)}) copy-start(s32[4]{0:T(128)} %owner.1) | copy-start | bytes 52
  54.3 13.5 %collective-permute-start.11 = (bf16[8,55296]{1,0:T(8,128)(2,1)S(1)}, bf16[8,55296]{1,0:T(8,128)(2,1)S(1)}, u32[]{:S(2)}, u32[]{:S(2)}) collective-permute-start(bf16[8,55296]{1,0:T(8,128)(2,1)S(1)} %shard_map.110.panel), channel_id=1, source_target_pairs={{0,1},{1,0},{2,3},{3,2},{4,5},{5,4},{6,7},{7,6},{8,9},{9,8},{10,11... | collective-permute-start | bytes 2654216 | tf_op jit(solution)/shard_map/ppermute | solution.py:551
  54.6 1.2 %collective-permute-start.7 = (f32[16,128]{1,0:T(8,128)S(1)}, f32[16,128]{1,0:T(8,128)S(1)}, u32[]{:S(2)}, u32[]{:S(2)}) collective-permute-start(f32[16,128]{1,0:T(8,128)S(1)} %collective-permute-done.6.refs_2_), channel_id=1, source_target_pairs={{0,2},{2,0},{4,6},{6,4},{8,10},{10,8},{12,14},{14,12},{16,18},{18,... | collective-permute-start | bytes 24584 | tf_op jit(solution)/shard_map/ppermute | solution.py:460
  55.8 11.9 %collective-permute-start.10 = (f32[8,128]{1,0:T(8,128)S(1)}, f32[8,128]{1,0:T(8,128)S(1)}, u32[]{:S(2)}, u32[]{:S(2)}) collective-permute-start(f32[8,128]{1,0:T(8,128)S(1)} %shard_map.108.added), channel_id=1, source_target_pairs={{0,1},{1,0},{2,3},{3,2},{4,5},{5,4},{6,7},{7,6},{8,9},{9,8},{10,11... | collective-permute-start | bytes 12296 | tf_op jit(solution)/shard_map/ppermute | solution.py:551
